TPU v7x, 32 devices: a whole 2x2x4 slice. The times are simulated.
32 devices in a mesh: dp: 4 (over z), fsdp: 8 (over y, x, core).
Axes of the slice: x: 2, y: 2, z: 4, core: 2. Of those that a mesh axis runs over, the one named last changes fastest.
Arguments:
- inputs: bfloat16 [32, 1024, 1024], P(('dp', 'fsdp')), may hold values from -6 to 6
- memory: bfloat16 [32, 512, 1024], P(('dp', 'fsdp')), may hold values from -6 to 6
- cotangent: bfloat16 [32, 1024, 1024], P(('dp', 'fsdp')), may hold values from -6 to 6
- target_lengths: int32 [32], P(('dp', 'fsdp')), may hold values from 1 to 1024, as said below
- memory_lengths: int32 [32], P(('dp', 'fsdp')), may hold values from 128 to 512, as said below
- norm_gains: bfloat16 [3, 1024], P(None, ('dp', 'fsdp')), may hold values from 0.5 to 1.5
- norm_biases: bfloat16 [3, 1024], P(None, ('dp', 'fsdp')), may hold values from -4 to 4
- self_qkv: bfloat16 [1024, 3072], P(('dp', 'fsdp')), may hold values from -0.1875 to 0.1875
- self_out: bfloat16 [1024, 1024], P(('dp', 'fsdp')), may hold values from -0.5 to 0.5
- cross_query: bfloat16 [1024, 1024], P(('dp', 'fsdp')), may hold values from -0.1875 to 0.1875
- cross_kv: bfloat16 [1024, 2048], P(('dp', 'fsdp')), may hold values from -0.1875 to 0.1875
- cross_out: bfloat16 [1024, 1024], P(('dp', 'fsdp')), may hold values from -0.5 to 0.5
- ffn_in: bfloat16 [1024, 4096], P(('dp', 'fsdp')), may hold values from -0.1875 to 0.1875
- ffn_out: bfloat16 [4096, 1024], P(('dp', 'fsdp')), may hold values from -0.09375 to 0.09375
- proj_biases: bfloat16 [7, 1024], P(None, ('dp', 'fsdp')), may hold values from -4 to 4
- ffn_in_bias: bfloat16 [4096], P(('dp', 'fsdp')), may hold values from -4 to 4
Outputs:
- layer_output: bfloat16 [32, 1024, 1024], P(('dp', 'fsdp'))
- input_grad: float32 [32, 1024, 1024], P(('dp', 'fsdp'))
- memory_grad: float32 [32, 512, 1024], P(('dp', 'fsdp'))
- norm_gains_grad: float32 [3, 1024], P(None, ('dp', 'fsdp'))
- norm_biases_grad: float32 [3, 1024], P(None, ('dp', 'fsdp'))
- self_qkv_grad: float32 [1024, 3072], P(('dp', 'fsdp'))
- self_out_grad: float32 [1024, 1024], P(('dp', 'fsdp'))
- cross_query_grad: float32 [1024, 1024], P(('dp', 'fsdp'))
- cross_kv_grad: float32 [1024, 2048], P(('dp', 'fsdp'))
- cross_out_grad: float32 [1024, 1024], P(('dp', 'fsdp'))
- ffn_in_grad: float32 [1024, 4096], P(('dp', 'fsdp'))
- ffn_out_grad: float32 [4096, 1024], P(('dp', 'fsdp'))
- proj_biases_grad: float32 [7, 1024], P(None, ('dp', 'fsdp'))
- ffn_in_bias_grad: float32 [4096], P(('dp', 'fsdp'))
Inputs may be any that keep to these rules, and one draw needn't show every extreme that they name: `target_lengths`: at least one row has all 1024 positions live. `memory_lengths`: at least one row has all 512 memory positions live.
All inputs are finite; a program needn't handle non-finite values.
Results may differ from a plain program's by a relative error of at most 0.017.
Values may be sent and summed in bfloat16 or wider, within the bound.
No kernel may reach another device: no remote copies, remote signals or barrier semaphores. Data moves between devices by JAX's collectives and lax.ppermute only.
A program may use at most 448 MiB of HBM per device.

v0:
```python
import jax
import jax.numpy as jnp
from jax import lax
from jax.sharding import PartitionSpec as P

HEADS = 16


eps_norm = 1e-05
masked_score = -1e30


def layer_norm(hidden, gain, shift):
    centred = hidden - jnp.mean(hidden, axis=-1, keepdims=True)
    spread = jnp.mean(centred * centred, axis=-1, keepdims=True)
    return centred * lax.rsqrt(spread + eps_norm) * gain + shift


def matmul(left, right):
    return jnp.dot(left, right, preferred_element_type=jnp.float32)


def times_transposed(left, right):
    return lax.dot_general(
        left, right, (((1,), (1,)), ((), ())), preferred_element_type=jnp.float32
    )


def transposed_times(left, right):
    return lax.dot_general(
        left, right, (((0,), (0,)), ((), ())), preferred_element_type=jnp.float32
    )


def column_sums(gradient):
    return jnp.sum(gradient.astype(jnp.float32), axis=0)


def causal_allowed(limit, sequence):

    def allowed_fn(offset, block_rows):
        query_pos = offset + jnp.arange(block_rows)
        key_pos = jnp.arange(sequence)
        return (key_pos[None, :] <= query_pos[:, None]) & (key_pos[None, :] < limit)

    return allowed_fn


def memory_allowed(limit, memory_size):

    def allowed_fn(offset, block_rows):
        key_pos = jnp.arange(memory_size)
        return jnp.broadcast_to(key_pos[None, :] < limit, (block_rows, memory_size))

    return allowed_fn


def split_heads(tokens_in, head_count):
    return tokens_in.reshape(tokens_in.shape[0], head_count, -1)


def block_scores(query_heads, key_heads, allowed):
    scaling = query_heads.shape[-1] ** (-0.5)
    scores = (
        jnp.einsum("qhd,khd->hqk", query_heads, key_heads, preferred_element_type=jnp.float32)
        * scaling
    )
    return jnp.where(allowed[None], scores, masked_score)


def attend_forward(queries, key_tokens, value_tokens, allowed_fn, head_count):
    length = queries.shape[0]
    block_rows = min(512, length)
    key_heads = split_heads(key_tokens, head_count)
    value_heads = split_heads(value_tokens, head_count)
    outputs, maxima, totals = ([], [], [])
    for offset in range(0, length, block_rows):
        query_heads = split_heads(queries[offset : offset + block_rows], head_count)
        scores = block_scores(query_heads, key_heads, allowed_fn(offset, block_rows))
        largest = jnp.max(scores, axis=-1, keepdims=True)
        exponent = jnp.exp(scores - largest)
        summed = jnp.sum(exponent, axis=-1, keepdims=True)
        probability = (exponent / summed).astype(jnp.bfloat16)
        blended = jnp.einsum(
            "hqk,khd->qhd", probability, value_heads, preferred_element_type=jnp.float32
        )
        outputs.append(blended.reshape(block_rows, -1))
        maxima.append(largest)
        totals.append(summed)
    return (jnp.concatenate(outputs, axis=0), maxima, totals)


def attend_backward(
    queries, key_tokens, value_tokens, grad_mixed, maxima, totals, allowed_fn, head_count
):
    length = queries.shape[0]
    block_rows = min(512, length)
    key_heads = split_heads(key_tokens, head_count)
    value_heads = split_heads(value_tokens, head_count)
    scaling = key_heads.shape[-1] ** (-0.5)
    grad_queries = []
    grad_keys = jnp.zeros(key_heads.shape, jnp.float32)
    grad_values = jnp.zeros(value_heads.shape, jnp.float32)
    for position, offset in enumerate(range(0, length, block_rows)):
        query_heads = split_heads(queries[offset : offset + block_rows], head_count)
        scores = block_scores(query_heads, key_heads, allowed_fn(offset, block_rows))
        probability = jnp.exp(scores - maxima[position]) / totals[position]
        probs_low = probability.astype(jnp.bfloat16)
        grad_heads = split_heads(grad_mixed[offset : offset + block_rows], head_count)
        grad_probs = jnp.einsum(
            "qhd,khd->hqk", grad_heads, value_heads, preferred_element_type=jnp.float32
        )
        inner_sum = jnp.sum(probability * grad_probs, axis=-1, keepdims=True)
        grad_scores = (probability * (grad_probs - inner_sum)).astype(jnp.bfloat16)
        block_grad = (
            jnp.einsum("hqk,khd->qhd", grad_scores, key_heads, preferred_element_type=jnp.float32)
            * scaling
        )
        grad_queries.append(block_grad.reshape(block_rows, -1))
        grad_keys = (
            grad_keys
            + jnp.einsum(
                "hqk,qhd->khd", grad_scores, query_heads, preferred_element_type=jnp.float32
            )
            * scaling
        )
        grad_values = grad_values + jnp.einsum(
            "hqk,qhd->khd", probs_low, grad_heads, preferred_element_type=jnp.float32
        )
    key_count = key_tokens.shape[0]
    return (
        jnp.concatenate(grad_queries, axis=0),
        grad_keys.reshape(key_count, -1),
        grad_values.reshape(key_count, -1),
    )


def local(
    inputs,
    memory,
    cotangent,
    target_lengths,
    memory_lengths,
    norm_gains,
    norm_biases,
    self_qkv,
    self_out,
    cross_query,
    cross_kv,
    cross_out,
    ffn_in,
    ffn_out,
    proj_biases,
    ffn_in_bias,
):
    row_count, sequence, width = inputs.shape
    memory_size = memory.shape[1]
    attention_set = (
        lax.all_gather(self_qkv, ("dp", "fsdp"), axis=0, tiled=True),
        lax.all_gather(self_out, ("dp", "fsdp"), axis=0, tiled=True),
        lax.all_gather(cross_query, ("dp", "fsdp"), axis=0, tiled=True),
        lax.all_gather(cross_kv, ("dp", "fsdp"), axis=0, tiled=True),
        lax.all_gather(cross_out, ("dp", "fsdp"), axis=0, tiled=True),
        lax.all_gather(norm_gains, ("dp", "fsdp"), axis=1, tiled=True),
        lax.all_gather(norm_biases, ("dp", "fsdp"), axis=1, tiled=True),
        lax.all_gather(proj_biases, ("dp", "fsdp"), axis=1, tiled=True),
    )
    feed_set = (
        lax.all_gather(ffn_in, ("dp", "fsdp"), axis=0, tiled=True),
        lax.all_gather(ffn_out, ("dp", "fsdp"), axis=0, tiled=True),
        lax.all_gather(ffn_in_bias, ("dp", "fsdp"), axis=0, tiled=True),
    )
    (
        full_triple,
        full_self_out,
        full_query,
        full_pair,
        full_cross_out,
        full_gains,
        full_shifts,
        full_biases,
    ) = attention_set
    full_inner, full_outer, full_inner_bias = feed_set
    gains = full_gains.astype(jnp.float32)
    shifts = full_shifts.astype(jnp.float32)
    biases = full_biases.astype(jnp.float32)
    inner_bias = full_inner_bias.astype(jnp.float32)
    tokens = inputs.reshape(row_count * sequence, width).astype(jnp.float32)
    memory_flat = memory.reshape(row_count * memory_size, width)
    self_masks = [causal_allowed(target_lengths[0], sequence)]
    cross_masks = [memory_allowed(memory_lengths[0], memory_size)]
    zero_bias = jnp.zeros_like(biases[0])
    normed_one, back_one = jax.vjp(layer_norm, tokens, gains[0], shifts[0])
    normed_one = normed_one.astype(jnp.bfloat16)
    triple = (
        matmul(normed_one, full_triple) + jnp.concatenate([biases[0], zero_bias, biases[1]])
    ).astype(jnp.bfloat16)
    self_parts, self_stats = ([], [])
    row_index = 0
    blended, maxima, totals = attend_forward(
        triple[:, :width],
        triple[:, width : 2 * width],
        triple[:, 2 * width :],
        self_masks[row_index],
        HEADS,
    )
    self_parts.append(blended)
    self_stats.append((maxima, totals))
    self_mixed = self_parts[0].astype(jnp.bfloat16)
    hidden_one = tokens + matmul(self_mixed, full_self_out) + biases[2]
    normed_two, back_two = jax.vjp(layer_norm, hidden_one, gains[1], shifts[1])
    normed_two = normed_two.astype(jnp.bfloat16)
    cross_queries = (matmul(normed_two, full_query) + biases[3]).astype(jnp.bfloat16)
    paired = (matmul(memory_flat, full_pair) + jnp.concatenate([zero_bias, biases[4]])).astype(
        jnp.bfloat16
    )
    cross_parts, cross_stats = ([], [])
    row_index = 0
    memory_span = slice(row_index * memory_size, (row_index + 1) * memory_size)
    blended, maxima, totals = attend_forward(
        cross_queries,
        paired[memory_span, :width],
        paired[memory_span, width:],
        cross_masks[row_index],
        HEADS,
    )
    cross_parts.append(blended)
    cross_stats.append((maxima, totals))
    cross_mixed = cross_parts[0].astype(jnp.bfloat16)
    hidden_two = hidden_one + matmul(cross_mixed, full_cross_out) + biases[5]
    normed_three, back_three = jax.vjp(layer_norm, hidden_two, gains[2], shifts[2])
    normed_three = normed_three.astype(jnp.bfloat16)
    inner = matmul(normed_three, full_inner) + inner_bias
    activated, gelu_back = jax.vjp(jax.nn.gelu, inner)
    active_low = activated.astype(jnp.bfloat16)
    result = hidden_two + matmul(active_low, full_outer) + biases[6]
    layer_output = result.astype(jnp.bfloat16).reshape(inputs.shape)
    back_attention = (
        lax.all_gather(self_qkv, ("dp", "fsdp"), axis=0, tiled=True),
        lax.all_gather(self_out, ("dp", "fsdp"), axis=0, tiled=True),
        lax.all_gather(cross_query, ("dp", "fsdp"), axis=0, tiled=True),
        lax.all_gather(cross_kv, ("dp", "fsdp"), axis=0, tiled=True),
        lax.all_gather(cross_out, ("dp", "fsdp"), axis=0, tiled=True),
        lax.all_gather(norm_gains, ("dp", "fsdp"), axis=1, tiled=True),
        lax.all_gather(norm_biases, ("dp", "fsdp"), axis=1, tiled=True),
        lax.all_gather(proj_biases, ("dp", "fsdp"), axis=1, tiled=True),
    )
    back_feed = (
        lax.all_gather(ffn_in, ("dp", "fsdp"), axis=0, tiled=True),
        lax.all_gather(ffn_out, ("dp", "fsdp"), axis=0, tiled=True),
        lax.all_gather(ffn_in_bias, ("dp", "fsdp"), axis=0, tiled=True),
    )
    (
        full_triple,
        full_self_out,
        full_query,
        full_pair,
        full_cross_out,
        unused_gains,
        unused_shifts,
        unused_biases,
    ) = back_attention
    full_inner, full_outer, unused_inner_bias = back_feed
    grad_out = cotangent.reshape(row_count * sequence, width).astype(jnp.float32)
    grad_branch = cotangent.reshape(row_count * sequence, width)
    grad_outer = transposed_times(active_low, grad_branch)
    grad_bias_six = column_sums(grad_branch)
    grad_active = times_transposed(grad_branch, full_outer)
    grad_inner = gelu_back(grad_active)[0].astype(jnp.bfloat16)
    grad_inner_weight = transposed_times(normed_three, grad_inner)
    grad_inner_bias = column_sums(grad_inner)
    feed_grads = (
        lax.psum_scatter(grad_inner_weight, ("dp", "fsdp"), scatter_dimension=0, tiled=True),
        lax.psum_scatter(grad_outer, ("dp", "fsdp"), scatter_dimension=0, tiled=True),
        lax.psum_scatter(grad_inner_bias, ("dp", "fsdp"), scatter_dimension=0, tiled=True),
    )
    grad_normed = times_transposed(grad_inner, full_inner)
    grad_part, grad_gain_three, grad_shift_three = back_three(grad_normed)
    grad_hidden = grad_out + grad_part
    grad_branch = grad_hidden.astype(jnp.bfloat16)
    grad_cross_out = transposed_times(cross_mixed, grad_branch)
    grad_bias_five = column_sums(grad_branch)
    grad_mixed = times_transposed(grad_branch, full_cross_out).astype(jnp.bfloat16)
    query_parts, key_parts, value_parts = ([], [], [])
    row_index = 0
    memory_span = slice(row_index * memory_size, (row_index + 1) * memory_size)
    maxima, totals = cross_stats[row_index]
    grad_q, grad_k, grad_v = attend_backward(
        cross_queries,
        paired[memory_span, :width],
        paired[memory_span, width:],
        grad_mixed,
        maxima,
        totals,
        cross_masks[row_index],
        HEADS,
    )
    query_parts.append(grad_q)
    key_parts.append(grad_k)
    value_parts.append(grad_v)
    grad_cross_queries = query_parts[0].astype(jnp.bfloat16)
    grad_paired = jnp.concatenate([key_parts[0], value_parts[0]], axis=1).astype(jnp.bfloat16)
    grad_query_weight = transposed_times(normed_two, grad_cross_queries)
    grad_bias_three = column_sums(grad_cross_queries)
    grad_pair_weight = transposed_times(memory_flat, grad_paired)
    grad_bias_four = column_sums(grad_paired[:, width:])
    memory_grad = times_transposed(grad_paired, full_pair).reshape(memory.shape)
    grad_normed = times_transposed(grad_cross_queries, full_query)
    grad_part, grad_gain_two, grad_shift_two = back_two(grad_normed)
    grad_hidden = grad_hidden + grad_part
    grad_branch = grad_hidden.astype(jnp.bfloat16)
    grad_self_out = transposed_times(self_mixed, grad_branch)
    grad_bias_two = column_sums(grad_branch)
    grad_mixed = times_transposed(grad_branch, full_self_out).astype(jnp.bfloat16)
    row_index = 0
    maxima, totals = self_stats[row_index]
    grad_q, grad_k, grad_v = attend_backward(
        triple[:, :width],
        triple[:, width : 2 * width],
        triple[:, 2 * width :],
        grad_mixed,
        maxima,
        totals,
        self_masks[row_index],
        HEADS,
    )
    triple_parts = jnp.concatenate([grad_q, grad_k, grad_v], axis=1)
    grad_triple = triple_parts.astype(jnp.bfloat16)
    grad_triple_weight = transposed_times(normed_one, grad_triple)
    grad_bias_zero = column_sums(grad_triple[:, :width])
    grad_bias_one = column_sums(grad_triple[:, 2 * width :])
    grad_normed = times_transposed(grad_triple, full_triple)
    grad_part, grad_gain_one, grad_shift_one = back_one(grad_normed)
    input_grad = (grad_hidden + grad_part).reshape(inputs.shape)
    grad_gains = jnp.stack([grad_gain_one, grad_gain_two, grad_gain_three])
    grad_shifts = jnp.stack([grad_shift_one, grad_shift_two, grad_shift_three])
    grad_biases = jnp.stack(
        [
            grad_bias_zero,
            grad_bias_one,
            grad_bias_two,
            grad_bias_three,
            grad_bias_four,
            grad_bias_five,
            grad_bias_six,
        ]
    )
    attention_grads = (
        lax.psum_scatter(grad_triple_weight, ("dp", "fsdp"), scatter_dimension=0, tiled=True),
        lax.psum_scatter(grad_self_out, ("dp", "fsdp"), scatter_dimension=0, tiled=True),
        lax.psum_scatter(grad_query_weight, ("dp", "fsdp"), scatter_dimension=0, tiled=True),
        lax.psum_scatter(grad_pair_weight, ("dp", "fsdp"), scatter_dimension=0, tiled=True),
        lax.psum_scatter(grad_cross_out, ("dp", "fsdp"), scatter_dimension=0, tiled=True),
        lax.psum_scatter(grad_gains, ("dp", "fsdp"), scatter_dimension=1, tiled=True),
        lax.psum_scatter(grad_shifts, ("dp", "fsdp"), scatter_dimension=1, tiled=True),
        lax.psum_scatter(grad_biases, ("dp", "fsdp"), scatter_dimension=1, tiled=True),
    )
    (
        owned_triple,
        owned_self_out,
        owned_query,
        owned_pair,
        owned_cross_out,
        owned_gains,
        owned_shifts,
        owned_biases,
    ) = attention_grads
    owned_inner, owned_outer, owned_inner_bias = feed_grads
    return (
        layer_output,
        input_grad,
        memory_grad,
        owned_gains,
        owned_shifts,
        owned_triple,
        owned_self_out,
        owned_query,
        owned_pair,
        owned_cross_out,
        owned_inner,
        owned_outer,
        owned_biases,
        owned_inner_bias,
    )


def solution(mesh):
    return jax.shard_map(
        local,
        mesh=mesh,
        in_specs=(
            P(("dp", "fsdp"), None, None),
            P(("dp", "fsdp"), None, None),
            P(("dp", "fsdp"), None, None),
            P(("dp", "fsdp")),
            P(("dp", "fsdp")),
            P(None, ("dp", "fsdp")),
            P(None, ("dp", "fsdp")),
            P(("dp", "fsdp"), None),
            P(("dp", "fsdp"), None),
            P(("dp", "fsdp"), None),
            P(("dp", "fsdp"), None),
            P(("dp", "fsdp"), None),
            P(("dp", "fsdp"), None),
            P(("dp", "fsdp"), None),
            P(None, ("dp", "fsdp")),
            P(("dp", "fsdp")),
        ),
        out_specs=(
            P(("dp", "fsdp"), None, None),
            P(("dp", "fsdp"), None, None),
            P(("dp", "fsdp"), None, None),
            P(None, ("dp", "fsdp")),
            P(None, ("dp", "fsdp")),
            P(("dp", "fsdp"), None),
            P(("dp", "fsdp"), None),
            P(("dp", "fsdp"), None),
            P(("dp", "fsdp"), None),
            P(("dp", "fsdp"), None),
            P(("dp", "fsdp"), None),
            P(("dp", "fsdp"), None),
            P(None, ("dp", "fsdp")),
            P(("dp", "fsdp")),
        ),
        check_vma=False,
    )
```

profile of v0, /device:TPU:0, one launch (start us, length us, event | category | flops | bytes accessed | tf_op | source)
XLA Modules:
  0.0 2326.6 jit_solution(11484627747303743532)
XLA Ops:
  13.8 43.2 %all-gather.3 = bf16[32,1,128]{2,1,0:T(2,128)(2,1)S(1)} all-gather(bf16[1,1,128]{2,1,0:T(2,128)(2,1)} %bitcast.354), channel_id=1, replica_groups=mesh['dp'=4,'fsdp'=8] {'dp','fsdp'}, dimensions={0}, use_global_device_ids=true | all-gather | bytes 8448 | tf_op jit(solution)/shard_map/all_gather | solution.py:171
  57.6 36.9 %all-gather = bf16[32,32,3]{1,2,0:T(4,128)(2,1)S(1)} all-gather(bf16[1,32,3]{1,2,0:T(4,128)(2,1)} %bitcast.352), channel_id=1, replica_groups=mesh['dp'=4,'fsdp'=8] {'dp','fsdp'}, dimensions={0}, use_global_device_ids=true | all-gather | bytes 6336 | tf_op jit(solution)/shard_map/all_gather | solution.py:164
  95.2 38.4 %all-gather.1 = bf16[32,32,3]{1,2,0:T(4,128)(2,1)S(1)} all-gather(bf16[1,32,3]{1,2,0:T(4,128)(2,1)} %bitcast.353), channel_id=1, replica_groups=mesh['dp'=4,'fsdp'=8] {'dp','fsdp'}, dimensions={0}, use_global_device_ids=true | all-gather | bytes 6336 | tf_op jit(solution)/shard_map/all_gather | solution.py:165
  134.3 37.1 %all-gather.2 = bf16[32,32,7]{1,2,0:T(8,128)(2,1)S(1)} all-gather(bf16[1,32,7]{1,2,0:T(8,128)(2,1)} %bitcast.351), channel_id=1, replica_groups=mesh['dp'=4,'fsdp'=8] {'dp','fsdp'}, dimensions={0}, use_global_device_ids=true | all-gather | bytes 14784 | tf_op jit(solution)/shard_map/all_gather | solution.py:166
  192.8 10.4 add_convert_fusion
  219.5 19.6 fusion.139
  239.1 15.2 fusion.78
  254.3 19.2 fusion.140
  273.5 15.1 fusion.75
  303.8 10.0 fusion.142
  313.8 11.2 fusion.143
  347.3 52.3 %all-gather.22.cloned.1.call-done = bf16[1024,4096]{1,0:T(8,128)(2,1)} async-done(((bf16[32,4096]{1,0:T(8,128)(2,1)}), bf16[1024,4096]{1,0:T(8,128)(2,1)}) %all-gather.22.cloned.1.call-update) | async-done | bytes 8388624 | tf_op jit(solution)/shard_map/all_gather | solution.py:169
  399.6 17.4 fusion.125
  417.1 61.5 %all-gather.24.cloned.1.call-done = bf16[4096,1024]{1,0:T(8,128)(2,1)} async-done(((bf16[128,1024]{1,0:T(8,128)(2,1)}), bf16[4096,1024]{1,0:T(8,128)(2,1)}) %all-gather.24.cloned.1.call-update) | async-done | bytes 8388624 | tf_op jit(solution)/shard_map/all_gather | solution.py:170
  478.6 24.5 %convert_reduce_fusion = (f32[4096]{0:T(1024)}, bf16[1024,4096]{1,0:T(8,128)(2,1)}) fusion(f32[1024,4096]{1,0:T(8,128)} %fusion.125, f32[4096]{0:T(1024)S(1)} %bitcast.335, bf16[4096,1024]{1,0:T(8,128)(2,1)} %all-gather.24.cloned.1.call-done, bf16[1,1024,1024]{2,1,0:T(8,128)(2,1)S(1)} %copy-done.34), kind=kOutput, calls=%fused_computation.23 | convolution fusion | flops 8686399488 | bytes 35684352 | tf_op jit(solution)/shard_map/dot_general | solution.py:24
  503.1 15.9 fusion.145
  537.1 10.2 fusion.49
  547.3 11.0 multiply_reduce_fusion.2
  558.3 10.7 multiply_reduce_fusion.3
  569.1 11.9 multiply_convert_fusion.3
  588.2 7.8 multiply_convert_fusion.2
  625.6 21.5 multiply_reduce_fusion.1
  647.1 27.9 %multiply_convert_fusion.1 = bf16[16,512,1024]{2,1,0:T(8,128)(2,1)} fusion(f32[16,512,1024]{2,1,0:T(8,128)} %get-tuple-element.130, f32[16,512]{1,0:T(8,128)S(1)} %get-tuple-element.129, f32[16,512,1024]{2,1,0:T(8,128)} %get-tuple-element.116, f32[16,512]{1,0:T(8,128)S(1)} %copy-done.83), kind=kLoop, calls=%fused_computation.6 | loop fusion | flops 33554432 | bytes 83951616 | tf_op jit(solution)/shard_map/convert_element_type | solution.py:114
  675.0 11.9 multiply_convert_fusion.8
  687.0 11.2 fusion.148
  698.2 14.6 fusion.25
  712.8 22.4 multiply_reduce_fusion
  735.2 8.5 add_convert_fusion.7
  744.9 14.4 add_convert_fusion.1
  760.6 28.1 %multiply_convert_fusion = bf16[16,512,1024]{2,1,0:T(8,128)(2,1)} fusion(f32[16,512,1024]{2,1,0:T(8,128)} %get-tuple-element.132, f32[16,512]{1,0:T(8,128)S(1)} %get-tuple-element.131, f32[16,512,1024]{2,1,0:T(8,128)} %get-tuple-element.114, f32[16,512]{1,0:T(8,128)S(1)} %copy-done.81), kind=kLoop, calls=%fused_computation.4 | loop fusion | flops 33554432 | bytes 83951616 | tf_op jit(solution)/shard_map/convert_element_type | solution.py:114
  788.7 12.0 multiply_convert_fusion.7
  800.7 10.4 multiply_convert_fusion.5
  811.2 12.5 fusion.147
  887.9 9.1 copy.170
  897.8 14.2 fusion.89
  913.5 19.6 fusion.59
  933.8 16.7 fusion.124
  951.2 16.2 fusion.58
  975.5 39.7 %all-reduce.1 = f32[4096]{0:T(1024)S(1)} all-reduce(f32[4096]{0:T(1024)S(1)} %copy-done.92), channel_id=12, replica_groups=mesh['dp'=4,'fsdp'=8] {'dp','fsdp'}, use_global_device_ids=true, to_apply=%region_48.49.clone | all-reduce | flops 4096 | bytes 32768
  1023.1 66.8 %reduce-scatter.31.cloned.1.call-done = f32[32,3]{1,0:T(8,128)} async-done(((f32[1024,3]{1,0:T(8,128)}), f32[32,3]{1,0:T(8,128)}) %reduce-scatter.31.cloned.1.call-update) | async-done | bytes 400
  1091.3 130.4 %reduce-scatter.37.cloned.1.call-done = f32[32,7]{1,0:T(8,128)} async-done(((f32[1024,7]{1,0:T(8,128)}), f32[32,7]{1,0:T(8,128)}) %reduce-scatter.37.cloned.1.call-update) | async-done | bytes 912
  1223.1 138.6 %reduce-scatter.25.cloned.1.call-done = f32[32,1024]{1,0:T(8,128)} async-done(((f32[1024,1024]{1,0:T(8,128)}), f32[32,1024]{1,0:T(8,128)}) %reduce-scatter.25.cloned.1.call-update) | async-done | bytes 131088 | tf_op jit(solution)/shard_map/reduce_scatter | solution.py:353
  1361.7 139.9 %reduce-scatter.23.cloned.1.call-done = f32[32,1024]{1,0:T(8,128)} async-done(((f32[1024,1024]{1,0:T(8,128)}), f32[32,1024]{1,0:T(8,128)}) %reduce-scatter.23.cloned.1.call-update) | async-done | bytes 131088 | tf_op jit(solution)/shard_map/reduce_scatter | solution.py:351
  1501.6 139.8 %reduce-scatter.21.cloned.1.call-done = f32[32,1024]{1,0:T(8,128)} async-done(((f32[1024,1024]{1,0:T(8,128)}), f32[32,1024]{1,0:T(8,128)}) %reduce-scatter.21.cloned.1.call-update) | async-done | bytes 131088 | tf_op jit(solution)/shard_map/reduce_scatter | solution.py:350
  1641.4 147.5 %reduce-scatter.35.cloned.1.call-done = f32[32,2048]{1,0:T(8,128)} async-done(((f32[1024,2048]{1,0:T(8,128)}), f32[32,2048]{1,0:T(8,128)}) %reduce-scatter.35.cloned.1.call-update) | async-done | bytes 262160
  1788.9 159.1 %reduce-scatter.19.cloned.1.call-done = f32[32,3072]{1,0:T(8,128)} async-done(((f32[1024,3072]{1,0:T(8,128)}), f32[32,3072]{1,0:T(8,128)}) %reduce-scatter.19.cloned.1.call-update) | async-done | bytes 393232 | tf_op jit(solution)/shard_map/reduce_scatter | solution.py:349
  1948.0 184.6 %reduce-scatter.29.cloned.1.call-done = f32[128,1024]{1,0:T(8,128)} async-done(((f32[4096,1024]{1,0:T(8,128)}), f32[128,1024]{1,0:T(8,128)}) %reduce-scatter.29.cloned.1.call-update) | async-done | bytes 524304 | tf_op jit(solution)/shard_map/reduce_scatter | solution.py:274
  2132.6 187.2 %reduce-scatter.27.cloned.1.call-done = f32[32,4096]{1,0:T(8,128)} async-done(((f32[1024,4096]{1,0:T(8,128)}), f32[32,4096]{1,0:T(8,128)}) %reduce-scatter.27.cloned.1.call-update) | async-done | bytes 524304 | tf_op jit(solution)/shard_map/reduce_scatter | solution.py:273
  (360 shorter events, 225.6 us)
Async XLA Ops:
  7.2 175.0 %copy-start = (bf16[1,512,1024]{2,1,0:T(8,128)(2,1)S(1)}, bf16[1,512,1024]{2,1,0:T(8,128)(2,1)}, u32[]{:S(2)}) copy-start(bf16[1,512,1024]{2,1,0:T(8,128)(2,1)} %param.17) | copy-start | bytes 3145732
  7.2 175.0 %all-gather.16.cloned.1.call-start = ((), (), s32[]{:S(2)}) async-start(), calls=%async_computation.12 | async-start | bytes 4325376 | tf_op jit(solution)/shard_map/all_gather | solution.py:162
  7.9 184.8 %all-gather.12.cloned.1.call-start = ((), (), s32[]{:S(2)}) async-start(), calls=%async_computation.10 | async-start | bytes 6488064 | tf_op jit(solution)/shard_map/all_gather | solution.py:159
  8.7 280.0 %all-gather.14.cloned.1.call-start = ((), (), s32[]{:S(2)}) async-start(), calls=%async_computation.11 | async-start | bytes 2162688 | tf_op jit(solution)/shard_map/all_gather | solution.py:160
  9.4 286.7 %all-gather.18.cloned.1.call-start = ((), (), s32[]{:S(2)}) async-start(), calls=%async_computation.13 | async-start | bytes 2162688 | tf_op jit(solution)/shard_map/all_gather | solution.py:161
  10.0 328.8 %all-gather.20.cloned.1.call-start = ((), (), s32[]{:S(2)}) async-start(), calls=%async_computation.14 | async-start | bytes 2162688 | tf_op jit(solution)/shard_map/all_gather | solution.py:163
  10.6 389.1 %all-gather.22.cloned.1.call-start = ((), (), s32[]{:S(2)}) async-start(), calls=%async_computation.15 | async-start | bytes 8650752 | tf_op jit(solution)/shard_map/all_gather | solution.py:169
  11.2 467.4 %all-gather.24.cloned.1.call-start = ((), (), s32[]{:S(2)}) async-start(), calls=%async_computation.16 | async-start | bytes 8650752 | tf_op jit(solution)/shard_map/all_gather | solution.py:170
  11.9 1009.8 %reduce-scatter.33.cloned.1.call-start = ((), (), s32[]{:S(2)}) async-start(), calls=%async_computation.24 | async-start | bytes 540672
  95.2 97.6 %copy-start.60 = (f32[1,1024]{1,0:T(1,128)}, f32[1,1024]{1,0:T(1,128)S(1)}, u32[]{:S(2)}) copy-start(f32[1,1024]{1,0:T(1,128)S(1)} %get-tuple-element.107) | copy-start | bytes 12292
  95.2 200.9 %copy-start.73 = (f32[1,1024]{1,0:T(1,128)}, f32[1,1024]{1,0:T(1,128)S(1)}, u32[]{:S(2)}) copy-start(f32[1,1024]{1,0:T(1,128)S(1)} %get-tuple-element.106) | copy-start | bytes 12292
  134.3 58.5 %copy-start.99 = (f32[1,1024]{1,0:T(1,128)}, f32[1,1024]{1,0:T(1,128)S(1)}, u32[]{:S(2)}) copy-start(f32[1,1024]{1,0:T(1,128)S(1)} %get-tuple-element.110) | copy-start | bytes 12292
  134.3 161.8 %copy-start.101 = (f32[1,1024]{1,0:T(1,128)}, f32[1,1024]{1,0:T(1,128)S(1)}, u32[]{:S(2)}) copy-start(f32[1,1024]{1,0:T(1,128)S(1)} %get-tuple-element.109) | copy-start | bytes 12292
  175.1 113.6 %copy-start.3 = (bf16[1,1024,1024]{1,2,0:T(8,128)(2,1)}, bf16[1,1024,1024]{1,2,0:T(8,128)(2,1)S(1)}, u32[]{:S(2)}) copy-start(bf16[1,1024,1024]{1,2,0:T(8,128)(2,1)S(1)} %copy.128) | copy-start | bytes 6291460
  175.5 17.3 copy-start.51
  176.7 16.1 copy-start.64
  239.1 15.3 copy-start.80
  273.5 15.2 copy-start.82
  325.0 244.0 %copy-start.84 = (f32[16,512]{1,0:T(8,128)}, f32[16,512]{1,0:T(8,128)S(1)}, u32[]{:S(2)}) copy-start(f32[16,512]{1,0:T(8,128)S(1)} %get-tuple-element.121) | copy-start | bytes 98308
  344.7 54.9 %copy-start.71 = (f32[1,1024]{1,0:T(1,128)S(1)}, f32[1,1024]{1,0:T(1,128)}, u32[]{:S(2)}) copy-start(f32[1,1024]{1,0:T(1,128)} %get-tuple-element.105) | copy-start | bytes 12292
  344.7 54.9 %copy-start.97 = (f32[1,1024]{1,0:T(1,128)S(1)}, f32[1,1024]{1,0:T(1,128)}, u32[]{:S(2)}) copy-start(f32[1,1024]{1,0:T(1,128)} %get-tuple-element.108) | copy-start | bytes 12292
  344.8 184.9 %copy-start.55 = (f32[1024]{0:T(1024)}, f32[1024]{0:T(1024)S(1)}, u32[]{:S(2)}) copy-start(f32[1024]{0:T(1024)S(1)} %broadcast_multiply_fusion) | copy-start | bytes 12292
  347.3 182.4 %copy-start.66 = (f32[1024]{0:T(1024)}, f32[1024]{0:T(1024)S(1)}, u32[]{:S(2)}) copy-start(f32[1024]{0:T(1024)S(1)} %fusion.99) | copy-start | bytes 12292
  399.6 78.9 %copy-start.34 = (bf16[1,1024,1024]{2,1,0:T(8,128)(2,1)S(1)}, bf16[1,1024,1024]{2,1,0:T(8,128)(2,1)}, u32[]{:S(2)}) copy-start(bf16[1,1024,1024]{2,1,0:T(8,128)(2,1)} %param.18) | copy-start | bytes 6291460
  399.6 78.9 %copy-start.90 = (f32[32,1,128]{2,1,0:T(1,128)S(1)}, f32[32,1,128]{2,1,0:T(1,128)}, u32[]{:S(2)}) copy-start(f32[32,1,128]{2,1,0:T(1,128)} %convert_element_type.153) | copy-start | bytes 49156
  531.2 86.9 %copy-start.53 = (f32[1024]{0:T(1024)}, f32[1024]{0:T(1024)S(1)}, u32[]{:S(2)}) copy-start(f32[1024]{0:T(1024)S(1)} %negate_multiply_fusion.2) | copy-start | bytes 12292
  537.1 21.2 copy-start.47
  569.0 16.7 slice-start
  569.0 16.7 slice-start.1
  569.1 17.9 slice-start.2
  624.9 22.3 copy-start.49
  647.1 27.9 %copy-start.20 = (bf16[1024,1024]{0,1:T(8,128)(2,1)S(1)}, bf16[1024,1024]{0,1:T(8,128)(2,1)}, u32[]{:S(2)}) copy-start(bf16[1024,1024]{0,1:T(8,128)(2,1)} %copy.134) | copy-start | bytes 6291460
  698.2 14.6 copy-start.39
  712.8 22.4 copy-start.48
  712.8 22.4 copy-start.85
  712.8 22.4 copy-start.108
  760.6 28.1 %copy-start.21 = (bf16[1024,1024]{0,1:T(8,128)(2,1)S(1)}, bf16[1024,1024]{0,1:T(8,128)(2,1)}, u32[]{:S(2)}) copy-start(bf16[1024,1024]{0,1:T(8,128)(2,1)} %copy.134) | copy-start | bytes 6291460
  824.8 265.2 %reduce-scatter.31.cloned.1.call-start = ((), (), s32[]{:S(2)}) async-start(), calls=%async_computation.23 | async-start | bytes 540672
  843.7 378.0 %reduce-scatter.37.cloned.1.call-start = ((), (), s32[]{:S(2)}) async-start(), calls=%async_computation.26 | async-start | bytes 540672
  846.8 515.0 %reduce-scatter.25.cloned.1.call-start = ((), (), s32[]{:S(2)}) async-start(), calls=%async_computation.20 | async-start | bytes 4325376 | tf_op jit(solution)/shard_map/reduce_scatter | solution.py:353
  853.5 648.1 %reduce-scatter.23.cloned.1.call-start = ((), (), s32[]{:S(2)}) async-start(), calls=%async_computation.19 | async-start | bytes 4325376 | tf_op jit(solution)/shard_map/reduce_scatter | solution.py:351
  861.4 780.0 %reduce-scatter.21.cloned.1.call-start = ((), (), s32[]{:S(2)}) async-start(), calls=%async_computation.18 | async-start | bytes 4325376 | tf_op jit(solution)/shard_map/reduce_scatter | solution.py:350
  868.2 920.7 %reduce-scatter.35.cloned.1.call-start = ((), (), s32[]{:S(2)}) async-start(), calls=%async_computation.25 | async-start | bytes 8650752
  897.1 1050.9 %reduce-scatter.19.cloned.1.call-start = ((), (), s32[]{:S(2)}) async-start(), calls=%async_computation.17 | async-start | bytes 12976128 | tf_op jit(solution)/shard_map/reduce_scatter | solution.py:349
  912.0 1220.6 %reduce-scatter.29.cloned.1.call-start = ((), (), s32[]{:S(2)}) async-start(), calls=%async_computation.22 | async-start | bytes 17301504 | tf_op jit(solution)/shard_map/reduce_scatter | solution.py:274
  933.2 1386.6 %reduce-scatter.27.cloned.1.call-start = ((), (), s32[]{:S(2)}) async-start(), calls=%async_computation.21 | async-start | bytes 17301504 | tf_op jit(solution)/shard_map/reduce_scatter | solution.py:273
  970.0 45.8 %copy-start.41 = (bf16[16,64,512]{2,1,0:T(8,128)(2,1)S(1)}, bf16[16,64,512]{2,1,0:T(8,128)(2,1)}, u32[]{:S(2)}) copy-start(bf16[16,64,512]{2,1,0:T(8,128)(2,1)} %copy-done.40) | copy-start | bytes 3145732
  970.0 45.8 %copy-start.44 = (bf16[16,64,512]{2,1,0:T(8,128)(2,1)S(1)}, bf16[16,64,512]{2,1,0:T(8,128)(2,1)}, u32[]{:S(2)}) copy-start(bf16[16,64,512]{2,1,0:T(8,128)(2,1)} %copy-done.42) | copy-start | bytes 3145732
  (82 other events, 382.6 us)
Sparse Core Ops, SparseCore 0:
  10.9 64.8 all-gather.15
  78.7 68.1 all-gather.11
  149.7 54.8 all-gather.13
  207.3 55.2 all-gather.17
  265.3 55.2 all-gather.19
  323.3 76.2 all-gather.21
  402.5 76.0 all-gather.23
  824.9 132.5 reduce-scatter.32
  959.8 130.0 reduce-scatter.30
  1092.0 129.6 reduce-scatter.36
  1224.7 137.0 reduce-scatter.24
  1364.5 137.0 reduce-scatter.22
  1504.6 136.8 reduce-scatter.20
  1644.3 144.6 reduce-scatter.34
  1796.4 151.5 reduce-scatter.18
  1950.7 181.8 reduce-scatter.28
  2135.3 184.4 reduce-scatter.26
where the time goes:
time: 2340 us; the launch traced here: 2330 us
  waiting for transfers between devices  1410 us (60%)
  matrix products  486 us (21%)
  blocking collectives  195 us (8%)
  other arithmetic  110 us (5%)
  local copies, waits for them, and re-layouts  105 us (4%)
    unnamed x21, waiting for transfers between devices  349 us
    reduce_scatter x1, waiting for transfers between devices, local(): lax.psum_scatter(grad_inner_weight, ('dp', 'fsdp'), scatter_dimension=0,...  187 us
    reduce_scatter x1, waiting for transfers between devices, local(): lax.psum_scatter(grad_outer, ('dp', 'fsdp'), scatter_dimension=0, tiled=T...  185 us
    reduce_scatter x1, waiting for transfers between devices, local(): lax.psum_scatter(grad_triple_weight, ('dp', 'fsdp'), scatter_dimension=0,...  159 us
    reduce_scatter x1, waiting for transfers between devices, local(): lax.psum_scatter(grad_query_weight, ('dp', 'fsdp'), scatter_dimension=0,...  140 us
    reduce_scatter x1, waiting for transfers between devices, local(): lax.psum_scatter(grad_self_out, ('dp', 'fsdp'), scatter_dimension=0, tile...  140 us
    reduce_scatter x1, waiting for transfers between devices, local(): lax.psum_scatter(grad_cross_out, ('dp', 'fsdp'), scatter_dimension=0, til...  139 us
    dot_general x7, matrix products, transposed_times(): lax.dot_general(left, right, (((0,), (0,)), ((), ())), preferred_element_...  76.7 us
  transfers between devices with their start and end apart: 17, of which 11 were waited for; matrix products, arithmetic and copies ran while one was open for 15% of the time, Pallas kernels for 0%

commit v1 on v0

v1 whole, which is shorter than its diff:
```python
import functools

import jax
import jax.numpy as jnp
from jax import lax
from jax.experimental import pallas as pl
from jax.experimental.pallas import tpu as pltpu
from jax.sharding import PartitionSpec as P

f32 = jnp.float32
bf16 = jnp.bfloat16

HEAD = 64
PAIR = 2 * HEAD
BLOCK = 256
ROWS = 256
SMALL = 128
eps_norm = 1e-05
masked_score = -1e30
gelu_slope = 0.7978845608028654
gelu_cubic = 0.044715
MiB = 1 << 20


def nn(left, right):
    return jnp.dot(left, right, preferred_element_type=f32)


def nt(left, right):
    return lax.dot_general(left, right, (((1,), (1,)), ((), ())), preferred_element_type=f32)


def tn(left, right):
    return lax.dot_general(left, right, (((0,), (0,)), ((), ())), preferred_element_type=f32)


def normalise(hidden):
    centred = hidden - jnp.mean(hidden, axis=-1, keepdims=True)
    spread = lax.rsqrt(jnp.mean(centred * centred, axis=-1, keepdims=True) + eps_norm)
    return centred * spread, spread


def norm_back(hidden, incoming, gain):
    normed, spread = normalise(hidden)
    scaled = incoming * gain
    part = spread * (
        scaled
        - jnp.mean(scaled, axis=-1, keepdims=True)
        - normed * jnp.mean(scaled * normed, axis=-1, keepdims=True)
    )
    gain_grad = jnp.sum(incoming * normed, axis=0, keepdims=True)
    shift_grad = jnp.sum(incoming, axis=0, keepdims=True)
    return part, gain_grad, shift_grad


def column_sum(gradient):
    return jnp.sum(gradient.astype(f32), axis=0, keepdims=True)


def params():
    return pltpu.CompilerParams(vmem_limit_bytes=60 * MiB)


def after(waits, kernel, in_specs):
    count = len(waits)

    def waiting(*refs):
        kernel(*refs[count:])

    return waiting, [pl.BlockSpec(memory_space=pl.ANY)] * count + in_specs


def cost(flops, nbytes, transcendentals=0, high=64):
    return pl.CostEstimate(
        flops=high * flops, bytes_accessed=high * nbytes, transcendentals=high * transcendentals
    )


def held(shape, at=None):
    place = (0,) * len(shape) if at is None else at
    return pl.BlockSpec(shape, lambda j: place, pipeline_mode=pl.Buffered(1))


def by_rows(shape):
    return pl.BlockSpec(shape, lambda j: (j, 0))


def out(shape, dtype):
    return jax.ShapeDtypeStruct(shape, dtype)


GAIN, SHIFT, BIAS, HIDDEN_BIAS = 0, 3, 6, 13


def row_of(table_ref, at):
    return table_ref[at : at + 1, :]


def entry_kernel(x_ref, weight_ref, table_ref, normed_ref, triple_ref):
    width = x_ref.shape[1]
    normed, _ = normalise(x_ref[...].astype(f32))
    low = (normed * row_of(table_ref, GAIN) + row_of(table_ref, SHIFT)).astype(bf16)
    normed_ref[...] = low
    for part in range(3):
        span = slice(part * width, (part + 1) * width)
        made = nn(low, weight_ref[:, span])
        if part == 0:
            made = made + row_of(table_ref, BIAS)
        if part == 2:
            made = made + row_of(table_ref, BIAS + 1)
        triple_ref[:, span] = made.astype(bf16)


def entry(x, weights, table, waits=()):
    tokens, width = x.shape
    kernel, in_specs = after(
        waits, entry_kernel, [by_rows((ROWS, width)), held(weights.shape), held(table.shape)]
    )
    return pl.pallas_call(
        kernel,
        grid=(tokens // ROWS,),
        in_specs=in_specs,
        out_specs=[by_rows((ROWS, width)), by_rows((ROWS, 3 * width))],
        out_shape=[out((tokens, width), bf16), out((tokens, 3 * width), bf16)],
        compiler_params=params(),
        cost_estimate=cost(6 * tokens * width * width, 10 * tokens * width + 6 * width * width),
        name="norm_and_qkv",
    )(*waits, x, weights, table)


def middle_kernel(x_ref, mixed_ref, out_ref, query_ref, table_ref, hidden_ref, normed_ref, made_ref):
    hidden = x_ref[...].astype(f32) + nn(mixed_ref[...], out_ref[...]) + row_of(table_ref, BIAS + 2)
    hidden_ref[...] = hidden
    normed, _ = normalise(hidden)
    low = (normed * row_of(table_ref, GAIN + 1) + row_of(table_ref, SHIFT + 1)).astype(bf16)
    normed_ref[...] = low
    made_ref[...] = (nn(low, query_ref[...]) + row_of(table_ref, BIAS + 3)).astype(bf16)


def middle(x, mixed, weights, table):
    tokens, width = x.shape
    block = by_rows((ROWS, width))
    return pl.pallas_call(
        middle_kernel,
        grid=(tokens // ROWS,),
        in_specs=[
            block,
            block,
            held((width, width), (0, 0)),
            held((width, width), (0, 1)),
            held(table.shape),
        ],
        out_specs=[block, block, block],
        out_shape=[out((tokens, width), f32), out((tokens, width), bf16), out((tokens, width), bf16)],
        compiler_params=params(),
        cost_estimate=cost(4 * tokens * width * width, 12 * tokens * width + 4 * width * width),
        name="self_out_norm_query",
    )(x, mixed, weights, weights, table)


def memory_kernel(memory_ref, weight_ref, table_ref, pair_ref):
    width = memory_ref.shape[1]
    rows = memory_ref[...]
    pair_ref[:, :width] = nn(rows, weight_ref[:, :width]).astype(bf16)
    pair_ref[:, width:] = (nn(rows, weight_ref[:, width:]) + row_of(table_ref, BIAS + 4)).astype(bf16)


def memory_pair(memory, weights, table):
    tokens, width = memory.shape
    return pl.pallas_call(
        memory_kernel,
        grid=(tokens // ROWS,),
        in_specs=[by_rows((ROWS, width)), held((width, 2 * width), (0, 1)), held(table.shape)],
        out_specs=by_rows((ROWS, 2 * width)),
        out_shape=out((tokens, 2 * width), bf16),
        compiler_params=params(),
        cost_estimate=cost(4 * tokens * width * width, 6 * tokens * width + 4 * width * width),
        name="memory_keys_values",
    )(memory, weights, table)


def late_kernel(hidden_ref, mixed_ref, out_ref, table_ref, next_ref, normed_ref):
    hidden = hidden_ref[...] + nn(mixed_ref[...], out_ref[...]) + row_of(table_ref, BIAS + 5)
    next_ref[...] = hidden
    normed, _ = normalise(hidden)
    normed_ref[...] = (normed * row_of(table_ref, GAIN + 2) + row_of(table_ref, SHIFT + 2)).astype(bf16)


def late(hidden, mixed, weights, table):
    tokens, width = hidden.shape
    block = by_rows((ROWS, width))
    return pl.pallas_call(
        late_kernel,
        grid=(tokens // ROWS,),
        in_specs=[block, block, held((width, width), (0, 4)), held(table.shape)],
        out_specs=[block, block],
        out_shape=[out((tokens, width), f32), out((tokens, width), bf16)],
        compiler_params=params(),
        cost_estimate=cost(2 * tokens * width * width, 12 * tokens * width + 2 * width * width),
        name="cross_out_norm",
    )(hidden, mixed, weights, table)


def head_operands(lane, side, query, key, key_bias):
    own = (lane < HEAD) if side == 0 else (lane >= HEAD)
    spare = lane == (HEAD if side == 0 else 0)
    zero = jnp.zeros((), bf16)
    query_own = jnp.where(own, query, zero)
    key_own = jnp.where(own, key, zero)
    query_wide = jnp.where(spare, jnp.ones((), bf16), query_own)
    key_wide = jnp.where(spare, key_bias, key_own)
    return own, query_own, query_wide, key_own, key_wide


def pair_operands(length_ref, query_ref, key_ref):
    lane = lax.broadcasted_iota(jnp.int32, (1, PAIR), 1)
    key_pos = lax.broadcasted_iota(jnp.int32, (key_ref.shape[0], 1), 0)
    key_bias = jnp.where(key_pos < length_ref[0], 0.0, masked_score).astype(bf16)
    query = query_ref[...] * jnp.asarray(HEAD**-0.5, bf16)
    key = key_ref[...]
    return lane, [head_operands(lane, side, query, key, key_bias) for side in (0, 1)]


def scores_by_key(key_wide, query_block, keys, allowed):
    scores = nt(key_wide[:keys], query_block)
    if allowed is None:
        return scores
    last = jnp.where(allowed, scores[keys - BLOCK :], masked_score)
    return last if keys == BLOCK else jnp.concatenate([scores[: keys - BLOCK], last], axis=0)


def causal_block():
    key = lax.broadcasted_iota(jnp.int32, (BLOCK, BLOCK), 0)
    query = lax.broadcasted_iota(jnp.int32, (BLOCK, BLOCK), 1)
    return key <= query


def attend_kernel(causal, length_ref, query_ref, key_ref, value_ref, mixed_ref, stat_ref):
    rows, keys_all = query_ref.shape[0], key_ref.shape[0]
    lane, heads = pair_operands(length_ref, query_ref, key_ref)
    value = value_ref[...]
    allowed = causal_block() if causal else None
    first = lane < HEAD
    value_wide = [jnp.where(heads[side][0], value, jnp.ones((), bf16)) for side in (0, 1)]
    for at in range(0, rows, BLOCK):
        keys = at + BLOCK if causal else keys_all
        got, tops = [], []
        for side in (0, 1):
            _, _, query_wide, _, key_wide = heads[side]
            scores = scores_by_key(key_wide, query_wide[at : at + BLOCK], keys, allowed)
            top = jnp.max(scores, axis=0, keepdims=True)
            exponent = jnp.exp(scores - top)
            got.append(tn(exponent.astype(bf16), value_wide[side][:keys]))
            tops.append(top)
        total = jnp.where(first, got[1], got[0])
        mixed = jnp.where(first, got[0], got[1]) / pltpu.roll(total, HEAD, 1)
        mixed_ref[at : at + BLOCK, :] = mixed.astype(bf16)
        logs = jnp.log(total).T
        stat_ref[0, 0:1, at : at + BLOCK] = tops[0] + logs[HEAD : HEAD + 1]
        stat_ref[0, 1:2, at : at + BLOCK] = tops[1] + logs[0:1]


def pair_block(rows, column=0):
    return pl.BlockSpec((rows, PAIR), lambda j: (0, column + j))


def attend(lengths, query, key, value, causal):
    rows, keys, width = query[0].shape[0], key[0].shape[0], query[2]
    pairs = width // PAIR
    return pl.pallas_call(
        functools.partial(attend_kernel, causal),
        grid=(pairs,),
        in_specs=[
            pl.BlockSpec(memory_space=pltpu.SMEM),
            pair_block(rows, query[1]),
            pair_block(keys, key[1]),
            pair_block(keys, value[1]),
        ],
        out_specs=[pair_block(rows), pl.BlockSpec((1, 2, rows), lambda j: (j, 0, 0))],
        out_shape=[out((rows, width), bf16), out((pairs, 2, rows), f32)],
        compiler_params=params(),
        cost_estimate=cost(16 * rows * keys * width, 4 * (rows + keys) * width, 16 * rows * keys),
        name="attend_causal" if causal else "attend_memory",
    )(lengths, query[0], key[0], value[0])


def attend_back_kernel(
    causal,
    length_ref,
    query_ref,
    key_ref,
    value_ref,
    mixed_ref,
    grad_ref,
    stat_ref,
    query_grad_ref,
    key_grad_ref,
    value_grad_ref,
    sums_ref,
    key_sum,
    value_sum,
):
    rows, keys_all = query_ref.shape[0], key_ref.shape[0]
    scale = HEAD**-0.5
    lane, heads = pair_operands(length_ref, query_ref, key_ref)
    value = value_ref[...]
    grad = grad_ref[...]
    inner = (grad.astype(f32) * mixed_ref[...].astype(f32)).T
    allowed = causal_block() if causal else None
    zero = jnp.zeros((), bf16)
    value_own = [jnp.where(heads[side][0], value, zero) for side in (0, 1)]
    grad_own = [jnp.where(heads[side][0], grad, zero) for side in (0, 1)]
    inner_sum = [
        jnp.sum(inner[side * HEAD : (side + 1) * HEAD], axis=0, keepdims=True) for side in (0, 1)
    ]
    for at in range(rows - BLOCK, -1, -BLOCK):
        keys = at + BLOCK if causal else keys_all
        span = slice(at, at + BLOCK)
        sums = None
        for side in (0, 1):
            _, query_own, query_wide, key_own, key_wide = heads[side]
            scores = scores_by_key(key_wide, query_wide[span], keys, allowed)
            probs = jnp.exp(scores - stat_ref[0, side : side + 1, span])
            grad_probs = nt(value_own[side][:keys], grad[span])
            grad_scores = (probs * (grad_probs - inner_sum[side][:, span])).astype(bf16)
            parts = (
                tn(grad_scores, key_own[:keys]),
                nn(grad_scores, query_own[span]),
                nn(probs.astype(bf16), grad_own[side][span]),
            )
            sums = parts if sums is None else tuple(a + b for a, b in zip(sums, parts))
        query_low = (sums[0] * scale).astype(bf16)
        query_grad_ref[span, :] = query_low
        query_total = column_sum(query_low) + (0.0 if at == rows - BLOCK else query_total)
        if at == rows - BLOCK:
            key_sum[...] = sums[1]
            value_sum[...] = sums[2]
        else:
            key_sum[:keys] += sums[1]
            value_sum[:keys] += sums[2]
    key_grad_ref[...] = key_sum[...].astype(bf16)
    value_low = value_sum[...].astype(bf16)
    value_grad_ref[...] = value_low
    sums_ref[...] = jnp.zeros_like(sums_ref)
    sums_ref[0:1, :] = query_total
    sums_ref[1:2, :] = column_sum(value_low)


def attend_back(lengths, query, key, value, mixed, grad, stats, causal, waits=(), share=(0, 1)):
    rows, keys = query[0].shape[0], key[0].shape[0]
    pairs = query[2] // PAIR // share[1]
    first, width = share[0] * pairs, pairs * PAIR
    kernel, in_specs = after(
        waits,
        functools.partial(attend_back_kernel, causal),
        [
            pl.BlockSpec(memory_space=pltpu.SMEM),
            pair_block(rows, query[1] + first),
            pair_block(keys, key[1] + first),
            pair_block(keys, value[1] + first),
            pair_block(rows, first),
            pair_block(rows, first),
            pl.BlockSpec((1, 2, rows), lambda j: (first + j, 0, 0)),
        ],
    )
    return pl.pallas_call(
        kernel,
        grid=(pairs,),
        in_specs=in_specs,
        out_specs=[pair_block(rows), pair_block(keys), pair_block(keys), pair_block(8)],
        out_shape=[
            out((rows, width), bf16),
            out((keys, width), bf16),
            out((keys, width), bf16),
            out((8, width), f32),
        ],
        scratch_shapes=[pltpu.VMEM((keys, PAIR), f32), pltpu.VMEM((keys, PAIR), f32)],
        compiler_params=params(),
        cost_estimate=cost(24 * rows * keys * width, 8 * (rows + keys) * width, 16 * rows * keys),
        name="attend_causal_back" if causal else "attend_memory_back",
    )(*waits, lengths, query[0], key[0], value[0], mixed, grad, stats)


FEED_ROWS = 512


def feed_kernel(
    split, me_ref, normed_ref, branch_ref, weight_ref, table_ref, made_ref, back_ref, bias_ref, *refs
):
    turned, act, dact = refs[-3:]
    step = pl.program_id(0)
    tokens, width = normed_ref.shape

    @pl.when(step == 0)
    def _():
        made_ref[...] = jnp.zeros_like(made_ref)
        back_ref[...] = jnp.zeros_like(back_ref)
        turned[...] = normed_ref[...].T

    bias = table_ref[pl.ds(HIDDEN_BIAS + step, 1), :]
    bias_sum = jnp.zeros((1, width), f32)
    for at in range(0, tokens, FEED_ROWS):
        span = slice(at, at + FEED_ROWS)
        inner = nn(normed_ref[span, :], weight_ref[:, :width]) + bias
        grad_active = nt(branch_ref[span, :], weight_ref[:, width:])
        square = inner * inner
        bent = jnp.tanh(inner * (gelu_slope + (gelu_slope * gelu_cubic) * square))
        half = 0.5 + 0.5 * bent
        active = (inner * half).astype(bf16)
        slope = half + (0.5 * inner) * (1.0 - bent * bent) * (
            gelu_slope + (3.0 * gelu_slope * gelu_cubic) * square
        )
        grad_inner = (grad_active * slope).astype(bf16)
        act[span, :] = active
        dact[span, :] = grad_inner
        bias_sum += column_sum(grad_inner)
        made_ref[span, :] += nn(active, weight_ref[:, width:])
        back_ref[span, :] += nt(grad_inner, weight_ref[:, :width])
    bias_ref[0] = jnp.broadcast_to(bias_sum, bias_ref.shape[1:])
    for at in range(0, width, FEED_ROWS):
        span = slice(at, at + FEED_ROWS)
        inner_part = nn(turned[span, :], dact[...]).astype(bf16)
        outer_part = tn(act[:, span], branch_ref[...]).astype(bf16)
        for part, columns in ((inner_part, slice(0, width)), (outer_part, slice(width, 2 * width))):
            if split is None:
                refs[0][span, columns] = part
            else:
                dp_size, own = split
                spread(part, at // (2 * own), own, dp_size, me_ref, refs[0], refs[1], columns)


def feed(normed, branch, weights, table, split):
    tokens, width = normed.shape
    steps = weights.shape[1] // (2 * width)
    hidden = steps * width
    whole = pl.BlockSpec((tokens, width), lambda j: (0, 0))
    tile = pl.BlockSpec((width, 2 * width), lambda j: (0, j))
    if split[1:]:
        grad_specs = [pl.BlockSpec((width // 2, 2 * width), lambda j: (0, j))] * 2
        grad_shapes = [out((width // 2, 2 * hidden), bf16)] * 2
    else:
        grad_specs, grad_shapes = [tile], [out((width, 2 * hidden), bf16)]
    return pl.pallas_call(
        functools.partial(feed_kernel, split[1:] or None),
        grid=(steps,),
        in_specs=[
            pl.BlockSpec(memory_space=pltpu.SMEM),
            held((tokens, width)),
            held((tokens, width)),
            tile,
            held(table.shape),
        ],
        out_specs=[whole, whole, pl.BlockSpec((1, 8, width), lambda j: (j, 0, 0))] + grad_specs,
        out_shape=[
            out((tokens, width), f32),
            out((tokens, width), f32),
            out((steps, 8, width), f32),
        ]
        + grad_shapes,
        scratch_shapes=[
            pltpu.VMEM((width, tokens), bf16),
            pltpu.VMEM((tokens, width), bf16),
            pltpu.VMEM((tokens, width), bf16),
        ],
        compiler_params=params(),
        cost_estimate=cost(
            12 * tokens * width * hidden, 8 * width * hidden + 12 * tokens * width, tokens * hidden
        ),
        name="feed_forward_both_ways",
    )(split[0], normed, branch, weights, table)


def add_rows(ref, rows):
    @pl.when(pl.program_id(0) == 0)
    def _():
        ref[...] = jnp.zeros_like(ref)

    for at, row in rows:
        ref[at : at + 1, :] += row


def turn_kernel(
    hidden_ref, made_ref, back_ref, cotangent_ref, out_ref, table_ref,
    result_ref, grad_ref, branch_ref, mixed_grad_ref, sums_ref,
):
    hidden = hidden_ref[...]
    low_in = cotangent_ref[...]
    result_ref[...] = (hidden + made_ref[...] + row_of(table_ref, BIAS + 6)).astype(bf16)
    part, gain_grad, shift_grad = norm_back(hidden, back_ref[...], row_of(table_ref, GAIN + 2))
    grad = low_in.astype(f32) + part
    grad_ref[...] = grad
    low = grad.astype(bf16)
    branch_ref[...] = low
    mixed_grad_ref[...] = nt(low, out_ref[...]).astype(bf16)
    add_rows(
        sums_ref,
        ((0, gain_grad), (1, shift_grad), (2, column_sum(low_in)), (3, column_sum(low))),
    )


def turn(hidden, made, back, cotangent, weights, table):
    tokens, width = hidden.shape
    block = by_rows((ROWS, width))
    return pl.pallas_call(
        turn_kernel,
        grid=(tokens // ROWS,),
        in_specs=[block, block, block, block, held((width, width), (0, 4)), held(table.shape)],
        out_specs=[block, block, block, block, pl.BlockSpec((8, width), lambda j: (0, 0))],
        out_shape=[
            out((tokens, width), bf16),
            out((tokens, width), f32),
            out((tokens, width), bf16),
            out((tokens, width), bf16),
            out((8, width), f32),
        ],
        compiler_params=params(),
        cost_estimate=cost(2 * tokens * width * width, 24 * tokens * width + 2 * width * width),
        name="norm_back_cross_out_back",
    )(hidden, made, back, cotangent, weights, table)


def middle_back_kernel(
    hidden_ref, grad_ref, query_grad_ref, query_ref, out_ref, table_ref,
    next_ref, branch_ref, mixed_grad_ref, sums_ref,
):
    incoming = nt(query_grad_ref[...], query_ref[...])
    part, gain_grad, shift_grad = norm_back(hidden_ref[...], incoming, row_of(table_ref, GAIN + 1))
    grad = grad_ref[...] + part
    next_ref[...] = grad
    low = grad.astype(bf16)
    branch_ref[...] = low
    mixed_grad_ref[...] = nt(low, out_ref[...]).astype(bf16)
    add_rows(
        sums_ref,
        ((0, gain_grad), (1, shift_grad), (3, column_sum(low))),
    )


def middle_back(hidden, grad, query_grad, weights, table, waits=()):
    tokens, width = hidden.shape
    block = by_rows((ROWS, width))
    kernel, in_specs = after(
        waits,
        middle_back_kernel,
        [
            block,
            block,
            block,
            held((width, width), (0, 1)),
            held((width, width), (0, 0)),
            held(table.shape),
        ],
    )
    return pl.pallas_call(
        kernel,
        grid=(tokens // ROWS,),
        in_specs=in_specs,
        out_specs=[block, block, block, pl.BlockSpec((8, width), lambda j: (0, 0))],
        out_shape=[
            out((tokens, width), f32),
            out((tokens, width), bf16),
            out((tokens, width), bf16),
            out((8, width), f32),
        ],
        compiler_params=params(),
        cost_estimate=cost(4 * tokens * width * width, 20 * tokens * width + 4 * width * width),
        name="query_norm_back_self_out_back",
    )(*waits, hidden, grad, query_grad, weights, weights, table)


def entry_back_kernel(x_ref, grad_ref, weight_ref, table_ref, *refs):
    grads, (input_grad_ref, sums_ref) = refs[:-2], refs[-2:]
    incoming, at = 0.0, 0
    for ref in grads:
        columns = ref.shape[1]
        incoming += nt(ref[...], weight_ref[:, at : at + columns])
        at += columns
    part, gain_grad, shift_grad = norm_back(x_ref[...].astype(f32), incoming, row_of(table_ref, GAIN))
    input_grad_ref[...] = grad_ref[...] + part
    add_rows(sums_ref, ((0, gain_grad), (1, shift_grad)))


def entry_back(x, grad, grads, weights, table, waits=()):
    tokens, width = x.shape
    block = by_rows((ROWS, width))
    kernel, in_specs = after(
        waits,
        entry_back_kernel,
        [block, block, held(weights.shape), held(table.shape)]
        + [by_rows((ROWS, part.shape[1])) for part in grads],
    )
    return pl.pallas_call(
        kernel,
        grid=(tokens // ROWS,),
        in_specs=in_specs,
        out_specs=[block, pl.BlockSpec((8, width), lambda j: (0, 0))],
        out_shape=[out((tokens, width), f32), out((8, width), f32)],
        compiler_params=params(),
        cost_estimate=cost(6 * tokens * width * width, 16 * tokens * width + 6 * width * width),
        name="qkv_norm_back",
    )(*waits, x, grad, weights, table, *grads)


def memory_back_kernel(key_grad_ref, value_grad_ref, weight_ref, memory_grad_ref):
    width = key_grad_ref.shape[1]
    made = nt(key_grad_ref[...], weight_ref[:, :width])
    memory_grad_ref[...] = made + nt(value_grad_ref[...], weight_ref[:, width:])


def memory_back(key_grad, value_grad, weights, waits=()):
    tokens, width = key_grad.shape
    block = by_rows((ROWS, width))
    kernel, in_specs = after(
        waits, memory_back_kernel, [block, block, held((width, 2 * width), (0, 1))]
    )
    return pl.pallas_call(
        kernel,
        grid=(tokens // ROWS,),
        in_specs=in_specs,
        out_specs=block,
        out_shape=out((tokens, width), f32),
        compiler_params=params(),
        cost_estimate=cost(4 * tokens * width * width, 8 * tokens * width + 4 * width * width, 0, 64),
        name="memory_back",
    )(*waits, key_grad, value_grad, weights)


def weight_grads_kernel(picks, *refs):
    step = pl.program_id(0)
    grads_ref = refs[-1]
    half, wide = grads_ref.shape[0] // 2, grads_ref.shape[1]
    for at, (left, right, column) in enumerate(picks):

        @pl.when(step == at)
        def _(left=left, right=right, column=column):
            for low in (0, half):
                grads_ref[low : low + half, :] = tn(
                    refs[left][:, low : low + half], refs[right][:, column : column + wide]
                ).astype(bf16)


def spread(made, first_pair, own, dp_size, me_ref, keep_ref, send_ref, columns):
    mine = me_ref[0]
    upper = lax.rem(mine, 2) == 1
    planes = keep_ref.shape[0] // own // dp_size
    mine_plane = lax.rem(lax.shift_right_logical(mine, 1), planes)
    for piece in range(made.shape[0] // (2 * own)):
        pair = first_pair + piece
        away = lax.bitwise_xor(mine_plane, pair % planes)
        place = away * dp_size + pair // planes
        span = pl.ds(pl.multiple_of(place * own, own), own)
        one = made[2 * own * piece : 2 * own * piece + own]
        two = made[2 * own * piece + own : 2 * own * (piece + 1)]
        keep_ref[span, columns] = jnp.where(upper, two, one)
        send_ref[span, columns] = jnp.where(upper, one, two)


def small_grads_kernel(one_ref, two_ref, three_ref, cross_ref, self_ref, hidden_ref, rows_ref):
    rows_ref[...] = jnp.zeros_like(rows_ref)
    places = [(GAIN, one_ref, 0), (GAIN + 1, two_ref, 0), (GAIN + 2, three_ref, 0)]
    places += [(SHIFT, one_ref, 1), (SHIFT + 1, two_ref, 1), (SHIFT + 2, three_ref, 1)]
    places += [(BIAS, self_ref, 0), (BIAS + 1, self_ref, 1), (BIAS + 2, two_ref, 3), (BIAS + 3, cross_ref, 0)]
    places += [(BIAS + 4, cross_ref, 1), (BIAS + 5, three_ref, 3), (BIAS + 6, three_ref, 2)]
    for at, ref, row in places:
        rows_ref[at : at + 1, :] = ref[row : row + 1, :]
    for step in range(hidden_ref.shape[0]):
        rows_ref[HIDDEN_BIAS + step : HIDDEN_BIAS + step + 1, :] = hidden_ref[step, 0:1, :]


def small_grads(*sums):
    width = sums[0].shape[1]
    return pl.pallas_call(
        small_grads_kernel,
        out_shape=out((24, width), f32),
        compiler_params=params(),
        name="small_grads",
    )(*sums)


def split_grads_kernel(picks, dp_size, own, me_ref, *refs):
    step = pl.program_id(0)
    keep_ref, send_ref = refs[-2:]
    half, wide = keep_ref.shape
    for at, (left, right, column) in enumerate(picks):

        @pl.when(step == at)
        def _(left=left, right=right, column=column):
            for low in (0, half):
                made = tn(refs[left][:, low : low + half], refs[right][:, column : column + wide])
                first_pair = low // (2 * own)
                spread(made.astype(bf16), first_pair, own, dp_size, me_ref, keep_ref, send_ref, slice(0, wide))


def weight_grads(pairs, split=None, waits=(), wide=1024):
    arrays, picks = [], []
    for left, right in pairs:
        at = []
        for array in (left, right):
            known = [i for i, other in enumerate(arrays) if other is array]
            if not known:
                arrays.append(array)
            at.append(known[0] if known else len(arrays) - 1)
        picks += [(at[0], at[1], column) for column in range(0, right.shape[1], wide)]
    width = pairs[0][0].shape[1]
    columns = sum(right.shape[1] for _, right in pairs)
    flops = sum(2 * left.shape[0] * width * right.shape[1] for left, right in pairs)
    nbytes = 2 * sum(a.size for a in arrays) + 2 * width * columns
    if split is None:
        return pl.pallas_call(
            functools.partial(weight_grads_kernel, tuple(picks)),
            grid=(len(picks),),
            in_specs=[held(array.shape) for array in arrays],
            out_specs=pl.BlockSpec((width, wide), lambda j: (0, j)),
            out_shape=out((width, columns), bf16),
            compiler_params=params(),
            cost_estimate=cost(flops, nbytes),
            name="weight_grads",
        )(*arrays)
    mine, dp_size, own = split
    half = pl.BlockSpec((width // 2, wide), lambda j: (0, j))
    kernel, in_specs = after(
        waits,
        functools.partial(split_grads_kernel, tuple(picks), dp_size, own),
        [pl.BlockSpec(memory_space=pltpu.SMEM)] + [held(array.shape) for array in arrays],
    )
    return pl.pallas_call(
        kernel,
        grid=(len(picks),),
        in_specs=in_specs,
        out_specs=[half, half],
        out_shape=[out((width // 2, columns), bf16)] * 2,
        compiler_params=params(),
        cost_estimate=cost(flops, nbytes),
        name="weight_grads_by_distance",
    )(*waits, mine, *arrays)


def place_kernel(me_ref, near_ref, far_ref, whole_ref):
    own = near_ref.shape[1]
    upper = lax.rem(me_ref[0], 2) == 1
    near, far = near_ref[0], far_ref[0]
    whole_ref[:own, :] = jnp.where(upper, far, near)
    whole_ref[own:, :] = jnp.where(upper, near, far)


def place(mine, near, far, dp_size):
    pairs, own, columns = near.shape
    planes = pairs // dp_size

    def pair_at(j, me_ref):
        away = lax.rem(j, dp_size) * planes + lax.div(j, dp_size)
        return lax.bitwise_xor(lax.shift_right_logical(me_ref[0], 1), away), 0

    block = pl.BlockSpec((1, own, columns), lambda j, me_ref: (j, 0, 0))
    return pl.pallas_call(
        place_kernel,
        grid_spec=pltpu.PrefetchScalarGridSpec(
            num_scalar_prefetch=1,
            grid=(pairs,),
            in_specs=[block, block],
            out_specs=pl.BlockSpec((2 * own, columns), pair_at),
        ),
        out_shape=out((2 * pairs * own, columns), bf16),
        compiler_params=params(),
        cost_estimate=cost(0, 8 * pairs * own * columns),
        name="place_by_device",
    )(mine, near, far)


def feed_own_kernel(*refs):
    owned, (inner_ref, outer_ref) = refs[:-2], refs[-2:]
    own, width = owned[0].shape[0], outer_ref.shape[1]
    tiles = [
        (ref, at * width) for ref in owned for at in range(0, ref.shape[1] // width, 2)
    ]
    for step, (ref, at) in enumerate(tiles):
        outer_ref[step * own : (step + 1) * own, :] = ref[:, at + width : at + 2 * width].astype(f32)
    for device in range(width // own):
        pieces = [ref[:, at + device * own : at + (device + 1) * own].astype(f32) for ref, at in tiles]
        span = len(tiles) * own
        inner_ref[:, device * span : (device + 1) * span] = jnp.concatenate(pieces, axis=1)


def feed_own_grads(owned, width, waits=()):
    own = owned[0].shape[0]
    steps = sum(part.shape[1] for part in owned) // (2 * width)
    vmem = pl.BlockSpec(memory_space=pltpu.VMEM)
    kernel, in_specs = after(waits, feed_own_kernel, [vmem] * len(owned))
    return pl.pallas_call(
        kernel,
        in_specs=in_specs,
        out_shape=[out((own, steps * width), f32), out((steps * own, width), f32)],
        compiler_params=params(),
        name="feed_own_grads",
    )(*waits, *owned)


def cut_kernel(cuts, whole_ref, *outs):
    for ref, (low, high) in zip(outs, cuts):
        ref[...] = whole_ref[:, low:high].astype(f32)


def cut_columns(whole, ends, waits=()):
    cuts = tuple(zip(ends[:-1], ends[1:]))
    own = whole.shape[0]
    vmem = pl.BlockSpec(memory_space=pltpu.VMEM)
    kernel, in_specs = after(waits, functools.partial(cut_kernel, cuts), [vmem])
    return pl.pallas_call(
        kernel,
        in_specs=in_specs,
        out_shape=[out((own, high - low), f32) for low, high in cuts],
        compiler_params=params(),
        name="own_columns",
    )(*waits, whole)


def plane_pieces_kernel(count, ranges, keep_ref, got_ref, *outs):
    rows = keep_ref.shape[0] // count
    for at, (low, high) in enumerate(ranges):
        for k in range(count):
            span = slice(k * rows, (k + 1) * rows)
            made = keep_ref[span, low:high].astype(f32) + got_ref[span, low:high].astype(f32)
            outs[at * count + k][...] = made.astype(bf16)


def lanes_of(columns):
    return next(n for n in (2048, 1664, 1408, 1280, 1024, 128) if columns % n == 0)


def plane_pieces(keep, got, count, waits, ends):
    rows, columns = keep.shape
    ranges = tuple(zip(ends[:-1], ends[1:]))
    if len(ranges) == 1:
        lanes = lanes_of(columns)
        steps, shapes, ranges = columns // lanes, [(columns, lanes)], ((0, lanes),)
    else:
        lanes, steps, shapes = columns, 1, [(high - low, high - low) for low, high in ranges]
    block = pl.BlockSpec((rows, lanes), lambda j: (0, j))
    kernel, in_specs = after(
        waits, functools.partial(plane_pieces_kernel, count, ranges), [block, block]
    )
    return pl.pallas_call(
        kernel,
        grid=(steps,),
        in_specs=in_specs,
        out_specs=[
            pl.BlockSpec((rows // count, n), lambda j: (0, j)) for _, n in shapes for _ in range(count)
        ],
        out_shape=[out((rows // count, n), bf16) for n, _ in shapes for _ in range(count)],
        compiler_params=params(),
        cost_estimate=cost(0, 6 * rows * columns),
        name="plane_pieces",
    )(*waits, keep, got)


def plane_total_kernel(*refs):
    total = refs[0][...].astype(f32)
    for ref in refs[1:-1]:
        total = total + ref[...].astype(f32)
    refs[-1][...] = total.astype(bf16)


def plane_total(pieces, waits=(), weight=0):
    rows, columns = pieces[0].shape
    lanes = lanes_of(columns)
    block = pl.BlockSpec((rows, lanes), lambda j: (0, j))
    kernel, in_specs = after(waits, plane_total_kernel, [block] * len(pieces))
    return pl.pallas_call(
        kernel,
        grid=(columns // lanes,),
        in_specs=in_specs,
        out_specs=block,
        out_shape=out((rows, columns), bf16),
        compiler_params=params(),
        cost_estimate=cost(weight * rows * columns, 2 * (len(pieces) + 1) * rows * columns),
        name="plane_total",
    )(*waits, *pieces)


def prepare_kernel(
    qkv_ref, out_ref, query_ref, pair_ref, cross_ref, inner_ref, outer_ref, gains_ref, shifts_ref, biases_ref, hidden_ref,
    first_ref, second_ref, third_ref,
):
    own, width = out_ref.shape
    steps = inner_ref.shape[1] // width
    devices = width // own
    rows = [gains_ref[...].astype(f32), shifts_ref[...].astype(f32), biases_ref[...].astype(f32)]
    hidden = hidden_ref[...].astype(f32)
    rows += [hidden[:, step * own : (step + 1) * own] for step in range(steps)]
    rows += [jnp.zeros((SMALL - HIDDEN_BIAS - steps, own), f32)]
    first_ref[:, : 3 * width] = qkv_ref[...]
    first_ref[:, 3 * width :] = jnp.concatenate(rows, axis=0).T.astype(bf16)
    second_ref[:, :width] = out_ref[...]
    second_ref[:, width : 2 * width] = query_ref[...]
    second_ref[:, 2 * width : 4 * width] = pair_ref[...]
    second_ref[:, 4 * width :] = cross_ref[...]
    for step in range(steps):
        pieces = [
            inner_ref[:, (device * steps + step) * own : (device * steps + step + 1) * own].astype(f32)
            for device in range(devices)
        ]
        third_ref[:, 2 * step * width : (2 * step + 1) * width] = jnp.concatenate(pieces, axis=1).astype(bf16)
        third_ref[:, (2 * step + 1) * width : (2 * step + 2) * width] = outer_ref[step * own : (step + 1) * own, :]


def prepare(*shards):
    own, width = shards[1].shape
    steps = shards[5].shape[1] // width
    return pl.pallas_call(
        prepare_kernel,
        out_shape=[
            out((own, 3 * width + SMALL), bf16),
            out((own, 5 * width), bf16),
            out((own, 2 * steps * width), bf16),
        ],
        compiler_params=params(),
        name="shards_to_gather",
    )(*shards)


AXES = ("dp", "fsdp")


def gather(shard):
    return lax.all_gather(shard, AXES, axis=0, tiled=True)


def scatter_sum(whole):
    return lax.psum_scatter(whole, AXES, scatter_dimension=0, tiled=True)


def exchange(array, axis, size, distance):
    return lax.ppermute(array, axis, [(i, i ^ distance) for i in range(size)])


def small_sum(sums, own, dp_size, fsdp_size):
    kept = sums
    for axis, size in (("fsdp", fsdp_size), ("dp", dp_size)):
        distance = 1
        while distance < size:
            kept = kept + exchange(kept, axis, size, distance)
            distance *= 2
    start = (lax.axis_index("dp") * fsdp_size + lax.axis_index("fsdp")) * own
    return lax.dynamic_slice_in_dim(kept, start, own, axis=1)


def add_low(left, right):
    return (left.astype(f32) + right.astype(f32)).astype(bf16)


def scatter_plane(keep, got, fsdp_size, waits=(), cut=()):
    planes = fsdp_size // 2
    made = list(plane_pieces(keep, got, planes, waits, (0, *cut, keep.shape[1])))
    both = [made[at : at + planes] for at in range(0, len(made), planes)]
    return [
        (part[1:], part[:1] + [exchange(part[k], "fsdp", fsdp_size, 2 * k) for k in range(1, planes)])
        for part in both
    ]


def scatter_line(total):
    return lax.psum_scatter(total, "dp", scatter_dimension=0, tiled=True)


def local(
    inputs,
    memory,
    cotangent,
    target_lengths,
    memory_lengths,
    norm_gains,
    norm_biases,
    self_qkv,
    self_out,
    cross_query,
    cross_kv,
    cross_out,
    ffn_in,
    ffn_out,
    proj_biases,
    ffn_in_bias,
):
    width = inputs.shape[2]
    own = self_qkv.shape[0]
    devices = width // own
    steps = ffn_in.shape[1] // width
    dp_size, fsdp_size = lax.axis_size("dp"), lax.axis_size("fsdp")
    by_distance = own % 16 == 0
    mine = (lax.axis_index("dp") * fsdp_size + lax.axis_index("fsdp")).astype(jnp.int32).reshape(1)
    split = (mine, dp_size, own) if by_distance else (mine,)

    if by_distance:
        first_shard, second_shard, feed_shard = prepare(
            self_qkv, self_out, cross_query, cross_kv, cross_out, ffn_in, ffn_out,
            norm_gains, norm_biases, proj_biases, ffn_in_bias.reshape(1, -1),
        )
    else:
        small = jnp.concatenate(
            [norm_gains, norm_biases, proj_biases, ffn_in_bias.reshape(steps, own)], axis=0
        )
        small = jnp.pad(small, ((0, SMALL - small.shape[0]), (0, 0))).T
        first_shard = jnp.concatenate([self_qkv, small], axis=1)
        second_shard = jnp.concatenate([self_out, cross_query, cross_kv, cross_out], axis=1)
        inner_shard = ffn_in.reshape(own, devices, steps, own).transpose(0, 2, 1, 3).reshape(own, steps, width)
        outer_shard = ffn_out.reshape(steps, own, width).transpose(1, 0, 2)
        feed_shard = jnp.concatenate([inner_shard, outer_shard], axis=2).reshape(own, 2 * steps * width)

    first = gather(first_shard)
    third = gather(feed_shard)
    x = inputs[0]
    rows = memory[0]
    branch = cotangent[0]
    waits = ()
    if by_distance:
        line = jnp.stack(
            [second_shard] + [exchange(second_shard, "dp", dp_size, k) for k in range(1, dp_size)]
        )
        plane = [exchange(line, "fsdp", fsdp_size, 2 * k) for k in range(1, fsdp_size // 2)]
        waits = (line,)
    table = first[:, 3 * width :].astype(f32).T[:24]

    normed_one, triple = entry(x, first, table, waits)
    parts = [(triple, at * (width // PAIR), width) for at in range(3)]
    self_mixed, self_stats = attend(target_lengths, *parts, True)
    if by_distance:
        near = jnp.concatenate([line] + plane)
        second = place(mine, near, exchange(near, "fsdp", fsdp_size, 1), dp_size)
    else:
        second = gather(second_shard)
    pair = memory_pair(rows, second, table)
    hidden_one, normed_two, queries = middle(x, self_mixed, second, table)
    cross_parts = [(queries, 0, width), (pair, 0, width), (pair, width // PAIR, width)]
    cross_mixed, cross_stats = attend(memory_lengths, *cross_parts, False)
    hidden_two, normed_three = late(hidden_one, cross_mixed, second, table)
    made, back, hidden_bias_sums, *feed_grads = feed(normed_three, branch, third, table, split)
    result, grad_two, branch_two, mixed_grad, sums_three = turn(
        hidden_two, made, back, branch, second, table
    )
    waits = ()
    if by_distance:
        feed_got = exchange(feed_grads[1], "fsdp", fsdp_size, 1)
        [(feed_sent, feed_plane)] = scatter_plane(feed_grads[0], feed_got, fsdp_size, (result,))
        waits = tuple(feed_sent)
    else:
        feed_own = scatter_sum(feed_grads[0])
    query_grad, key_grad, value_grad, cross_sums = attend_back(
        memory_lengths, *cross_parts, cross_mixed, mixed_grad, cross_stats, False, waits
    )
    cross_pairs = [
        (cross_mixed, branch_two),
        (normed_two, query_grad),
        (rows, key_grad),
        (rows, value_grad),
    ]
    waits = ()
    if by_distance:
        cross_keep, cross_send = weight_grads(cross_pairs, split)
        cross_got = exchange(cross_send, "fsdp", fsdp_size, 1)
        waits = (cross_send,)
    grad_one, branch_one, mixed_grad, sums_two = middle_back(
        hidden_one, grad_two, query_grad, second, table, waits
    )
    if by_distance:
        [(cross_sent, cross_plane)] = scatter_plane(cross_keep, cross_got, fsdp_size, (grad_one,))
        waits = tuple(cross_sent)
    *self_grads, self_sums = attend_back(
        target_lengths, *parts, self_mixed, mixed_grad, self_stats, True, waits
    )
    self_pairs = [(self_mixed, branch_one)] + [(normed_one, part) for part in self_grads]
    waits = ()
    if by_distance:
        feed_total = plane_total(feed_plane, (self_sums,))
        feed_own = scatter_line(feed_total)
        self_keep, self_send = weight_grads(self_pairs, split, (feed_total,))
        self_got = exchange(self_send, "fsdp", fsdp_size, 1)
        cross_total = plane_total(cross_plane, (self_send,), 4096)
        cross_own = scatter_line(cross_total)
        [(self_sent, self_plane)] = scatter_plane(self_keep, self_got, fsdp_size, (cross_total,))
        waits = tuple(self_sent)
    input_grad, sums_one = entry_back(x, grad_one, self_grads, first, table, waits)
    sums = small_grads(sums_one, sums_two, sums_three, cross_sums, self_sums, hidden_bias_sums)
    if by_distance:
        memory_grad = memory_back(key_grad, value_grad, second, (input_grad,))
        inner_own, outer_own = feed_own_grads([feed_own], width, (memory_grad,))
        cross_out_own, query_own, pair_own = cut_columns(
            cross_own, (0, width, 2 * width, 4 * width), (inner_own,)
        )
        self_total = plane_total(self_plane, (cross_out_own,))
        self_own = scatter_line(self_total)
        self_out_own, triple_own = cut_columns(self_own, (0, width, 4 * width))
    else:
        memory_grad = memory_back(key_grad, value_grad, second)
        cross_own = scatter_sum(weight_grads(cross_pairs)).astype(f32)
        cross_out_own, query_own = cross_own[:, :width], cross_own[:, width : 2 * width]
        pair_own = cross_own[:, 2 * width :]
        self_own = scatter_sum(weight_grads(self_pairs)).astype(f32)
        self_out_own, triple_own = self_own[:, :width], self_own[:, width:]
        feed_own = feed_own.astype(f32).reshape(own, steps, 2, width)
        inner_own = feed_own[:, :, 0].reshape(own, steps, devices, own).transpose(0, 2, 1, 3)
        inner_own = inner_own.reshape(own, steps * width)
        outer_own = feed_own[:, :, 1].transpose(1, 0, 2).reshape(steps * own, width)
    small_own = small_sum(sums, own, dp_size, fsdp_size)
    return (
        result[None],
        input_grad[None],
        memory_grad[None],
        small_own[GAIN:SHIFT],
        small_own[SHIFT:BIAS],
        triple_own,
        self_out_own,
        query_own,
        pair_own,
        cross_out_own,
        inner_own,
        outer_own,
        small_own[BIAS:HIDDEN_BIAS],
        small_own[HIDDEN_BIAS : HIDDEN_BIAS + steps].reshape(steps * own),
    )


def solution(mesh):
    rows = P(AXES, None, None)
    lengths = P(AXES)
    split = P(AXES, None)
    features = P(None, AXES)
    return jax.shard_map(
        local,
        mesh=mesh,
        in_specs=(rows, rows, rows, lengths, lengths, features, features)
        + (split,) * 7
        + (features, lengths),
        out_specs=(rows, rows, rows, features, features) + (split,) * 7 + (features, lengths),
        check_vma=False,
    )
```

time: 2340 us -> 576 us (0.25)
  waiting for transfers between devices: 1410 us -> 166 us
  matrix products: 486 us -> 0 us
  Pallas kernels: 0 us -> 348 us
  blocking collectives: 195 us -> 0 us
  other arithmetic: 110 us -> 2.81 us
  local copies, waits for them, and re-layouts: 105 us -> 10.4 us
    reduce_scatter x6 -> x3, waiting for transfers between devices: 949 us -> 9.04 us  [scatter_line(): return lax.psum_scatter(total, 'dp', scatter_dimension=0, tiled=True)]
    dot_general x41 -> x0, matrix products: 426 us -> none  [the longest x7 76.7 us: transposed_times(): lax.dot_general(left, right, (((0,), (0,)), ((), ())), preferred_element_...]
    unnamed x21 -> x5, waiting for transfers between devices: 349 us -> 0.08 us
    pallas_call x0 -> x27, Pallas kernels: none -> 348 us  [the longest x2 68.1 us: attend_back(): pl.pallas_call(kernel, grid=(pairs,), in_specs=in_specs, out_specs=[pair_...]
    all_gather x4 -> x0, blocking collectives: 156 us -> none  [the longest x1 43.2 us: local(): lax.all_gather(ffn_in_bias, ('dp', 'fsdp'), axis=0, tiled=True)]
    ppermute x0 -> x24, waiting for transfers between devices: none -> 150 us  [exchange(): return lax.ppermute(array, axis, [(i, i ^ distance) for i in range(size)])]
    all_gather x7 -> x2, waiting for transfers between devices: 114 us -> 7.32 us  [gather(): return lax.all_gather(shard, AXES, axis=0, tiled=True)]
    convert_element_type x8 -> x0, other arithmetic: 76.2 us -> none  [the longest x4 75.6 us: attend_backward(): grad_scores = (probability * (grad_probs - inner_sum)).astype(jnp.bfloat16)]
  transfers between devices with their start and end apart: 17 -> 29, of which waited for: 11 -> 15; matrix products, arithmetic and copies ran while one was open for 15% -> 2% of each run, Pallas kernels for 0% -> 47%
where the time goes in v1:
time: 576 us; the launch traced here: 567 us
  Pallas kernels  348 us (60%)
  waiting for transfers between devices  166 us (29%)
  starting transfers between devices  23.3 us (4%)
  between operations  15.4 us (3%)
  local copies, waits for them, and re-layouts  10.4 us (2%)
    ppermute x24, waiting for transfers between devices, exchange(): return lax.ppermute(array, axis, [(i, i ^ distance) for i in range(size)])  150 us
    pallas_call x2, Pallas kernels, attend_back(): pl.pallas_call(kernel, grid=(pairs,), in_specs=in_specs, out_specs=[pair_...  68.1 us
    pallas_call x1, Pallas kernels, feed(): pl.pallas_call(functools.partial(feed_kernel, split[1:] or None), grid=(s...  65.8 us
    pallas_call x2, Pallas kernels, attend(): pl.pallas_call(functools.partial(attend_kernel, causal), grid=(pairs,), i...  45.2 us
    pallas_call x2, Pallas kernels, weight_grads(): pl.pallas_call(kernel, grid=(len(picks),), in_specs=in_specs, out_specs=[...  29.5 us
    ppermute x24, starting transfers between devices, exchange(): return lax.ppermute(array, axis, [(i, i ^ distance) for i in range(size)])  23.1 us
    pallas_call x3, Pallas kernels, plane_pieces(): pl.pallas_call(kernel, grid=(steps,), in_specs=in_specs, out_specs=[pl.Bl...  20.2 us
    pallas_call x1, Pallas kernels, entry_back(): pl.pallas_call(kernel, grid=(tokens // ROWS,), in_specs=in_specs, out_spe...  14.5 us
  transfers between devices with their start and end apart: 29, of which 15 were waited for; matrix products, arithmetic and copies ran while one was open for 2% of the time, Pallas kernels for 47%

profile of v1, /device:TPU:0, one launch (start us, length us, event | category | flops | bytes accessed | tf_op | source)
XLA Modules:
  0.0 566.7 jit_solution(13109139946578949940)
XLA Ops:
  7.2 2.5 shards_to_gather.1
  9.8 5.1 collective-permute-start.2
  15.6 1.8 constant_dynamic-update-slice_fusion.6
  17.4 6.5 %collective-permute-done.2 = bf16[32,5120]{1,0:T(8,128)(2,1)S(1)} collective-permute-done((bf16[32,5120]{1,0:T(8,128)(2,1)}, bf16[32,5120]{1,0:T(8,128)(2,1)S(1)}, u32[]{:S(2)}, u32[]{:S(2)}) %collective-permute-start.2) | collective-permute-done | bytes 327712 | tf_op jit(solution)/shard_map/ppermute | solution.py:933
  23.8 23.6 %collective-permute-done.1 = bf16[32,5120]{1,0:T(8,128)(2,1)S(1)} collective-permute-done((bf16[32,5120]{1,0:T(8,128)(2,1)}, bf16[32,5120]{1,0:T(8,128)(2,1)S(1)}, u32[]{:S(2)}, u32[]{:S(2)}) %collective-permute-start.1) | collective-permute-done | bytes 327712 | tf_op jit(solution)/shard_map/ppermute | solution.py:933
  48.6 1.6 collective-permute-start.3
  50.1 1.5 collective-permute-start.4
  54.4 39.1 %collective-permute-done.3 = bf16[4,32,5120]{2,1,0:T(8,128)(2,1)S(1)} collective-permute-done((bf16[4,32,5120]{2,1,0:T(8,128)(2,1)S(1)}, bf16[4,32,5120]{2,1,0:T(8,128)(2,1)S(1)}, u32[]{:S(2)}, u32[]{:S(2)}) %collective-permute-start.3) | collective-permute-done | bytes 1310752 | tf_op jit(solution)/shard_map/ppermute | solution.py:933
  95.8 26.8 %collective-permute-done.5 = bf16[4,32,5120]{2,1,0:T(8,128)(2,1)S(1)} collective-permute-done((bf16[4,32,5120]{2,1,0:T(8,128)(2,1)S(1)}, bf16[4,32,5120]{2,1,0:T(8,128)(2,1)S(1)}, u32[]{:S(2)}, u32[]{:S(2)}) %collective-permute-start.5) | collective-permute-done | bytes 1310752 | tf_op jit(solution)/shard_map/ppermute | solution.py:933
  125.2 7.6 %collective-permute-done.6.far_ref = bf16[16,32,5120]{2,1,0:T(8,128)(2,1)} collective-permute-done((bf16[16,32,5120]{2,1,0:T(8,128)(2,1)}, bf16[16,32,5120]{2,1,0:T(8,128)(2,1)}, u32[]{:S(2)}, u32[]{:S(2)}) %collective-permute-start.6) | collective-permute-done | bytes 5242912 | tf_op jit(solution)/shard_map/ppermute | solution.py:933
  132.8 12.9 %place_by_device.1.out_ref.query_ref.weight_ref.refs_4_.refs_5_.refs_3_ = bf16[1024,5120]{1,0:T(8,128)(2,1)} custom-call(s32[1]{0:T(128)} %bitcast.7.me_ref.refs_0_.refs_1_, bf16[16,32,5120]{2,1,0:T(8,128)(2,1)} %constant_dynamic-update-slice_fusion.near_ref, bf16[16,32,5120]{2,1,0:T(8,128)(2,1)} %collective-permute-done.6.far_ref), custom_call_target="tpu_custom_call" | custom-call | bytes 1342177280 | tf_op jit(solution)/shard_map/place_by_device/pallas_call | solution.py:755
  147.5 12.6 %norm_and_qkv.1 = (bf16[1024,1024]{1,0:T(8,128)(2,1)}, bf16[1024,3072]{1,0:T(8,128)(2,1)}) custom-call(bf16[4,32,5120]{2,1,0:T(8,128)(2,1)} %copy-done, bf16[1024,1024]{1,0:T(8,128)(2,1)} %bitcast.27, bf16[1024,3200]{1,0:T(8,128)(2,1)} %all-gather.3.cloned.1.call-done.refs_2_.refs_5_, f32[24,1024]{1,0:T(8,128)} %slice_convert_fusion.refs_3_.table_ref.refs_6_), custom_call_target="tpu_custom_call" | custom-call | flops 412316860416 | bytes 1073741824 | tf_op jit(solution)/shard_map/norm_and_qkv/pallas_call | solution.py:119
  160.1 23.7 %attend_causal.1 = (bf16[1024,1024]{1,0:T(8,128)(2,1)}, f32[8,2,1024]{2,1,0:T(2,128)}) custom-call(s32[1]{0:T(128)S(6)} %copy.41.length_ref.refs_3_, bf16[1024,3072]{1,0:T(8,128)(2,1)} %get-tuple-element.77.query_ref.key_ref.value_ref.refs_4_.refs_5_.refs_6_, bf16[1024,3072]{1,0:T(8,128)(2,1)} %get-tuple-element.77.query_ref.key_ref.value_ref.refs_4_.refs_5_.refs_6_, ...), custom_call_target="tpu_custom_call" | custom-call | flops 1099511627776 | bytes 536870912 | tf_op jit(solution)/shard_map/attend_causal/pallas_call | solution.py:270
  183.8 11.5 %self_out_norm_query.1 = (f32[1024,1024]{1,0:T(8,128)}, bf16[1024,1024]{1,0:T(8,128)(2,1)}, bf16[1024,1024]{1,0:T(8,128)(2,1)}) custom-call(bf16[1024,1024]{1,0:T(8,128)(2,1)} %bitcast.28, bf16[1024,1024]{1,0:T(8,128)(2,1)} %get-tuple-element.78.mixed_ref.refs_7_.refs_2_, ...), custom_call_target="tpu_custom_call" | custom-call | flops 274877906944 | bytes 1073741824 | tf_op jit(solution)/shard_map/self_out_norm_query/pallas_call | solution.py:143
  195.3 6.0 %memory_keys_values.1.key_ref.value_ref.refs_5_.refs_6_ = bf16[512,2048]{1,0:T(8,128)(2,1)} custom-call(bf16[512,1024]{1,0:T(8,128)(2,1)} %bitcast.30, bf16[1024,5120]{1,0:T(8,128)(2,1)} %place_by_device.1.out_ref.query_ref.weight_ref.refs_4_.refs_5_.refs_3_, f32[24,1024]{1,0:T(8,128)} %slice_convert_fusion.refs_3_.table_ref.refs_6_), custom_call_target="tpu_custom_call" | custom-call | flops 137438953472 | bytes 469762048 | tf_op jit(solution)/shard_map/memory_keys_values/pallas_call | solution.py:170
  201.3 21.5 %attend_memory.1 = (bf16[1024,1024]{1,0:T(8,128)(2,1)}, f32[8,2,1024]{2,1,0:T(2,128)}) custom-call(s32[1]{0:T(128)S(6)} %copy.42.length_ref.refs_3_, bf16[1024,1024]{1,0:T(8,128)(2,1)} %get-tuple-element.80.query_ref.refs_4_, bf16[512,2048]{1,0:T(8,128)(2,1)} %memory_keys_values.1.key_ref.value_ref.refs_5_.refs_6_, ...), custom_call_target="tpu_custom_call" | custom-call | flops 549755813888 | bytes 402653184 | tf_op jit(solution)/shard_map/attend_memory/pallas_call | solution.py:270
  222.7 8.1 %cross_out_norm.1 = (f32[1024,1024]{1,0:T(8,128)}, bf16[1024,1024]{1,0:T(8,128)(2,1)}) custom-call(f32[1024,1024]{1,0:T(8,128)} %get-tuple-element.79.hidden_ref.refs_1_, bf16[1024,1024]{1,0:T(8,128)(2,1)} %get-tuple-element.81.mixed_ref.refs_7_.refs_1_, bf16[1024,5120]{1,0:T(8,128)(2,1)} %place_by_device.1.out_ref.query_ref.weight_ref.refs_4_.refs_5_.refs_3_, ...), custom_call_target="tpu_custom_call" | custom-call | flops 137438953472 | bytes 939524096 | tf_op jit(solution)/shard_map/cross_out_norm/pallas_call | solution.py:192
  230.8 7.3 %all-gather.5.cloned.1.call-done.weight_ref = bf16[1024,8192]{1,0:T(8,128)(2,1)} async-done(((bf16[32,8192]{1,0:T(8,128)(2,1)}), bf16[1024,8192]{1,0:T(8,128)(2,1)}) %all-gather.5.cloned.1.call-update) | async-done | bytes 16777232 | tf_op jit(solution)/shard_map/all_gather | solution.py:925
  238.1 65.8 %feed_forward_both_ways.1 = (f32[1024,1024]{1,0:T(8,128)}, f32[1024,1024]{1,0:T(8,128)}, f32[4,8,1024]{2,1,0:T(8,128)}, bf16[512,8192]{1,0:T(8,128)(2,1)}, bf16[512,8192]{1,0:T(8,128)(2,1)}) custom-call(s32[1]{0:T(128)} %bitcast.7.me_ref.refs_0_.refs_1_, bf16[1024,1024]{1,0:T(8,128)(2,1)} %get-tuple-element.83.normed_ref, bf16[1024,1024]{1,0:T(8,128)(2,1)} %bitcast.25, ...), custom_call_target="tpu_custom_call" | custom-call | flops 3298534883328 | bytes 2952790016 | tf_op jit(solution)/shard_map/feed_forward_both_ways/pallas_call | solution.py:443
  304.2 13.0 %norm_back_cross_out_back.1 = (bf16[1024,1024]{1,0:T(8,128)(2,1)}, f32[1024,1024]{1,0:T(8,128)}, bf16[1024,1024]{1,0:T(8,128)(2,1)}, bf16[1024,1024]{1,0:T(8,128)(2,1)}, f32[8,1024]{1,0:T(8,128)}) custom-call(f32[1024,1024]{1,0:T(8,128)} %get-tuple-element.82.hidden_ref, f32[1024,1024]{1,0:T(8,128)} %get-tuple-element.85.made_ref, ...), custom_call_target="tpu_custom_call" | custom-call | flops 137438953472 | bytes 1744830464 | tf_op jit(solution)/shard_map/norm_back_cross_out_back/pallas_call | solution.py:504
  317.5 9.4 %plane_pieces.3 = (bf16[128,8192]{1,0:T(8,128)(2,1)}, bf16[128,8192]{1,0:T(8,128)(2,1)}, bf16[128,8192]{1,0:T(8,128)(2,1)}, bf16[128,8192]{1,0:T(8,128)(2,1)}) custom-call(bf16[1024,1024]{1,0:T(8,128)(2,1)} %get-tuple-element.87.refs_0_, bf16[512,8192]{1,0:T(8,128)(2,1)} %get-tuple-element.90.refs_1_, bf16[512,8192]{1,0:T(8,128)(2,1)} %collective-permute-done.7.refs_2_), custom_call_target="tpu_custom_call" | custom-call | bytes 1610612736 | tf_op jit(solution)/shard_map/plane_pieces/pallas_call | solution.py:842
  328.9 1.4 collective-permute-start.11
  330.3 31.2 %attend_memory_back.1 = (bf16[1024,1024]{1,0:T(8,128)(2,1)}, bf16[512,1024]{1,0:T(8,128)(2,1)}, bf16[512,1024]{1,0:T(8,128)(2,1)}, f32[8,1024]{1,0:T(8,128)}) custom-call(bf16[128,8192]{1,0:T(8,128)(2,1)} %get-tuple-element.92.refs_0_, bf16[128,8192]{1,0:T(8,128)(2,1)} %get-tuple-element.93.refs_1_, bf16[128,8192]{1,0:T(8,128)(2,1)} %get-tuple-element.94.refs_2_, ...), custom_call_target="tpu_custom_call" | custom-call | flops 824633720832 | bytes 805306368 | tf_op jit(solution)/shard_map/attend_memory_back/pallas_call | solution.py:366
  361.6 13.2 %weight_grads_by_distance.2 = (bf16[512,4096]{1,0:T(8,128)(2,1)}, bf16[512,4096]{1,0:T(8,128)(2,1)}) custom-call(s32[1]{0:T(128)} %bitcast.7.me_ref.refs_0_.refs_1_, bf16[1024,1024]{1,0:T(8,128)(2,1)} %get-tuple-element.81.mixed_ref.refs_7_.refs_1_, bf16[1024,1024]{1,0:T(8,128)(2,1)} %get-tuple-element.88.refs_2_, ...), custom_call_target="tpu_custom_call" | custom-call | flops 412316860416 | bytes 1275068416 | tf_op jit(solution)/shard_map/weight_grads_by_distance/pallas_call | solution.py:726
  374.8 13.1 %query_norm_back_self_out_back.1 = (f32[1024,1024]{1,0:T(8,128)}, bf16[1024,1024]{1,0:T(8,128)(2,1)}, bf16[1024,1024]{1,0:T(8,128)(2,1)}, f32[8,1024]{1,0:T(8,128)}) custom-call(bf16[512,4096]{1,0:T(8,128)(2,1)} %get-tuple-element.100.refs_0_, f32[1024,1024]{1,0:T(8,128)} %get-tuple-element.79.hidden_ref.refs_1_, f32[1024,1024]{1,0:T(8,128)} %get-tuple-element.101.refs_2_, ...), custom_call_target="tpu_custom_call" | custom-call | flops 274877906944 | bytes 1610612736 | tf_op jit(solution)/shard_map/query_norm_back_self_out_back/pallas_call | solution.py:554
  387.9 5.3 plane_pieces.4
  395.2 36.8 %attend_causal_back.1 = (bf16[1024,1024]{1,0:T(8,128)(2,1)}, bf16[1024,1024]{1,0:T(8,128)(2,1)}, bf16[1024,1024]{1,0:T(8,128)(2,1)}, f32[8,1024]{1,0:T(8,128)}) custom-call(bf16[128,4096]{1,0:T(8,128)(2,1)} %get-tuple-element.104.refs_0_, bf16[128,4096]{1,0:T(8,128)(2,1)} %get-tuple-element.105.refs_1_, bf16[128,4096]{1,0:T(8,128)(2,1)} %get-tuple-element.106.refs_2_, ...), custom_call_target="tpu_custom_call" | custom-call | flops 1649267441664 | bytes 1073741824 | tf_op jit(solution)/shard_map/attend_causal_back/pallas_call | solution.py:366
  432.1 1.5 collective-permute-start.14
  433.6 5.5 plane_total.3.refs_0_
  439.2 16.3 %weight_grads_by_distance.3 = (bf16[512,4096]{1,0:T(8,128)(2,1)}, bf16[512,4096]{1,0:T(8,128)(2,1)}) custom-call(bf16[128,8192]{1,0:T(8,128)(2,1)} %plane_total.3.refs_0_, s32[1]{0:T(128)} %bitcast.7.me_ref.refs_0_.refs_1_, bf16[1024,1024]{1,0:T(8,128)(2,1)} %get-tuple-element.78.mixed_ref.refs_7_.refs_2_, bf16[1024,1024]{1,0:T(8,128)(2,1)} %get-tuple-element.111.refs_3_, ...), custom_call_target="tpu_custom_call" | custom-call | flops 549755813888 | bytes 1342177280 | tf_op jit(solution)/shard_map/weight_grads_by_distance/pallas_call | solution.py:726
  455.5 10.3 %collective-permute-done.14.refs_4_ = bf16[128,4096]{1,0:T(8,128)(2,1)} collective-permute-done((bf16[128,4096]{1,0:T(8,128)(2,1)}, bf16[128,4096]{1,0:T(8,128)(2,1)}, u32[]{:S(2)}, u32[]{:S(2)}) %collective-permute-start.14) | collective-permute-done | bytes 1048608 | tf_op jit(solution)/shard_map/ppermute | solution.py:933
  465.8 3.3 plane_total.4.refs_0_
  469.2 5.5 plane_pieces.5
  475.5 1.5 collective-permute-start.22
  478.2 14.5 %qkv_norm_back.1 = (f32[1024,1024]{1,0:T(8,128)}, f32[8,1024]{1,0:T(8,128)}) custom-call(bf16[128,4096]{1,0:T(8,128)(2,1)} %get-tuple-element.119.refs_0_, bf16[128,4096]{1,0:T(8,128)(2,1)} %get-tuple-element.120.refs_1_, bf16[128,4096]{1,0:T(8,128)(2,1)} %get-tuple-element.121.refs_2_, bf16[1024,1024]{1,0:T(8,128)(2,1)} %bitcast.29, ...), custom_call_target="tpu_custom_call" | custom-call | flops 412316860416 | bytes 1476395008 | tf_op jit(solution)/shard_map/qkv_norm_back/pallas_call | solution.py:592
  492.7 6.1 %memory_back.1.refs_0_ = f32[512,1024]{1,0:T(8,128)} custom-call(f32[1024,1024]{1,0:T(8,128)} %get-tuple-element.122.refs_0_, bf16[512,1024]{1,0:T(8,128)(2,1)} %get-tuple-element.98.refs_6_.refs_1_, bf16[512,1024]{1,0:T(8,128)(2,1)} %get-tuple-element.99.refs_7_.refs_2_, bf16[1024,5120]{1,0:T(8,128)(2,1)} %place_by_device.1.out_ref.query_ref.weight_ref.refs_4_.refs_5_.refs_3_), custom_call_target="tpu_custom_call" | custom-call | flops 137438953472 | bytes 536870912 | tf_op jit(solution)/shard_map/memory_back/pallas_call | solution.py:616
  498.8 2.3 feed_own_grads.1
  501.0 9.0 %reduce-scatter.6.cloned.1.call-done.refs_1_ = bf16[32,4096]{1,0:T(8,128)(2,1)} async-done(((bf16[128,4096]{1,0:T(8,128)(2,1)}), bf16[32,4096]{1,0:T(8,128)(2,1)}) %reduce-scatter.6.cloned.1.call-update) | async-done | bytes 262160 | tf_op jit(solution)/shard_map/reduce_scatter | solution.py:962
  510.1 1.7 own_columns.2
  511.8 11.2 %collective-permute-done.22.refs_3_ = bf16[128,4096]{1,0:T(8,128)(2,1)} collective-permute-done((bf16[128,4096]{1,0:T(8,128)(2,1)}, bf16[128,4096]{1,0:T(8,128)(2,1)}, u32[]{:S(2)}, u32[]{:S(2)}) %collective-permute-start.22) | collective-permute-done | bytes 1048608 | tf_op jit(solution)/shard_map/ppermute | solution.py:933
  523.0 3.3 plane_total.5
  526.4 1.7 small_grads.1
  528.0 1.5 collective-permute-done.16
  531.5 3.9 collective-permute-done.17
  536.7 3.4 collective-permute-done.18
  540.6 9.3 %collective-permute-done.19 = f32[24,1024]{1,0:T(8,128)S(1)} collective-permute-done((f32[24,1024]{1,0:T(8,128)S(1)}, f32[24,1024]{1,0:T(8,128)S(1)}, u32[]{:S(2)}, u32[]{:S(2)}) %collective-permute-start.19) | collective-permute-done | bytes 98336 | tf_op jit(solution)/shard_map/ppermute | solution.py:933
  550.0 6.3 %collective-permute-done.20 = f32[24,1024]{1,0:T(8,128)S(1)} collective-permute-done((f32[24,1024]{1,0:T(8,128)S(1)}, f32[24,1024]{1,0:T(8,128)S(1)}, u32[]{:S(2)}, u32[]{:S(2)}) %collective-permute-start.20) | collective-permute-done | bytes 98336 | tf_op jit(solution)/shard_map/ppermute | solution.py:933
  558.2 1.7 own_columns.3
  (64 shorter events, 22.6 us)
Async XLA Ops:
  7.2 138.6 %all-gather.3.cloned.1.call-start = ((), (), s32[]{:S(2)}) async-start(), calls=%async_computation.3 | async-start | bytes 6758400 | tf_op jit(solution)/shard_map/all_gather | solution.py:925
  9.8 228.3 %all-gather.5.cloned.1.call-start = ((), (), s32[]{:S(2)}) async-start(), calls=%async_computation.4 | async-start | bytes 17301504 | tf_op jit(solution)/shard_map/all_gather | solution.py:925
  9.8 14.0 %collective-permute-start.2 = (bf16[32,5120]{1,0:T(8,128)(2,1)}, bf16[32,5120]{1,0:T(8,128)(2,1)S(1)}, u32[]{:S(2)}, u32[]{:S(2)}) collective-permute-start(bf16[32,5120]{1,0:T(8,128)(2,1)} %get-tuple-element.75), channel_id=1, source_target_pairs={{0,24},{8,16},{16,8},{24,0},{1,25},{9,17},{17,9},{25,1},{2,26},{10... | collective-permute-start | bytes 983048 | tf_op jit(solution)/shard_map/ppermute | solution.py:933
  15.0 32.5 %collective-permute-start.1 = (bf16[32,5120]{1,0:T(8,128)(2,1)}, bf16[32,5120]{1,0:T(8,128)(2,1)S(1)}, u32[]{:S(2)}, u32[]{:S(2)}) collective-permute-start(bf16[32,5120]{1,0:T(8,128)(2,1)} %get-tuple-element.75), channel_id=1, source_target_pairs={{0,16},{8,24},{16,0},{24,8},{1,17},{9,25},{17,1},{25,9},{2,18},{10... | collective-permute-start | bytes 983048 | tf_op jit(solution)/shard_map/ppermute | solution.py:933
  15.0 32.5 %collective-permute-start = (bf16[32,5120]{1,0:T(8,128)(2,1)}, bf16[32,5120]{1,0:T(8,128)(2,1)S(1)}, u32[]{:S(2)}, u32[]{:S(2)}) collective-permute-start(bf16[32,5120]{1,0:T(8,128)(2,1)} %get-tuple-element.75), channel_id=1, source_target_pairs={{0,8},{8,0},{16,24},{24,16},{1,9},{9,1},{17,25},{25,17},{2,10},{10... | collective-permute-start | bytes 983048 | tf_op jit(solution)/shard_map/ppermute | solution.py:933
  48.6 75.3 %copy-start = (bf16[4,32,5120]{2,1,0:T(8,128)(2,1)}, bf16[4,32,5120]{2,1,0:T(8,128)(2,1)S(1)}, u32[]{:S(2)}) copy-start(bf16[4,32,5120]{2,1,0:T(8,128)(2,1)S(1)} %pad_maximum_fusion.refs_0_) | copy-start | bytes 3932164
  48.6 44.9 %collective-permute-start.3 = (bf16[4,32,5120]{2,1,0:T(8,128)(2,1)S(1)}, bf16[4,32,5120]{2,1,0:T(8,128)(2,1)S(1)}, u32[]{:S(2)}, u32[]{:S(2)}) collective-permute-start(bf16[4,32,5120]{2,1,0:T(8,128)(2,1)S(1)} %pad_maximum_fusion.refs_0_), channel_id=1, source_target_pairs={{0,2},{1,3},{2,0},{3,1},{4,6},{5,7},{6,4},{7,5},{8,10},{9,11},{10,... | collective-permute-start | bytes 3932168 | tf_op jit(solution)/shard_map/ppermute | solution.py:933
  50.1 44.5 %collective-permute-start.4 = (bf16[4,32,5120]{2,1,0:T(8,128)(2,1)S(1)}, bf16[4,32,5120]{2,1,0:T(8,128)(2,1)S(1)}, u32[]{:S(2)}, u32[]{:S(2)}) collective-permute-start(bf16[4,32,5120]{2,1,0:T(8,128)(2,1)S(1)} %pad_maximum_fusion.refs_0_), channel_id=1, source_target_pairs={{0,4},{1,5},{2,6},{3,7},{4,0},{5,1},{6,2},{7,3},{8,12},{9,13},{10,... | collective-permute-start | bytes 3932168 | tf_op jit(solution)/shard_map/ppermute | solution.py:933
  51.7 71.0 %collective-permute-start.5 = (bf16[4,32,5120]{2,1,0:T(8,128)(2,1)S(1)}, bf16[4,32,5120]{2,1,0:T(8,128)(2,1)S(1)}, u32[]{:S(2)}, u32[]{:S(2)}) collective-permute-start(bf16[4,32,5120]{2,1,0:T(8,128)(2,1)S(1)} %pad_maximum_fusion.refs_0_), channel_id=1, source_target_pairs={{0,6},{1,7},{2,4},{3,5},{4,2},{5,3},{6,0},{7,1},{8,14},{9,15},{10,... | collective-permute-start | bytes 3932168 | tf_op jit(solution)/shard_map/ppermute | solution.py:933
  123.8 9.0 %collective-permute-start.6 = (bf16[16,32,5120]{2,1,0:T(8,128)(2,1)}, bf16[16,32,5120]{2,1,0:T(8,128)(2,1)}, u32[]{:S(2)}, u32[]{:S(2)}) collective-permute-start(bf16[16,32,5120]{2,1,0:T(8,128)(2,1)} %constant_dynamic-update-slice_fusion.near_ref), channel_id=1, source_target_pairs={{0,1},{1,0},{2,3},{3,2},{4,5},{5,4},{6,7},{7,6},{8,9},{9,8},{10,11... | collective-permute-start | bytes 15728648 | tf_op jit(solution)/shard_map/ppermute | solution.py:933
  123.9 374.9 %reduce-scatter.4.cloned.1.call-start = ((), (), s32[]{:S(2)}) async-start(), calls=%async_computation.5 | async-start | bytes 2621440 | tf_op jit(solution)/shard_map/reduce_scatter | solution.py:962
  303.9 13.6 %collective-permute-start.7 = (bf16[512,8192]{1,0:T(8,128)(2,1)}, bf16[512,8192]{1,0:T(8,128)(2,1)}, u32[]{:S(2)}, u32[]{:S(2)}) collective-permute-start(bf16[512,8192]{1,0:T(8,128)(2,1)} %get-tuple-element.91), channel_id=1, source_target_pairs={{0,1},{1,0},{2,3},{3,2},{4,5},{5,4},{6,7},{7,6},{8,9},{9,8},{10,11... | collective-permute-start | bytes 25165832 | tf_op jit(solution)/shard_map/ppermute | solution.py:933
  326.8 105.2 %collective-permute-start.9 = (bf16[128,8192]{1,0:T(8,128)(2,1)}, bf16[128,8192]{1,0:T(8,128)(2,1)}, u32[]{:S(2)}, u32[]{:S(2)}) collective-permute-start(bf16[128,8192]{1,0:T(8,128)(2,1)} %get-tuple-element.92.refs_0_), channel_id=1, source_target_pairs={{0,2},{1,3},{2,0},{3,1},{4,6},{5,7},{6,4},{7,5},{8,10},{9,11},{10,... | collective-permute-start | bytes 6291464 | tf_op jit(solution)/shard_map/ppermute | solution.py:933
  328.1 105.5 %collective-permute-start.10 = (bf16[128,8192]{1,0:T(8,128)(2,1)}, bf16[128,8192]{1,0:T(8,128)(2,1)}, u32[]{:S(2)}, u32[]{:S(2)}) collective-permute-start(bf16[128,8192]{1,0:T(8,128)(2,1)} %get-tuple-element.93.refs_1_), channel_id=1, source_target_pairs={{0,4},{1,5},{2,6},{3,7},{4,0},{5,1},{6,2},{7,3},{8,12},{9,13},{10,... | collective-permute-start | bytes 6291464 | tf_op jit(solution)/shard_map/ppermute | solution.py:933
  328.9 104.7 %collective-permute-start.11 = (bf16[128,8192]{1,0:T(8,128)(2,1)}, bf16[128,8192]{1,0:T(8,128)(2,1)}, u32[]{:S(2)}, u32[]{:S(2)}) collective-permute-start(bf16[128,8192]{1,0:T(8,128)(2,1)} %get-tuple-element.94.refs_2_), channel_id=1, source_target_pairs={{0,6},{1,7},{2,4},{3,5},{4,2},{5,3},{6,0},{7,1},{8,14},{9,15},{10,... | collective-permute-start | bytes 6291464 | tf_op jit(solution)/shard_map/ppermute | solution.py:933
  374.8 13.1 %collective-permute-start.8 = (bf16[512,4096]{1,0:T(8,128)(2,1)}, bf16[512,4096]{1,0:T(8,128)(2,1)}, u32[]{:S(2)}, u32[]{:S(2)}) collective-permute-start(bf16[512,4096]{1,0:T(8,128)(2,1)} %get-tuple-element.100.refs_0_), channel_id=1, source_target_pairs={{0,1},{1,0},{2,3},{3,2},{4,5},{5,4},{6,7},{7,6},{8,9},{9,8},{10,11... | collective-permute-start | bytes 12582920 | tf_op jit(solution)/shard_map/ppermute | solution.py:933
  393.2 62.3 %collective-permute-start.12 = (bf16[128,4096]{1,0:T(8,128)(2,1)}, bf16[128,4096]{1,0:T(8,128)(2,1)}, u32[]{:S(2)}, u32[]{:S(2)}) collective-permute-start(bf16[128,4096]{1,0:T(8,128)(2,1)} %get-tuple-element.104.refs_0_), channel_id=1, source_target_pairs={{0,2},{1,3},{2,0},{3,1},{4,6},{5,7},{6,4},{7,5},{8,10},{9,11},{10,... | collective-permute-start | bytes 3145736 | tf_op jit(solution)/shard_map/ppermute | solution.py:933
  394.4 61.1 %collective-permute-start.13 = (bf16[128,4096]{1,0:T(8,128)(2,1)}, bf16[128,4096]{1,0:T(8,128)(2,1)}, u32[]{:S(2)}, u32[]{:S(2)}) collective-permute-start(bf16[128,4096]{1,0:T(8,128)(2,1)} %get-tuple-element.105.refs_1_), channel_id=1, source_target_pairs={{0,4},{1,5},{2,6},{3,7},{4,0},{5,1},{6,2},{7,3},{8,12},{9,13},{10,... | collective-permute-start | bytes 3145736 | tf_op jit(solution)/shard_map/ppermute | solution.py:933
  432.1 33.8 %collective-permute-start.14 = (bf16[128,4096]{1,0:T(8,128)(2,1)}, bf16[128,4096]{1,0:T(8,128)(2,1)}, u32[]{:S(2)}, u32[]{:S(2)}) collective-permute-start(bf16[128,4096]{1,0:T(8,128)(2,1)} %get-tuple-element.106.refs_2_), channel_id=1, source_target_pairs={{0,6},{1,7},{2,4},{3,5},{4,2},{5,3},{6,0},{7,1},{8,14},{9,15},{10,... | collective-permute-start | bytes 3145736 | tf_op jit(solution)/shard_map/ppermute | solution.py:933
  439.1 70.9 %reduce-scatter.6.cloned.1.call-start = ((), (), s32[]{:S(2)}) async-start(), calls=%async_computation.6 | async-start | bytes 1310720 | tf_op jit(solution)/shard_map/reduce_scatter | solution.py:962
  455.5 13.7 %collective-permute-start.15 = (bf16[512,4096]{1,0:T(8,128)(2,1)}, bf16[512,4096]{1,0:T(8,128)(2,1)}, u32[]{:S(2)}, u32[]{:S(2)}) collective-permute-start(bf16[512,4096]{1,0:T(8,128)(2,1)} %get-tuple-element.116.refs_0_), channel_id=1, source_target_pairs={{0,1},{1,0},{2,3},{3,2},{4,5},{5,4},{6,7},{7,6},{8,9},{9,8},{10,11... | collective-permute-start | bytes 12582920 | tf_op jit(solution)/shard_map/ppermute | solution.py:933
  469.1 89.0 %reduce-scatter.8.cloned.1.call-start = ((), (), s32[]{:S(2)}) async-start(), calls=%async_computation.7 | async-start | bytes 1310720 | tf_op jit(solution)/shard_map/reduce_scatter | solution.py:962
  474.7 37.1 %collective-permute-start.21 = (bf16[128,4096]{1,0:T(8,128)(2,1)}, bf16[128,4096]{1,0:T(8,128)(2,1)}, u32[]{:S(2)}, u32[]{:S(2)}) collective-permute-start(bf16[128,4096]{1,0:T(8,128)(2,1)} %get-tuple-element.119.refs_0_), channel_id=1, source_target_pairs={{0,2},{1,3},{2,0},{3,1},{4,6},{5,7},{6,4},{7,5},{8,10},{9,11},{10,... | collective-permute-start | bytes 3145736 | tf_op jit(solution)/shard_map/ppermute | solution.py:933
  475.5 47.6 %collective-permute-start.22 = (bf16[128,4096]{1,0:T(8,128)(2,1)}, bf16[128,4096]{1,0:T(8,128)(2,1)}, u32[]{:S(2)}, u32[]{:S(2)}) collective-permute-start(bf16[128,4096]{1,0:T(8,128)(2,1)} %get-tuple-element.120.refs_1_), channel_id=1, source_target_pairs={{0,4},{1,5},{2,6},{3,7},{4,0},{5,1},{6,2},{7,3},{8,12},{9,13},{10,... | collective-permute-start | bytes 3145736 | tf_op jit(solution)/shard_map/ppermute | solution.py:933
  476.9 46.1 %collective-permute-start.23 = (bf16[128,4096]{1,0:T(8,128)(2,1)}, bf16[128,4096]{1,0:T(8,128)(2,1)}, u32[]{:S(2)}, u32[]{:S(2)}) collective-permute-start(bf16[128,4096]{1,0:T(8,128)(2,1)} %get-tuple-element.121.refs_2_), channel_id=1, source_target_pairs={{0,6},{1,7},{2,4},{3,5},{4,2},{5,3},{6,0},{7,1},{8,14},{9,15},{10,... | collective-permute-start | bytes 3145736 | tf_op jit(solution)/shard_map/ppermute | solution.py:933
  528.0 1.5 collective-permute-start.16
  530.5 4.9 collective-permute-start.17
  535.4 4.7 collective-permute-start.18
  540.1 9.8 %collective-permute-start.19 = (f32[24,1024]{1,0:T(8,128)S(1)}, f32[24,1024]{1,0:T(8,128)S(1)}, u32[]{:S(2)}, u32[]{:S(2)}) collective-permute-start(f32[24,1024]{1,0:T(8,128)S(1)} %add.31), channel_id=1, source_target_pairs={{0,8},{8,0},{16,24},{24,16},{1,9},{9,1},{17,25},{25,17},{2,10},{10... | collective-permute-start | bytes 294920 | tf_op jit(solution)/shard_map/ppermute | solution.py:933
  549.9 6.3 %collective-permute-start.20 = (f32[24,1024]{1,0:T(8,128)S(1)}, f32[24,1024]{1,0:T(8,128)S(1)}, u32[]{:S(2)}, u32[]{:S(2)}) collective-permute-start(f32[24,1024]{1,0:T(8,128)S(1)} %add.32), channel_id=1, source_target_pairs={{0,16},{8,24},{16,0},{24,8},{1,17},{9,25},{17,1},{25,9},{2,18},{10... | collective-permute-start | bytes 294920 | tf_op jit(solution)/shard_map/ppermute | solution.py:933
Sparse Core Ops, SparseCore 0:
  11.4 94.7 all-gather.2
  124.0 114.1 all-gather.4
  439.2 42.0 reduce-scatter.3
  483.6 26.4 reduce-scatter.5
  526.5 28.6 reduce-scatter.7

commit v2 on v1

--- a/solution.py
+++ b/solution.py
@@ -123,7 +123,7 @@
         out_specs=[by_rows((ROWS, width)), by_rows((ROWS, 3 * width))],
         out_shape=[out((tokens, width), bf16), out((tokens, 3 * width), bf16)],
         compiler_params=params(),
-        cost_estimate=cost(6 * tokens * width * width, 10 * tokens * width + 6 * width * width),
+        cost_estimate=cost(6 * tokens * width * width, 10 * tokens * width + 6 * width * width, 0, 1),
         name="norm_and_qkv",
     )(*waits, x, weights, table)
 
@@ -153,7 +153,7 @@
         out_specs=[block, block, block],
         out_shape=[out((tokens, width), f32), out((tokens, width), bf16), out((tokens, width), bf16)],
         compiler_params=params(),
-        cost_estimate=cost(4 * tokens * width * width, 12 * tokens * width + 4 * width * width),
+        cost_estimate=cost(4 * tokens * width * width, 12 * tokens * width + 4 * width * width, 0, 1),
         name="self_out_norm_query",
     )(x, mixed, weights, weights, table)
 
@@ -174,7 +174,7 @@
         out_specs=by_rows((ROWS, 2 * width)),
         out_shape=out((tokens, 2 * width), bf16),
         compiler_params=params(),
-        cost_estimate=cost(4 * tokens * width * width, 6 * tokens * width + 4 * width * width),
+        cost_estimate=cost(4 * tokens * width * width, 6 * tokens * width + 4 * width * width, 0, 1),
         name="memory_keys_values",
     )(memory, weights, table)
 
@@ -196,7 +196,7 @@
         out_specs=[block, block],
         out_shape=[out((tokens, width), f32), out((tokens, width), bf16)],
         compiler_params=params(),
-        cost_estimate=cost(2 * tokens * width * width, 12 * tokens * width + 2 * width * width),
+        cost_estimate=cost(2 * tokens * width * width, 12 * tokens * width + 2 * width * width, 0, 1),
         name="cross_out_norm",
     )(hidden, mixed, weights, table)
 
@@ -279,7 +279,7 @@
         out_specs=[pair_block(rows), pl.BlockSpec((1, 2, rows), lambda j: (j, 0, 0))],
         out_shape=[out((rows, width), bf16), out((pairs, 2, rows), f32)],
         compiler_params=params(),
-        cost_estimate=cost(16 * rows * keys * width, 4 * (rows + keys) * width, 16 * rows * keys),
+        cost_estimate=cost(16 * rows * keys * width, 4 * (rows + keys) * width, 16 * rows * keys, 1),
         name="attend_causal" if causal else "attend_memory",
     )(lengths, query[0], key[0], value[0])
 
@@ -313,9 +313,10 @@
     inner_sum = [
         jnp.sum(inner[side * HEAD : (side + 1) * HEAD], axis=0, keepdims=True) for side in (0, 1)
     ]
-    for at in range(rows - BLOCK, -1, -BLOCK):
-        keys = at + BLOCK if causal else keys_all
-        span = slice(at, at + BLOCK)
+    block = BLOCK if causal else rows
+    for at in range(rows - block, -1, -block):
+        keys = at + block if causal else keys_all
+        span = slice(at, at + block)
         sums = None
         for side in (0, 1):
             _, query_own, query_wide, key_own, key_wide = heads[side]
@@ -331,8 +332,8 @@
             sums = parts if sums is None else tuple(a + b for a, b in zip(sums, parts))
         query_low = (sums[0] * scale).astype(bf16)
         query_grad_ref[span, :] = query_low
-        query_total = column_sum(query_low) + (0.0 if at == rows - BLOCK else query_total)
-        if at == rows - BLOCK:
+        query_total = column_sum(query_low) + (0.0 if at == rows - block else query_total)
+        if at == rows - block:
             key_sum[...] = sums[1]
             value_sum[...] = sums[2]
         else:
@@ -480,13 +481,10 @@
 
 
 def turn_kernel(
-    hidden_ref, made_ref, back_ref, cotangent_ref, out_ref, table_ref,
-    result_ref, grad_ref, branch_ref, mixed_grad_ref, sums_ref,
+    hidden_ref, back_ref, cotangent_ref, out_ref, table_ref, grad_ref, branch_ref, mixed_grad_ref, sums_ref
 ):
-    hidden = hidden_ref[...]
     low_in = cotangent_ref[...]
-    result_ref[...] = (hidden + made_ref[...] + row_of(table_ref, BIAS + 6)).astype(bf16)
-    part, gain_grad, shift_grad = norm_back(hidden, back_ref[...], row_of(table_ref, GAIN + 2))
+    part, gain_grad, shift_grad = norm_back(hidden_ref[...], back_ref[...], row_of(table_ref, GAIN + 2))
     grad = low_in.astype(f32) + part
     grad_ref[...] = grad
     low = grad.astype(bf16)
@@ -498,25 +496,44 @@
     )
 
 
-def turn(hidden, made, back, cotangent, weights, table):
+def turn(hidden, back, cotangent, weights, table):
     tokens, width = hidden.shape
     block = by_rows((ROWS, width))
     return pl.pallas_call(
         turn_kernel,
         grid=(tokens // ROWS,),
-        in_specs=[block, block, block, block, held((width, width), (0, 4)), held(table.shape)],
-        out_specs=[block, block, block, block, pl.BlockSpec((8, width), lambda j: (0, 0))],
+        in_specs=[block, block, block, held((width, width), (0, 4)), held(table.shape)],
+        out_specs=[block, block, block, pl.BlockSpec((8, width), lambda j: (0, 0))],
         out_shape=[
-            out((tokens, width), bf16),
             out((tokens, width), f32),
             out((tokens, width), bf16),
             out((tokens, width), bf16),
             out((8, width), f32),
         ],
         compiler_params=params(),
-        cost_estimate=cost(2 * tokens * width * width, 24 * tokens * width + 2 * width * width),
+        cost_estimate=cost(2 * tokens * width * width, 18 * tokens * width + 2 * width * width),
         name="norm_back_cross_out_back",
-    )(hidden, made, back, cotangent, weights, table)
+    )(hidden, back, cotangent, weights, table)
+
+
+def result_kernel(hidden_ref, made_ref, table_ref, result_ref):
+    result_ref[...] = (hidden_ref[...] + made_ref[...] + row_of(table_ref, BIAS + 6)).astype(bf16)
+
+
+def layer_result(hidden, made, table, waits=()):
+    tokens, width = hidden.shape
+    block = by_rows((ROWS, width))
+    kernel, in_specs = after(waits, result_kernel, [block, block, held(table.shape)])
+    return pl.pallas_call(
+        kernel,
+        grid=(tokens // ROWS,),
+        in_specs=in_specs,
+        out_specs=block,
+        out_shape=out((tokens, width), bf16),
+        compiler_params=params(),
+        cost_estimate=cost(0, 10 * tokens * width),
+        name="layer_result",
+    )(*waits, hidden, made, table)
 
 
 def middle_back_kernel(
@@ -677,16 +694,29 @@
     )(*sums)
 
 
-def split_grads_kernel(picks, dp_size, own, me_ref, *refs):
+def split_grads_kernel(picks, dp_size, own, count, me_ref, *refs):
     step = pl.program_id(0)
-    keep_ref, send_ref = refs[-2:]
+    keep_ref, send_ref = refs[count : count + 2]
+    held_refs, sems = refs[count + 2 : -1], refs[-1]
     half, wide = keep_ref.shape
+    copies = [pltpu.make_async_copy(refs[i], held_refs[i], sems.at[i]) for i in range(count)]
+
+    @pl.when(step == 0)
+    def _():
+        for copy in copies:
+            copy.start()
+
+    known = set()
     for at, (left, right, column) in enumerate(picks):
+        fresh = sorted({left, right} - known)
+        known.update(fresh)
 
         @pl.when(step == at)
-        def _(left=left, right=right, column=column):
+        def _(left=left, right=right, column=column, fresh=fresh):
+            for i in fresh:
+                copies[i].wait()
             for low in (0, half):
-                made = tn(refs[left][:, low : low + half], refs[right][:, column : column + wide])
+                made = tn(held_refs[left][:, low : low + half], held_refs[right][:, column : column + wide])
                 first_pair = low // (2 * own)
                 spread(made.astype(bf16), first_pair, own, dp_size, me_ref, keep_ref, send_ref, slice(0, wide))
 
@@ -720,8 +750,8 @@
     half = pl.BlockSpec((width // 2, wide), lambda j: (0, j))
     kernel, in_specs = after(
         waits,
-        functools.partial(split_grads_kernel, tuple(picks), dp_size, own),
-        [pl.BlockSpec(memory_space=pltpu.SMEM)] + [held(array.shape) for array in arrays],
+        functools.partial(split_grads_kernel, tuple(picks), dp_size, own, len(arrays)),
+        [pl.BlockSpec(memory_space=pltpu.SMEM)] + [pl.BlockSpec(memory_space=pl.ANY)] * len(arrays),
     )
     return pl.pallas_call(
         kernel,
@@ -729,37 +759,60 @@
         in_specs=in_specs,
         out_specs=[half, half],
         out_shape=[out((width // 2, columns), bf16)] * 2,
+        scratch_shapes=[pltpu.VMEM(array.shape, bf16) for array in arrays]
+        + [pltpu.SemaphoreType.DMA((len(arrays),))],
         compiler_params=params(),
         cost_estimate=cost(flops, nbytes),
         name="weight_grads_by_distance",
     )(*waits, mine, *arrays)
 
 
-def place_kernel(me_ref, near_ref, far_ref, whole_ref):
-    own = near_ref.shape[1]
-    upper = lax.rem(me_ref[0], 2) == 1
-    near, far = near_ref[0], far_ref[0]
-    whole_ref[:own, :] = jnp.where(upper, far, near)
-    whole_ref[own:, :] = jnp.where(upper, near, far)
+def near_kernel(*refs):
+    whole_ref = refs[-1]
+    rows = refs[0].shape[0]
+    for at, ref in enumerate(refs[:-1]):
+        whole_ref[at * rows : (at + 1) * rows] = ref[...]
+
+
+def near_rows(pieces, waits=()):
+    rows, own, columns = pieces[0].shape
+    lanes = 1024
+    block = pl.BlockSpec((rows, own, lanes), lambda j: (0, 0, j))
+    kernel, in_specs = after(waits, near_kernel, [block] * len(pieces))
+    return pl.pallas_call(
+        kernel,
+        grid=(columns // lanes,),
+        in_specs=in_specs,
+        out_specs=pl.BlockSpec((len(pieces) * rows, own, lanes), lambda j: (0, 0, j)),
+        out_shape=out((len(pieces) * rows, own, columns), bf16),
+        compiler_params=params(),
+        cost_estimate=cost(0, 4 * len(pieces) * rows * own * columns),
+        name="near_rows",
+    )(*waits, *pieces)
+
+
+def place_kernel(dp_size, me_ref, near_ref, far_ref, whole_ref):
+    pairs, own = near_ref.shape[:2]
+    planes = pairs // dp_size
+    mine = me_ref[0]
+    side = lax.rem(mine, 2)
+    mine_pair = lax.shift_right_logical(mine, 1)
+    for at in range(pairs):
+        pair = lax.bitwise_xor(mine_pair, at % dp_size * planes + at // dp_size)
+        for ref, core in ((near_ref, side), (far_ref, 1 - side)):
+            rows = pl.ds(pl.multiple_of((2 * pair + core) * own, own), own)
+            whole_ref[rows, :] = ref[at]
 
 
 def place(mine, near, far, dp_size):
     pairs, own, columns = near.shape
-    planes = pairs // dp_size
-
-    def pair_at(j, me_ref):
-        away = lax.rem(j, dp_size) * planes + lax.div(j, dp_size)
-        return lax.bitwise_xor(lax.shift_right_logical(me_ref[0], 1), away), 0
-
-    block = pl.BlockSpec((1, own, columns), lambda j, me_ref: (j, 0, 0))
-    return pl.pallas_call(
-        place_kernel,
-        grid_spec=pltpu.PrefetchScalarGridSpec(
-            num_scalar_prefetch=1,
-            grid=(pairs,),
-            in_specs=[block, block],
-            out_specs=pl.BlockSpec((2 * own, columns), pair_at),
-        ),
+    lanes = 1024
+    block = pl.BlockSpec((pairs, own, lanes), lambda j: (0, 0, j))
+    return pl.pallas_call(
+        functools.partial(place_kernel, dp_size),
+        grid=(columns // lanes,),
+        in_specs=[pl.BlockSpec(memory_space=pltpu.SMEM), block, block],
+        out_specs=pl.BlockSpec((2 * pairs * own, lanes), lambda j: (0, j)),
         out_shape=out((2 * pairs * own, columns), bf16),
         compiler_params=params(),
         cost_estimate=cost(0, 8 * pairs * own * columns),
@@ -1023,7 +1076,7 @@
     parts = [(triple, at * (width // PAIR), width) for at in range(3)]
     self_mixed, self_stats = attend(target_lengths, *parts, True)
     if by_distance:
-        near = jnp.concatenate([line] + plane)
+        near = near_rows([line] + plane, (triple,))
         second = place(mine, near, exchange(near, "fsdp", fsdp_size, 1), dp_size)
     else:
         second = gather(second_shard)
@@ -1033,13 +1086,11 @@
     cross_mixed, cross_stats = attend(memory_lengths, *cross_parts, False)
     hidden_two, normed_three = late(hidden_one, cross_mixed, second, table)
     made, back, hidden_bias_sums, *feed_grads = feed(normed_three, branch, third, table, split)
-    result, grad_two, branch_two, mixed_grad, sums_three = turn(
-        hidden_two, made, back, branch, second, table
-    )
+    grad_two, branch_two, mixed_grad, sums_three = turn(hidden_two, back, branch, second, table)
     waits = ()
     if by_distance:
         feed_got = exchange(feed_grads[1], "fsdp", fsdp_size, 1)
-        [(feed_sent, feed_plane)] = scatter_plane(feed_grads[0], feed_got, fsdp_size, (result,))
+        [(feed_sent, feed_plane)] = scatter_plane(feed_grads[0], feed_got, fsdp_size, (sums_three,))
         waits = tuple(feed_sent)
     else:
         feed_own = scatter_sum(feed_grads[0])
@@ -1073,15 +1124,16 @@
         feed_own = scatter_line(feed_total)
         self_keep, self_send = weight_grads(self_pairs, split, (feed_total,))
         self_got = exchange(self_send, "fsdp", fsdp_size, 1)
-        cross_total = plane_total(cross_plane, (self_send,), 4096)
+        memory_grad = memory_back(key_grad, value_grad, second, (self_send,))
+        [(self_sent, self_plane)] = scatter_plane(self_keep, self_got, fsdp_size, (memory_grad,))
+        cross_total = plane_total(cross_plane, (self_sent[0],))
         cross_own = scatter_line(cross_total)
-        [(self_sent, self_plane)] = scatter_plane(self_keep, self_got, fsdp_size, (cross_total,))
-        waits = tuple(self_sent)
+        waits = (*self_sent, cross_total)
     input_grad, sums_one = entry_back(x, grad_one, self_grads, first, table, waits)
     sums = small_grads(sums_one, sums_two, sums_three, cross_sums, self_sums, hidden_bias_sums)
     if by_distance:
-        memory_grad = memory_back(key_grad, value_grad, second, (input_grad,))
-        inner_own, outer_own = feed_own_grads([feed_own], width, (memory_grad,))
+        result = layer_result(hidden_two, made, table, (input_grad,))
+        inner_own, outer_own = feed_own_grads([feed_own], width, (result,))
         cross_out_own, query_own, pair_own = cut_columns(
             cross_own, (0, width, 2 * width, 4 * width), (inner_own,)
         )
@@ -1089,6 +1141,7 @@
         self_own = scatter_line(self_total)
         self_out_own, triple_own = cut_columns(self_own, (0, width, 4 * width))
     else:
+        result = layer_result(hidden_two, made, table)
         memory_grad = memory_back(key_grad, value_grad, second)
         cross_own = scatter_sum(weight_grads(cross_pairs)).astype(f32)
         cross_out_own, query_own = cross_own[:, :width], cross_own[:, width : 2 * width]

time: 576 us -> 550 us (0.955)
  waiting for transfers between devices: 166 us -> 152 us
  local copies, waits for them, and re-layouts: 10.4 us -> 2.91 us
    ppermute x24, waiting for transfers between devices: 150 us -> 72.6 us  [exchange(): return lax.ppermute(array, axis, [(i, i ^ distance) for i in range(size)])]
    all_gather x2, waiting for transfers between devices: 7.32 us -> 66.1 us  [gather(): return lax.all_gather(shard, AXES, axis=0, tiled=True)]
    pallas_call x1 -> x3, Pallas kernels: 12.9 us -> 21.4 us  [the longest x1 9.78 us: place(): pl.pallas_call(functools.partial(place_kernel, dp_size), grid=(columns //...]
    unnamed x9 -> x5, local copies, waits for them, and re-layouts: 6.51 us -> 0.15 us
  transfers between devices with their start and end apart: 29 -> 29, of which waited for: 15 -> 16; matrix products, arithmetic and copies ran while one was open for 2% -> 1% of each run, Pallas kernels for 47% -> 49%
where the time goes in v2:
time: 550 us; the launch traced here: 541 us
  Pallas kernels  345 us (63%)
  waiting for transfers between devices  152 us (28%)
  starting transfers between devices  22.7 us (4%)
  between operations  15.5 us (3%)
    ppermute x24, waiting for transfers between devices, exchange(): return lax.ppermute(array, axis, [(i, i ^ distance) for i in range(size)])  72.6 us
    all_gather x2, waiting for transfers between devices, gather(): return lax.all_gather(shard, AXES, axis=0, tiled=True)  66.1 us
    pallas_call x1, Pallas kernels, feed(): pl.pallas_call(functools.partial(feed_kernel, split[1:] or None), grid=(s...  65.7 us
    pallas_call x2, Pallas kernels, attend_back(): pl.pallas_call(kernel, grid=(pairs,), in_specs=in_specs, out_specs=[pair_...  64.5 us
    pallas_call x2, Pallas kernels, attend(): pl.pallas_call(functools.partial(attend_kernel, causal), grid=(pairs,), i...  45.1 us
    pallas_call x2, Pallas kernels, weight_grads(): pl.pallas_call(kernel, grid=(len(picks),), in_specs=in_specs, out_specs=[...  24.7 us
    ppermute x24, starting transfers between devices, exchange(): return lax.ppermute(array, axis, [(i, i ^ distance) for i in range(size)])  22.5 us
    pallas_call x3, Pallas kernels, plane_pieces(): pl.pallas_call(kernel, grid=(steps,), in_specs=in_specs, out_specs=[pl.Bl...  19.8 us
  transfers between devices with their start and end apart: 29, of which 16 were waited for; matrix products, arithmetic and copies ran while one was open for 1% of the time, Pallas kernels for 49%

profile of v2, /device:TPU:0, one launch (start us, length us, event | category | flops | bytes accessed | tf_op | source)
XLA Modules:
  0.0 541.3 jit_solution(14436089565040509672)
XLA Ops:
  7.2 2.5 shards_to_gather.1
  10.6 5.1 collective-permute-start.2
  16.3 8.4 %collective-permute-done.2 = bf16[32,5120]{1,0:T(8,128)(2,1)S(1)} collective-permute-done((bf16[32,5120]{1,0:T(8,128)(2,1)}, bf16[32,5120]{1,0:T(8,128)(2,1)S(1)}, u32[]{:S(2)}, u32[]{:S(2)}) %collective-permute-start.2) | collective-permute-done | bytes 327712 | tf_op jit(solution)/shard_map/ppermute | solution.py:986
  24.8 23.4 %collective-permute-done.1 = bf16[32,5120]{1,0:T(8,128)(2,1)S(1)} collective-permute-done((bf16[32,5120]{1,0:T(8,128)(2,1)}, bf16[32,5120]{1,0:T(8,128)(2,1)S(1)}, u32[]{:S(2)}, u32[]{:S(2)}) %collective-permute-start.1) | collective-permute-done | bytes 327712 | tf_op jit(solution)/shard_map/ppermute | solution.py:986
  49.3 1.6 collective-permute-start.3
  50.9 1.5 collective-permute-start.4
  52.9 54.2 %all-gather.3.cloned.1.call-done.refs_2_.refs_6_ = bf16[1024,3200]{1,0:T(8,128)(2,1)} async-done(((bf16[32,3200]{1,0:T(8,128)(2,1)}), bf16[1024,3200]{1,0:T(8,128)(2,1)}) %all-gather.3.cloned.1.call-update) | async-done | bytes 6553616 | tf_op jit(solution)/shard_map/all_gather | solution.py:978
  108.9 12.6 %norm_and_qkv.1 = (bf16[1024,1024]{1,0:T(8,128)(2,1)}, bf16[1024,3072]{1,0:T(8,128)(2,1)}) custom-call(bf16[4,32,5120]{2,1,0:T(8,128)(2,1)} %copy-done, bf16[1024,1024]{1,0:T(8,128)(2,1)} %bitcast.15, bf16[1024,3200]{1,0:T(8,128)(2,1)} %all-gather.3.cloned.1.call-done.refs_2_.refs_6_, f32[24,1024]{1,0:T(8,128)} %slice_convert_fusion.refs_3_.table_ref.refs_6_.refs_7_), custom_call_target="tpu_custom_call" | custom-call | flops 6442450944 | bytes 16777216 | tf_op jit(solution)/shard_map/norm_and_qkv/pallas_call | solution.py:119
  121.5 4.7 collective-permute-done.5.refs_4_
  126.1 6.5 %near_rows.1.near_ref = bf16[16,32,5120]{2,1,0:T(8,128)(2,1)} custom-call(bf16[1024,3072]{1,0:T(8,128)(2,1)} %get-tuple-element.76.query_ref.key_ref.value_ref.refs_0_.refs_4_.refs_5_.refs_6_, bf16[4,32,5120]{2,1,0:T(8,128)(2,1)} %copy-done, bf16[4,32,5120]{2,1,0:T(8,128)(2,1)} %copy-done.1, bf16[4,32,5120]{2,1,0:T(8,128)(2,1)} %collective-permute-done.4.refs_3_, ...), custom_call_target="tpu_custom_call" | custom-call | bytes 671088640 | tf_op jit(solution)/shard_map/near_rows/pallas_call | solution.py:782
  133.9 23.7 %attend_causal.1 = (bf16[1024,1024]{1,0:T(8,128)(2,1)}, f32[8,2,1024]{2,1,0:T(2,128)}) custom-call(s32[1]{0:T(128)S(6)} %copy.35.length_ref.refs_3_, bf16[1024,3072]{1,0:T(8,128)(2,1)} %get-tuple-element.76.query_ref.key_ref.value_ref.refs_0_.refs_4_.refs_5_.refs_6_, ...), custom_call_target="tpu_custom_call" | custom-call | flops 17179869184 | bytes 8388608 | tf_op jit(solution)/shard_map/attend_causal/pallas_call | solution.py:270
  157.6 9.8 %place_by_device.1.out_ref.query_ref.weight_ref.refs_4_.refs_5_.refs_3_ = bf16[1024,5120]{1,0:T(8,128)(2,1)} custom-call(s32[1]{0:T(128)} %bitcast.me_ref.refs_0_.refs_1_, bf16[16,32,5120]{2,1,0:T(8,128)(2,1)} %near_rows.1.near_ref, bf16[16,32,5120]{2,1,0:T(8,128)(2,1)} %collective-permute-done.6.far_ref), custom_call_target="tpu_custom_call" | custom-call | bytes 1342177280 | tf_op jit(solution)/shard_map/place_by_device/pallas_call | solution.py:811
  167.4 5.9 %memory_keys_values.1.key_ref.value_ref.refs_5_.refs_6_ = bf16[512,2048]{1,0:T(8,128)(2,1)} custom-call(bf16[512,1024]{1,0:T(8,128)(2,1)} %bitcast.19, bf16[1024,5120]{1,0:T(8,128)(2,1)} %place_by_device.1.out_ref.query_ref.weight_ref.refs_4_.refs_5_.refs_3_, f32[24,1024]{1,0:T(8,128)} %slice_convert_fusion.refs_3_.table_ref.refs_6_.refs_7_), custom_call_target="tpu_custom_call" | custom-call | flops 2147483648 | bytes 7340032 | tf_op jit(solution)/shard_map/memory_keys_values/pallas_call | solution.py:170
  173.3 10.6 %self_out_norm_query.1 = (f32[1024,1024]{1,0:T(8,128)}, bf16[1024,1024]{1,0:T(8,128)(2,1)}, bf16[1024,1024]{1,0:T(8,128)(2,1)}) custom-call(bf16[1024,1024]{1,0:T(8,128)(2,1)} %bitcast.16, bf16[1024,1024]{1,0:T(8,128)(2,1)} %get-tuple-element.77.mixed_ref.refs_7_.refs_2_, ...), custom_call_target="tpu_custom_call" | custom-call | flops 4294967296 | bytes 16777216 | tf_op jit(solution)/shard_map/self_out_norm_query/pallas_call | solution.py:143
  183.9 21.4 %attend_memory.1 = (bf16[1024,1024]{1,0:T(8,128)(2,1)}, f32[8,2,1024]{2,1,0:T(2,128)}) custom-call(s32[1]{0:T(128)S(6)} %copy.36.length_ref.refs_3_, bf16[1024,1024]{1,0:T(8,128)(2,1)} %get-tuple-element.78.query_ref.refs_4_, bf16[512,2048]{1,0:T(8,128)(2,1)} %memory_keys_values.1.key_ref.value_ref.refs_5_.refs_6_, ...), custom_call_target="tpu_custom_call" | custom-call | flops 8589934592 | bytes 6291456 | tf_op jit(solution)/shard_map/attend_memory/pallas_call | solution.py:270
  205.3 7.9 %cross_out_norm.1 = (f32[1024,1024]{1,0:T(8,128)}, bf16[1024,1024]{1,0:T(8,128)(2,1)}) custom-call(f32[1024,1024]{1,0:T(8,128)} %get-tuple-element.80.hidden_ref.refs_1_, bf16[1024,1024]{1,0:T(8,128)(2,1)} %get-tuple-element.79.mixed_ref.refs_7_.refs_1_, bf16[1024,5120]{1,0:T(8,128)(2,1)} %place_by_device.1.out_ref.query_ref.weight_ref.refs_4_.refs_5_.refs_3_, ...), custom_call_target="tpu_custom_call" | custom-call | flops 2147483648 | bytes 14680064 | tf_op jit(solution)/shard_map/cross_out_norm/pallas_call | solution.py:192
  213.2 11.9 %all-gather.5.cloned.1.call-done.weight_ref = bf16[1024,8192]{1,0:T(8,128)(2,1)} async-done(((bf16[32,8192]{1,0:T(8,128)(2,1)}), bf16[1024,8192]{1,0:T(8,128)(2,1)}) %all-gather.5.cloned.1.call-update) | async-done | bytes 16777232 | tf_op jit(solution)/shard_map/all_gather | solution.py:978
  225.1 65.7 %feed_forward_both_ways.1 = (f32[1024,1024]{1,0:T(8,128)}, f32[1024,1024]{1,0:T(8,128)}, f32[4,8,1024]{2,1,0:T(8,128)}, bf16[512,8192]{1,0:T(8,128)(2,1)}, bf16[512,8192]{1,0:T(8,128)(2,1)}) custom-call(s32[1]{0:T(128)} %bitcast.me_ref.refs_0_.refs_1_, bf16[1024,1024]{1,0:T(8,128)(2,1)} %get-tuple-element.82.normed_ref, bf16[1024,1024]{1,0:T(8,128)(2,1)} %bitcast.27, ...), custom_call_target="tpu_custom_call" | custom-call | flops 3298534883328 | bytes 2952790016 | tf_op jit(solution)/shard_map/feed_forward_both_ways/pallas_call | solution.py:444
  291.2 11.2 %norm_back_cross_out_back.1 = (f32[1024,1024]{1,0:T(8,128)}, bf16[1024,1024]{1,0:T(8,128)(2,1)}, bf16[1024,1024]{1,0:T(8,128)(2,1)}, f32[8,1024]{1,0:T(8,128)}) custom-call(f32[1024,1024]{1,0:T(8,128)} %get-tuple-element.81.hidden_ref.refs_1_, f32[1024,1024]{1,0:T(8,128)} %get-tuple-element.84.back_ref, bf16[1024,1024]{1,0:T(8,128)(2,1)} %bitcast.28, ...), custom_call_target="tpu_custom_call" | custom-call | flops 137438953472 | bytes 1342177280 | tf_op jit(solution)/shard_map/norm_back_cross_out_back/pallas_call | solution.py:502
  302.4 2.0 collective-permute-done.7.refs_2_
  304.4 9.3 %plane_pieces.3 = (bf16[128,8192]{1,0:T(8,128)(2,1)}, bf16[128,8192]{1,0:T(8,128)(2,1)}, bf16[128,8192]{1,0:T(8,128)(2,1)}, bf16[128,8192]{1,0:T(8,128)(2,1)}) custom-call(f32[8,1024]{1,0:T(8,128)} %get-tuple-element.87.refs_0_.three_ref, bf16[512,8192]{1,0:T(8,128)(2,1)} %get-tuple-element.88.refs_1_, bf16[512,8192]{1,0:T(8,128)(2,1)} %collective-permute-done.7.refs_2_), custom_call_target="tpu_custom_call" | custom-call | bytes 1610612736 | tf_op jit(solution)/shard_map/plane_pieces/pallas_call | solution.py:895
  315.8 1.4 collective-permute-start.11
  317.2 27.8 %attend_memory_back.1 = (bf16[1024,1024]{1,0:T(8,128)(2,1)}, bf16[512,1024]{1,0:T(8,128)(2,1)}, bf16[512,1024]{1,0:T(8,128)(2,1)}, f32[8,1024]{1,0:T(8,128)}) custom-call(bf16[128,8192]{1,0:T(8,128)(2,1)} %get-tuple-element.90.refs_0_, bf16[128,8192]{1,0:T(8,128)(2,1)} %get-tuple-element.91.refs_1_, bf16[128,8192]{1,0:T(8,128)(2,1)} %get-tuple-element.92.refs_2_, ...), custom_call_target="tpu_custom_call" | custom-call | flops 824633720832 | bytes 805306368 | tf_op jit(solution)/shard_map/attend_memory_back/pallas_call | solution.py:367
  345.0 11.2 %weight_grads_by_distance.2 = (bf16[512,4096]{1,0:T(8,128)(2,1)}, bf16[512,4096]{1,0:T(8,128)(2,1)}) custom-call(s32[1]{0:T(128)} %bitcast.me_ref.refs_0_.refs_1_, bf16[1024,1024]{1,0:T(8,128)(2,1)} %get-tuple-element.79.mixed_ref.refs_7_.refs_1_, bf16[1024,1024]{1,0:T(8,128)(2,1)} %get-tuple-element.85.refs_2_, ...), custom_call_target="tpu_custom_call" | custom-call | flops 412316860416 | bytes 1275068416 | tf_op jit(solution)/shard_map/weight_grads_by_distance/pallas_call | solution.py:756
  356.3 13.1 %query_norm_back_self_out_back.1 = (f32[1024,1024]{1,0:T(8,128)}, bf16[1024,1024]{1,0:T(8,128)(2,1)}, bf16[1024,1024]{1,0:T(8,128)(2,1)}, f32[8,1024]{1,0:T(8,128)}) custom-call(bf16[512,4096]{1,0:T(8,128)(2,1)} %get-tuple-element.98.refs_0_, f32[1024,1024]{1,0:T(8,128)} %get-tuple-element.80.hidden_ref.refs_1_, f32[1024,1024]{1,0:T(8,128)} %get-tuple-element.99.refs_2_, ...), custom_call_target="tpu_custom_call" | custom-call | flops 274877906944 | bytes 1610612736 | tf_op jit(solution)/shard_map/query_norm_back_self_out_back/pallas_call | solution.py:571
  369.3 5.3 plane_pieces.4
  376.7 36.8 %attend_causal_back.1 = (bf16[1024,1024]{1,0:T(8,128)(2,1)}, bf16[1024,1024]{1,0:T(8,128)(2,1)}, bf16[1024,1024]{1,0:T(8,128)(2,1)}, f32[8,1024]{1,0:T(8,128)}) custom-call(bf16[128,4096]{1,0:T(8,128)(2,1)} %get-tuple-element.102.refs_0_, bf16[128,4096]{1,0:T(8,128)(2,1)} %get-tuple-element.103.refs_1_, bf16[128,4096]{1,0:T(8,128)(2,1)} %get-tuple-element.104.refs_2_, ...), custom_call_target="tpu_custom_call" | custom-call | flops 1649267441664 | bytes 1073741824 | tf_op jit(solution)/shard_map/attend_causal_back/pallas_call | solution.py:367
  413.5 1.5 collective-permute-start.15
  414.9 5.5 %plane_total.3.refs_0_ = bf16[128,8192]{1,0:T(8,128)(2,1)} custom-call(f32[8,1024]{1,0:T(8,128)} %get-tuple-element.107.refs_0_.self_ref, bf16[128,8192]{1,0:T(8,128)(2,1)} %get-tuple-element.108.refs_1_, bf16[128,8192]{1,0:T(8,128)(2,1)} %collective-permute-done.9.refs_2_, bf16[128,8192]{1,0:T(8,128)(2,1)} %collective-permute-done.10.refs_3_, ...), custom_call_target="tpu_custom_call" | custom-call | bytes 671088640 | tf_op jit(solution)/shard_map/plane_total/pallas_call | solution.py:921
  420.5 13.5 %weight_grads_by_distance.3 = (bf16[512,4096]{1,0:T(8,128)(2,1)}, bf16[512,4096]{1,0:T(8,128)(2,1)}) custom-call(bf16[128,8192]{1,0:T(8,128)(2,1)} %plane_total.3.refs_0_, s32[1]{0:T(128)} %bitcast.me_ref.refs_0_.refs_1_, bf16[1024,1024]{1,0:T(8,128)(2,1)} %get-tuple-element.77.mixed_ref.refs_7_.refs_2_, bf16[1024,1024]{1,0:T(8,128)(2,1)} %get-tuple-element.109.refs_3_, ...), custom_call_target="tpu_custom_call" | custom-call | flops 549755813888 | bytes 1342177280 | tf_op jit(solution)/shard_map/weight_grads_by_distance/pallas_call | solution.py:756
  434.1 6.1 %memory_back.1.refs_0_ = f32[512,1024]{1,0:T(8,128)} custom-call(bf16[512,4096]{1,0:T(8,128)(2,1)} %get-tuple-element.114.refs_0_, bf16[512,1024]{1,0:T(8,128)(2,1)} %get-tuple-element.96.refs_6_.refs_1_, bf16[512,1024]{1,0:T(8,128)(2,1)} %get-tuple-element.97.refs_7_.refs_2_, ...), custom_call_target="tpu_custom_call" | custom-call | flops 137438953472 | bytes 536870912 | tf_op jit(solution)/shard_map/memory_back/pallas_call | solution.py:633
  441.6 5.3 plane_pieces.5
  450.5 2.9 collective-permute-done.15.refs_4_
  453.4 3.2 plane_total.4.refs_3_
  456.7 14.6 %qkv_norm_back.1 = (f32[1024,1024]{1,0:T(8,128)}, f32[8,1024]{1,0:T(8,128)}) custom-call(bf16[128,4096]{1,0:T(8,128)(2,1)} %get-tuple-element.116.refs_0_, bf16[128,4096]{1,0:T(8,128)(2,1)} %get-tuple-element.117.refs_1_, bf16[128,4096]{1,0:T(8,128)(2,1)} %get-tuple-element.118.refs_2_, bf16[128,4096]{1,0:T(8,128)(2,1)} %plane_total.4.refs_3_, ...), custom_call_target="tpu_custom_call" | custom-call | flops 412316860416 | bytes 1476395008 | tf_op jit(solution)/shard_map/qkv_norm_back/pallas_call | solution.py:609
  471.2 5.2 layer_result.1.refs_0_
  476.4 2.3 feed_own_grads.1
  478.7 12.8 %reduce-scatter.6.cloned.1.call-done.refs_1_ = bf16[32,4096]{1,0:T(8,128)(2,1)} async-done(((bf16[128,4096]{1,0:T(8,128)(2,1)}), bf16[32,4096]{1,0:T(8,128)(2,1)}) %reduce-scatter.6.cloned.1.call-update) | async-done | bytes 262160 | tf_op jit(solution)/shard_map/reduce_scatter | solution.py:1015
  491.5 1.7 own_columns.2
  493.2 4.5 collective-permute-done.23.refs_4_
  497.7 3.2 plane_total.5
  500.9 1.7 small_grads.1
  502.6 1.5 collective-permute-done.16
  505.8 4.1 collective-permute-done.17
  510.8 3.8 collective-permute-done.18
  515.1 9.5 %collective-permute-done.19 = f32[24,1024]{1,0:T(8,128)S(1)} collective-permute-done((f32[24,1024]{1,0:T(8,128)S(1)}, f32[24,1024]{1,0:T(8,128)S(1)}, u32[]{:S(2)}, u32[]{:S(2)}) %collective-permute-start.19) | collective-permute-done | bytes 98336 | tf_op jit(solution)/shard_map/ppermute | solution.py:986
  524.7 6.2 %collective-permute-done.20 = f32[24,1024]{1,0:T(8,128)S(1)} collective-permute-done((f32[24,1024]{1,0:T(8,128)S(1)}, f32[24,1024]{1,0:T(8,128)S(1)}, u32[]{:S(2)}, u32[]{:S(2)}) %collective-permute-start.20) | collective-permute-done | bytes 98336 | tf_op jit(solution)/shard_map/ppermute | solution.py:986
  532.8 1.7 own_columns.3
  (61 shorter events, 19.6 us)
Async XLA Ops:
  7.2 99.9 %all-gather.3.cloned.1.call-start = ((), (), s32[]{:S(2)}) async-start(), calls=%async_computation.3 | async-start | bytes 6758400 | tf_op jit(solution)/shard_map/all_gather | solution.py:978
  9.8 215.4 %all-gather.5.cloned.1.call-start = ((), (), s32[]{:S(2)}) async-start(), calls=%async_computation.4 | async-start | bytes 17301504 | tf_op jit(solution)/shard_map/all_gather | solution.py:978
  10.5 465.9 %reduce-scatter.4.cloned.1.call-start = ((), (), s32[]{:S(2)}) async-start(), calls=%async_computation.5 | async-start | bytes 2621440 | tf_op jit(solution)/shard_map/reduce_scatter | solution.py:1015
  10.6 14.2 %collective-permute-start.2 = (bf16[32,5120]{1,0:T(8,128)(2,1)}, bf16[32,5120]{1,0:T(8,128)(2,1)S(1)}, u32[]{:S(2)}, u32[]{:S(2)}) collective-permute-start(bf16[32,5120]{1,0:T(8,128)(2,1)} %get-tuple-element.74), channel_id=1, source_target_pairs={{0,24},{8,16},{16,8},{24,0},{1,25},{9,17},{17,9},{25,1},{2,26},{10... | collective-permute-start | bytes 983048 | tf_op jit(solution)/shard_map/ppermute | solution.py:986
  15.7 32.5 %collective-permute-start.1 = (bf16[32,5120]{1,0:T(8,128)(2,1)}, bf16[32,5120]{1,0:T(8,128)(2,1)S(1)}, u32[]{:S(2)}, u32[]{:S(2)}) collective-permute-start(bf16[32,5120]{1,0:T(8,128)(2,1)} %get-tuple-element.74), channel_id=1, source_target_pairs={{0,16},{8,24},{16,0},{24,8},{1,17},{9,25},{17,1},{25,9},{2,18},{10... | collective-permute-start | bytes 983048 | tf_op jit(solution)/shard_map/ppermute | solution.py:986
  15.7 32.5 %collective-permute-start = (bf16[32,5120]{1,0:T(8,128)(2,1)}, bf16[32,5120]{1,0:T(8,128)(2,1)S(1)}, u32[]{:S(2)}, u32[]{:S(2)}) collective-permute-start(bf16[32,5120]{1,0:T(8,128)(2,1)} %get-tuple-element.74), channel_id=1, source_target_pairs={{0,8},{8,0},{16,24},{24,16},{1,9},{9,1},{17,25},{25,17},{2,10},{10... | collective-permute-start | bytes 983048 | tf_op jit(solution)/shard_map/ppermute | solution.py:986
  49.3 59.6 %copy-start = (bf16[4,32,5120]{2,1,0:T(8,128)(2,1)}, bf16[4,32,5120]{2,1,0:T(8,128)(2,1)S(1)}, u32[]{:S(2)}) copy-start(bf16[4,32,5120]{2,1,0:T(8,128)(2,1)S(1)} %pad_maximum_fusion.refs_0_.refs_1_) | copy-start | bytes 3932164
  49.3 72.1 %collective-permute-start.3 = (bf16[4,32,5120]{2,1,0:T(8,128)(2,1)S(1)}, bf16[4,32,5120]{2,1,0:T(8,128)(2,1)S(1)}, u32[]{:S(2)}, u32[]{:S(2)}) collective-permute-start(bf16[4,32,5120]{2,1,0:T(8,128)(2,1)S(1)} %pad_maximum_fusion.refs_0_.refs_1_), channel_id=1, source_target_pairs={{0,2},{1,3},{2,0},{3,1},{4,6},{5,7},{6,4},{7,5},{8,10},{9,11},{10,... | collective-permute-start | bytes 3932168 | tf_op jit(solution)/shard_map/ppermute | solution.py:986
  50.9 70.6 %collective-permute-start.4 = (bf16[4,32,5120]{2,1,0:T(8,128)(2,1)S(1)}, bf16[4,32,5120]{2,1,0:T(8,128)(2,1)}, u32[]{:S(2)}, u32[]{:S(2)}) collective-permute-start(bf16[4,32,5120]{2,1,0:T(8,128)(2,1)S(1)} %pad_maximum_fusion.refs_0_.refs_1_), channel_id=1, source_target_pairs={{0,4},{1,5},{2,6},{3,7},{4,0},{5,1},{6,2},{7,3},{8,12},{9,13},{10,... | collective-permute-start | bytes 3932168 | tf_op jit(solution)/shard_map/ppermute | solution.py:986
  52.4 73.7 %collective-permute-start.5 = (bf16[4,32,5120]{2,1,0:T(8,128)(2,1)S(1)}, bf16[4,32,5120]{2,1,0:T(8,128)(2,1)}, u32[]{:S(2)}, u32[]{:S(2)}) collective-permute-start(bf16[4,32,5120]{2,1,0:T(8,128)(2,1)S(1)} %pad_maximum_fusion.refs_0_.refs_1_), channel_id=1, source_target_pairs={{0,6},{1,7},{2,4},{3,5},{4,2},{5,3},{6,0},{7,1},{8,14},{9,15},{10,... | collective-permute-start | bytes 3932168 | tf_op jit(solution)/shard_map/ppermute | solution.py:986
  121.4 4.7 copy-start.1
  132.6 25.0 %collective-permute-start.6 = (bf16[16,32,5120]{2,1,0:T(8,128)(2,1)}, bf16[16,32,5120]{2,1,0:T(8,128)(2,1)}, u32[]{:S(2)}, u32[]{:S(2)}) collective-permute-start(bf16[16,32,5120]{2,1,0:T(8,128)(2,1)} %near_rows.1.near_ref), channel_id=1, source_target_pairs={{0,1},{1,0},{2,3},{3,2},{4,5},{5,4},{6,7},{7,6},{8,9},{9,8},{10,11... | collective-permute-start | bytes 15728648 | tf_op jit(solution)/shard_map/ppermute | solution.py:986
  290.9 13.6 %collective-permute-start.7 = (bf16[512,8192]{1,0:T(8,128)(2,1)}, bf16[512,8192]{1,0:T(8,128)(2,1)}, u32[]{:S(2)}, u32[]{:S(2)}) collective-permute-start(bf16[512,8192]{1,0:T(8,128)(2,1)} %get-tuple-element.89), channel_id=1, source_target_pairs={{0,1},{1,0},{2,3},{3,2},{4,5},{5,4},{6,7},{7,6},{8,9},{9,8},{10,11... | collective-permute-start | bytes 25165832 | tf_op jit(solution)/shard_map/ppermute | solution.py:986
  313.7 99.7 %collective-permute-start.9 = (bf16[128,8192]{1,0:T(8,128)(2,1)}, bf16[128,8192]{1,0:T(8,128)(2,1)}, u32[]{:S(2)}, u32[]{:S(2)}) collective-permute-start(bf16[128,8192]{1,0:T(8,128)(2,1)} %get-tuple-element.90.refs_0_), channel_id=1, source_target_pairs={{0,2},{1,3},{2,0},{3,1},{4,6},{5,7},{6,4},{7,5},{8,10},{9,11},{10,... | collective-permute-start | bytes 6291464 | tf_op jit(solution)/shard_map/ppermute | solution.py:986
  315.0 99.9 %collective-permute-start.10 = (bf16[128,8192]{1,0:T(8,128)(2,1)}, bf16[128,8192]{1,0:T(8,128)(2,1)}, u32[]{:S(2)}, u32[]{:S(2)}) collective-permute-start(bf16[128,8192]{1,0:T(8,128)(2,1)} %get-tuple-element.91.refs_1_), channel_id=1, source_target_pairs={{0,4},{1,5},{2,6},{3,7},{4,0},{5,1},{6,2},{7,3},{8,12},{9,13},{10,... | collective-permute-start | bytes 6291464 | tf_op jit(solution)/shard_map/ppermute | solution.py:986
  315.8 99.1 %collective-permute-start.11 = (bf16[128,8192]{1,0:T(8,128)(2,1)}, bf16[128,8192]{1,0:T(8,128)(2,1)}, u32[]{:S(2)}, u32[]{:S(2)}) collective-permute-start(bf16[128,8192]{1,0:T(8,128)(2,1)} %get-tuple-element.92.refs_2_), channel_id=1, source_target_pairs={{0,6},{1,7},{2,4},{3,5},{4,2},{5,3},{6,0},{7,1},{8,14},{9,15},{10,... | collective-permute-start | bytes 6291464 | tf_op jit(solution)/shard_map/ppermute | solution.py:986
  356.2 13.2 %collective-permute-start.8 = (bf16[512,4096]{1,0:T(8,128)(2,1)}, bf16[512,4096]{1,0:T(8,128)(2,1)}, u32[]{:S(2)}, u32[]{:S(2)}) collective-permute-start(bf16[512,4096]{1,0:T(8,128)(2,1)} %get-tuple-element.98.refs_0_), channel_id=1, source_target_pairs={{0,1},{1,0},{2,3},{3,2},{4,5},{5,4},{6,7},{7,6},{8,9},{9,8},{10,11... | collective-permute-start | bytes 12582920 | tf_op jit(solution)/shard_map/ppermute | solution.py:986
  374.6 74.3 %collective-permute-start.13 = (bf16[128,4096]{1,0:T(8,128)(2,1)}, bf16[128,4096]{1,0:T(8,128)(2,1)}, u32[]{:S(2)}, u32[]{:S(2)}) collective-permute-start(bf16[128,4096]{1,0:T(8,128)(2,1)} %get-tuple-element.102.refs_0_), channel_id=1, source_target_pairs={{0,2},{1,3},{2,0},{3,1},{4,6},{5,7},{6,4},{7,5},{8,10},{9,11},{10,... | collective-permute-start | bytes 3145736 | tf_op jit(solution)/shard_map/ppermute | solution.py:986
  375.9 74.6 %collective-permute-start.14 = (bf16[128,4096]{1,0:T(8,128)(2,1)}, bf16[128,4096]{1,0:T(8,128)(2,1)}, u32[]{:S(2)}, u32[]{:S(2)}) collective-permute-start(bf16[128,4096]{1,0:T(8,128)(2,1)} %get-tuple-element.103.refs_1_), channel_id=1, source_target_pairs={{0,4},{1,5},{2,6},{3,7},{4,0},{5,1},{6,2},{7,3},{8,12},{9,13},{10,... | collective-permute-start | bytes 3145736 | tf_op jit(solution)/shard_map/ppermute | solution.py:986
  413.5 39.9 %collective-permute-start.15 = (bf16[128,4096]{1,0:T(8,128)(2,1)}, bf16[128,4096]{1,0:T(8,128)(2,1)}, u32[]{:S(2)}, u32[]{:S(2)}) collective-permute-start(bf16[128,4096]{1,0:T(8,128)(2,1)} %get-tuple-element.104.refs_2_), channel_id=1, source_target_pairs={{0,6},{1,7},{2,4},{3,5},{4,2},{5,3},{6,0},{7,1},{8,14},{9,15},{10,... | collective-permute-start | bytes 3145736 | tf_op jit(solution)/shard_map/ppermute | solution.py:986
  420.5 71.0 %reduce-scatter.6.cloned.1.call-start = ((), (), s32[]{:S(2)}) async-start(), calls=%async_computation.6 | async-start | bytes 1310720 | tf_op jit(solution)/shard_map/reduce_scatter | solution.py:1015
  434.0 7.6 %collective-permute-start.12 = (bf16[512,4096]{1,0:T(8,128)(2,1)}, bf16[512,4096]{1,0:T(8,128)(2,1)}, u32[]{:S(2)}, u32[]{:S(2)}) collective-permute-start(bf16[512,4096]{1,0:T(8,128)(2,1)} %get-tuple-element.114.refs_0_), channel_id=1, source_target_pairs={{0,1},{1,0},{2,3},{3,2},{4,5},{5,4},{6,7},{7,6},{8,9},{9,8},{10,11... | collective-permute-start | bytes 12582920 | tf_op jit(solution)/shard_map/ppermute | solution.py:986
  446.9 46.3 %collective-permute-start.21 = (bf16[128,4096]{1,0:T(8,128)(2,1)}, bf16[128,4096]{1,0:T(8,128)(2,1)}, u32[]{:S(2)}, u32[]{:S(2)}) collective-permute-start(bf16[128,4096]{1,0:T(8,128)(2,1)} %get-tuple-element.116.refs_0_), channel_id=1, source_target_pairs={{0,2},{1,3},{2,0},{3,1},{4,6},{5,7},{6,4},{7,5},{8,10},{9,11},{10,... | collective-permute-start | bytes 3145736 | tf_op jit(solution)/shard_map/ppermute | solution.py:986
  448.1 45.1 %collective-permute-start.22 = (bf16[128,4096]{1,0:T(8,128)(2,1)}, bf16[128,4096]{1,0:T(8,128)(2,1)}, u32[]{:S(2)}, u32[]{:S(2)}) collective-permute-start(bf16[128,4096]{1,0:T(8,128)(2,1)} %get-tuple-element.117.refs_1_), channel_id=1, source_target_pairs={{0,4},{1,5},{2,6},{3,7},{4,0},{5,1},{6,2},{7,3},{8,12},{9,13},{10,... | collective-permute-start | bytes 3145736 | tf_op jit(solution)/shard_map/ppermute | solution.py:986
  448.9 48.7 %collective-permute-start.23 = (bf16[128,4096]{1,0:T(8,128)(2,1)}, bf16[128,4096]{1,0:T(8,128)(2,1)}, u32[]{:S(2)}, u32[]{:S(2)}) collective-permute-start(bf16[128,4096]{1,0:T(8,128)(2,1)} %get-tuple-element.118.refs_2_), channel_id=1, source_target_pairs={{0,6},{1,7},{2,4},{3,5},{4,2},{5,3},{6,0},{7,1},{8,14},{9,15},{10,... | collective-permute-start | bytes 3145736 | tf_op jit(solution)/shard_map/ppermute | solution.py:986
  456.6 76.1 %reduce-scatter.8.cloned.1.call-start = ((), (), s32[]{:S(2)}) async-start(), calls=%async_computation.7 | async-start | bytes 1310720 | tf_op jit(solution)/shard_map/reduce_scatter | solution.py:1015
  502.6 1.5 collective-permute-start.16
  505.0 4.9 collective-permute-start.17
  509.9 4.7 collective-permute-start.18
  514.6 10.0 %collective-permute-start.19 = (f32[24,1024]{1,0:T(8,128)S(1)}, f32[24,1024]{1,0:T(8,128)S(1)}, u32[]{:S(2)}, u32[]{:S(2)}) collective-permute-start(f32[24,1024]{1,0:T(8,128)S(1)} %add.31), channel_id=1, source_target_pairs={{0,8},{8,0},{16,24},{24,16},{1,9},{9,1},{17,25},{25,17},{2,10},{10... | collective-permute-start | bytes 294920 | tf_op jit(solution)/shard_map/ppermute | solution.py:986
  524.6 6.3 %collective-permute-start.20 = (f32[24,1024]{1,0:T(8,128)S(1)}, f32[24,1024]{1,0:T(8,128)S(1)}, u32[]{:S(2)}, u32[]{:S(2)}) collective-permute-start(f32[24,1024]{1,0:T(8,128)S(1)} %add.32), channel_id=1, source_target_pairs={{0,16},{8,24},{16,0},{24,8},{1,17},{9,25},{17,1},{25,9},{2,18},{10... | collective-permute-start | bytes 294920 | tf_op jit(solution)/shard_map/ppermute | solution.py:986
Sparse Core Ops, SparseCore 0:
  11.4 95.6 all-gather.2
  110.5 114.5 all-gather.4
  420.6 42.0 reduce-scatter.3
  465.0 26.4 reduce-scatter.5
  501.0 29.2 reduce-scatter.7

commit v3 on v2

--- a/solution.py
+++ b/solution.py
@@ -767,28 +767,41 @@
     )(*waits, mine, *arrays)
 
 
-def near_kernel(*refs):
-    whole_ref = refs[-1]
-    rows = refs[0].shape[0]
-    for at, ref in enumerate(refs[:-1]):
-        whole_ref[at * rows : (at + 1) * rows] = ref[...]
-
-
-def near_rows(pieces, waits=()):
-    rows, own, columns = pieces[0].shape
-    lanes = 1024
-    block = pl.BlockSpec((rows, own, lanes), lambda j: (0, 0, j))
-    kernel, in_specs = after(waits, near_kernel, [block] * len(pieces))
+def near_kernel(steps, first_x_ref, first_x_got_ref, first_y_ref, first_y_got_ref, whole_ref):
+    step = pl.program_id(0)
+    rows = first_x_ref.shape[0] // 2
+
+    def put(place, ref, at):
+        whole_ref[place * rows : (place + 1) * rows] = ref[at * rows : (at + 1) * rows]
+
+    @pl.when(step < steps)
+    def _():
+        for place, ref, at in ((0, first_x_ref, 0), (1, first_x_ref, 1), (2, first_x_got_ref, 0), (3, first_x_got_ref, 1)):
+            put(place, ref, at)
+
+    @pl.when(step >= steps)
+    def _():
+        for place, ref, at in ((0, first_y_ref, 0), (2, first_y_ref, 1), (1, first_y_got_ref, 0), (3, first_y_got_ref, 1)):
+            put(place, ref, at)
+
+
+def near_rows(first_x, first_x_got, first_y, first_y_got, waits=()):
+    rows, own, columns = first_x.shape
+    lanes = 512
+    steps = columns // lanes
+    low = pl.BlockSpec((rows, own, lanes), lambda j: (0, 0, jnp.minimum(j, steps - 1)))
+    high = pl.BlockSpec((rows, own, lanes), lambda j: (0, 0, jnp.maximum(j - steps, 0)))
+    kernel, in_specs = after(waits, functools.partial(near_kernel, steps), [low, low, high, high])
     return pl.pallas_call(
         kernel,
-        grid=(columns // lanes,),
+        grid=(2 * steps,),
         in_specs=in_specs,
-        out_specs=pl.BlockSpec((len(pieces) * rows, own, lanes), lambda j: (0, 0, j)),
-        out_shape=out((len(pieces) * rows, own, columns), bf16),
-        compiler_params=params(),
-        cost_estimate=cost(0, 4 * len(pieces) * rows * own * columns),
+        out_specs=pl.BlockSpec((2 * rows, own, lanes), lambda j: (0, 0, j)),
+        out_shape=out((2 * rows, own, 2 * columns), bf16),
+        compiler_params=params(),
+        cost_estimate=cost(0, 8 * rows * own * columns),
         name="near_rows",
-    )(*waits, *pieces)
+    )(*waits, first_x, first_x_got, first_y, first_y_got)
 
 
 def place_kernel(dp_size, me_ref, near_ref, far_ref, whole_ref):
@@ -986,13 +999,16 @@
     return lax.ppermute(array, axis, [(i, i ^ distance) for i in range(size)])
 
 
+def sum_along(sums, axis, size):
+    distance = 1
+    while distance < size:
+        sums = sums + exchange(sums, axis, size, distance)
+        distance *= 2
+    return sums
+
+
 def small_sum(sums, own, dp_size, fsdp_size):
-    kept = sums
-    for axis, size in (("fsdp", fsdp_size), ("dp", dp_size)):
-        distance = 1
-        while distance < size:
-            kept = kept + exchange(kept, axis, size, distance)
-            distance *= 2
+    kept = sum_along(sums, "fsdp", fsdp_size)
     start = (lax.axis_index("dp") * fsdp_size + lax.axis_index("fsdp")) * own
     return lax.dynamic_slice_in_dim(kept, start, own, axis=1)
 
@@ -1038,7 +1054,7 @@
     devices = width // own
     steps = ffn_in.shape[1] // width
     dp_size, fsdp_size = lax.axis_size("dp"), lax.axis_size("fsdp")
-    by_distance = own % 16 == 0
+    by_distance = own % 16 == 0 and fsdp_size == 8
     mine = (lax.axis_index("dp") * fsdp_size + lax.axis_index("fsdp")).astype(jnp.int32).reshape(1)
     split = (mine, dp_size, own) if by_distance else (mine,)
 
@@ -1068,15 +1084,20 @@
         line = jnp.stack(
             [second_shard] + [exchange(second_shard, "dp", dp_size, k) for k in range(1, dp_size)]
         )
-        plane = [exchange(line, "fsdp", fsdp_size, 2 * k) for k in range(1, fsdp_size // 2)]
-        waits = (line,)
+        side = line.shape[2] // 2
+        first_x, first_y = line[:, :, :side], line[:, :, side:]
+        first_x = jnp.concatenate([first_x, exchange(first_x, "fsdp", fsdp_size, 2)])
+        first_y = jnp.concatenate([first_y, exchange(first_y, "fsdp", fsdp_size, 4)])
+        first_x_got = exchange(first_x, "fsdp", fsdp_size, 4)
+        first_y_got = exchange(first_y, "fsdp", fsdp_size, 2)
+        waits = (first_x, first_y)
     table = first[:, 3 * width :].astype(f32).T[:24]
 
     normed_one, triple = entry(x, first, table, waits)
     parts = [(triple, at * (width // PAIR), width) for at in range(3)]
     self_mixed, self_stats = attend(target_lengths, *parts, True)
     if by_distance:
-        near = near_rows([line] + plane, (triple,))
+        near = near_rows(first_x, first_x_got, first_y, first_y_got, (triple,))
         second = place(mine, near, exchange(near, "fsdp", fsdp_size, 1), dp_size)
     else:
         second = gather(second_shard)
@@ -1131,13 +1152,14 @@
         waits = (*self_sent, cross_total)
     input_grad, sums_one = entry_back(x, grad_one, self_grads, first, table, waits)
     sums = small_grads(sums_one, sums_two, sums_three, cross_sums, self_sums, hidden_bias_sums)
+    sums = sum_along(sums, "dp", dp_size)
     if by_distance:
         result = layer_result(hidden_two, made, table, (input_grad,))
         inner_own, outer_own = feed_own_grads([feed_own], width, (result,))
         cross_out_own, query_own, pair_own = cut_columns(
             cross_own, (0, width, 2 * width, 4 * width), (inner_own,)
         )
-        self_total = plane_total(self_plane, (cross_out_own,))
+        self_total = plane_total(self_plane, (cross_out_own, sums))
         self_own = scatter_line(self_total)
         self_out_own, triple_own = cut_columns(self_own, (0, width, 4 * width))
     else:

time: 550 us -> 544 us (0.989)
  waiting for transfers between devices: 152 us -> 139 us
    all_gather x2, waiting for transfers between devices: 66.1 us -> 47.9 us  [gather(): return lax.all_gather(shard, AXES, axis=0, tiled=True)]
    ppermute x24 -> x25, waiting for transfers between devices: 72.6 us -> 76.6 us  [exchange(): return lax.ppermute(array, axis, [(i, i ^ distance) for i in range(size)])]
    ppermute x24 -> x25, starting transfers between devices: 22.5 us -> 25 us  [exchange(): return lax.ppermute(array, axis, [(i, i ^ distance) for i in range(size)])]
  transfers between devices with their start and end apart: 29 -> 30, of which waited for: 16 -> 14; matrix products, arithmetic and copies ran while one was open for 1% -> 1% of each run, Pallas kernels for 49% -> 50%
where the time goes in v3:
time: 544 us; the launch traced here: 535 us
  Pallas kernels  349 us (64%)
  waiting for transfers between devices  139 us (26%)
  starting transfers between devices  25.2 us (5%)
  between operations  15.5 us (3%)
    ppermute x25, waiting for transfers between devices, exchange(): return lax.ppermute(array, axis, [(i, i ^ distance) for i in range(size)])  76.6 us
    pallas_call x1, Pallas kernels, feed(): pl.pallas_call(functools.partial(feed_kernel, split[1:] or None), grid=(s...  65.7 us
    pallas_call x2, Pallas kernels, attend_back(): pl.pallas_call(kernel, grid=(pairs,), in_specs=in_specs, out_specs=[pair_...  64.5 us
    all_gather x2, waiting for transfers between devices, gather(): return lax.all_gather(shard, AXES, axis=0, tiled=True)  47.9 us
    pallas_call x2, Pallas kernels, attend(): pl.pallas_call(functools.partial(attend_kernel, causal), grid=(pairs,), i...  45.1 us
    ppermute x25, starting transfers between devices, exchange(): return lax.ppermute(array, axis, [(i, i ^ distance) for i in range(size)])  25 us
    pallas_call x2, Pallas kernels, weight_grads(): pl.pallas_call(kernel, grid=(len(picks),), in_specs=in_specs, out_specs=[...  24.7 us
    pallas_call x3, Pallas kernels, plane_pieces(): pl.pallas_call(kernel, grid=(steps,), in_specs=in_specs, out_specs=[pl.Bl...  20.1 us
  transfers between devices with their start and end apart: 30, of which 14 were waited for; matrix products, arithmetic and copies ran while one was open for 1% of the time, Pallas kernels for 50%

profile of v3, /device:TPU:0, one launch (start us, length us, event | category | flops | bytes accessed | tf_op | source)
XLA Modules:
  0.0 534.9 jit_solution(4963956754110527460)
XLA Ops:
  7.2 2.5 shards_to_gather.1
  10.6 5.1 collective-permute-start.2
  16.3 8.4 %collective-permute-done.2 = bf16[32,5120]{1,0:T(8,128)(2,1)S(1)} collective-permute-done((bf16[32,5120]{1,0:T(8,128)(2,1)}, bf16[32,5120]{1,0:T(8,128)(2,1)S(1)}, u32[]{:S(2)}, u32[]{:S(2)}) %collective-permute-start.2) | collective-permute-done | bytes 327712 | tf_op jit(solution)/shard_map/ppermute | solution.py:999
  24.8 23.4 %collective-permute-done.1 = bf16[32,5120]{1,0:T(8,128)(2,1)S(1)} collective-permute-done((bf16[32,5120]{1,0:T(8,128)(2,1)}, bf16[32,5120]{1,0:T(8,128)(2,1)S(1)}, u32[]{:S(2)}, u32[]{:S(2)}) %collective-permute-start.1) | collective-permute-done | bytes 327712 | tf_op jit(solution)/shard_map/ppermute | solution.py:999
  49.4 1.6 collective-permute-start.3
  51.0 1.5 collective-permute-start.4
  52.5 16.2 %collective-permute-done.3 = bf16[4,32,2560]{2,1,0:T(8,128)(2,1)S(1)} collective-permute-done((bf16[4,32,2560]{2,1,0:T(8,128)(2,1)S(1)}, bf16[4,32,2560]{2,1,0:T(8,128)(2,1)S(1)}, u32[]{:S(2)}, u32[]{:S(2)}) %collective-permute-start.3) | collective-permute-done | bytes 655392 | tf_op jit(solution)/shard_map/ppermute | solution.py:999
  68.8 1.5 collective-permute-start.5
  71.1 35.4 %all-gather.3.cloned.1.call-done.refs_3_.refs_6_ = bf16[1024,3200]{1,0:T(8,128)(2,1)} async-done(((bf16[32,3200]{1,0:T(8,128)(2,1)}), bf16[1024,3200]{1,0:T(8,128)(2,1)}) %all-gather.3.cloned.1.call-update) | async-done | bytes 6553616 | tf_op jit(solution)/shard_map/all_gather | solution.py:991
  108.3 12.6 %norm_and_qkv.1 = (bf16[1024,1024]{1,0:T(8,128)(2,1)}, bf16[1024,3072]{1,0:T(8,128)(2,1)}) custom-call(bf16[8,32,2560]{2,1,0:T(8,128)(2,1)} %copy-done, bf16[8,32,2560]{2,1,0:T(8,128)(2,1)} %copy-done.1, bf16[1024,1024]{1,0:T(8,128)(2,1)} %bitcast.15, bf16[1024,3200]{1,0:T(8,128)(2,1)} %all-gather.3.cloned.1.call-done.refs_3_.refs_6_, ...), custom_call_target="tpu_custom_call" | custom-call | flops 6442450944 | bytes 16777216 | tf_op jit(solution)/shard_map/norm_and_qkv/pallas_call | solution.py:119
  120.9 8.4 %near_rows.1.near_ref = bf16[16,32,5120]{2,1,0:T(8,128)(2,1)} custom-call(bf16[1024,3072]{1,0:T(8,128)(2,1)} %get-tuple-element.76.query_ref.key_ref.value_ref.refs_0_.refs_4_.refs_5_.refs_6_, bf16[8,32,2560]{2,1,0:T(8,128)(2,1)} %copy-done, bf16[8,32,2560]{2,1,0:T(8,128)(2,1)} %collective-permute-done.5.refs_2_, bf16[8,32,2560]{2,1,0:T(8,128)(2,1)} %copy-done.1, ...), custom_call_target="tpu_custom_call" | custom-call | bytes 335544320 | tf_op jit(solution)/shard_map/near_rows/pallas_call | solution.py:795
  130.8 23.7 %attend_causal.1 = (bf16[1024,1024]{1,0:T(8,128)(2,1)}, f32[8,2,1024]{2,1,0:T(2,128)}) custom-call(s32[1]{0:T(128)S(6)} %copy.35.length_ref.refs_3_, bf16[1024,3072]{1,0:T(8,128)(2,1)} %get-tuple-element.76.query_ref.key_ref.value_ref.refs_0_.refs_4_.refs_5_.refs_6_, ...), custom_call_target="tpu_custom_call" | custom-call | flops 17179869184 | bytes 8388608 | tf_op jit(solution)/shard_map/attend_causal/pallas_call | solution.py:270
  154.5 9.8 %place_by_device.1.out_ref.query_ref.weight_ref.refs_4_.refs_5_.refs_3_ = bf16[1024,5120]{1,0:T(8,128)(2,1)} custom-call(s32[1]{0:T(128)} %bitcast.me_ref.refs_0_.refs_1_, bf16[16,32,5120]{2,1,0:T(8,128)(2,1)} %near_rows.1.near_ref, bf16[16,32,5120]{2,1,0:T(8,128)(2,1)} %collective-permute-done.7.far_ref), custom_call_target="tpu_custom_call" | custom-call | bytes 1342177280 | tf_op jit(solution)/shard_map/place_by_device/pallas_call | solution.py:824
  164.3 5.9 %memory_keys_values.1.key_ref.value_ref.refs_5_.refs_6_ = bf16[512,2048]{1,0:T(8,128)(2,1)} custom-call(bf16[512,1024]{1,0:T(8,128)(2,1)} %bitcast.19, bf16[1024,5120]{1,0:T(8,128)(2,1)} %place_by_device.1.out_ref.query_ref.weight_ref.refs_4_.refs_5_.refs_3_, f32[24,1024]{1,0:T(8,128)} %slice_convert_fusion.refs_4_.table_ref.refs_6_.refs_7_.refs_3_), custom_call_target="tpu_custom_call" | custom-call | flops 2147483648 | bytes 7340032 | tf_op jit(solution)/shard_map/memory_keys_values/pallas_call | solution.py:170
  170.2 11.5 %self_out_norm_query.1 = (f32[1024,1024]{1,0:T(8,128)}, bf16[1024,1024]{1,0:T(8,128)(2,1)}, bf16[1024,1024]{1,0:T(8,128)(2,1)}) custom-call(bf16[1024,1024]{1,0:T(8,128)(2,1)} %bitcast.16, bf16[1024,1024]{1,0:T(8,128)(2,1)} %get-tuple-element.77.mixed_ref.refs_7_.refs_2_, ...), custom_call_target="tpu_custom_call" | custom-call | flops 4294967296 | bytes 16777216 | tf_op jit(solution)/shard_map/self_out_norm_query/pallas_call | solution.py:143
  181.7 21.4 %attend_memory.1 = (bf16[1024,1024]{1,0:T(8,128)(2,1)}, f32[8,2,1024]{2,1,0:T(2,128)}) custom-call(s32[1]{0:T(128)S(6)} %copy.36.length_ref.refs_3_, bf16[1024,1024]{1,0:T(8,128)(2,1)} %get-tuple-element.78.query_ref.refs_4_, bf16[512,2048]{1,0:T(8,128)(2,1)} %memory_keys_values.1.key_ref.value_ref.refs_5_.refs_6_, ...), custom_call_target="tpu_custom_call" | custom-call | flops 8589934592 | bytes 6291456 | tf_op jit(solution)/shard_map/attend_memory/pallas_call | solution.py:270
  203.1 8.3 %cross_out_norm.1 = (f32[1024,1024]{1,0:T(8,128)}, bf16[1024,1024]{1,0:T(8,128)(2,1)}) custom-call(f32[1024,1024]{1,0:T(8,128)} %get-tuple-element.80.hidden_ref.refs_1_, bf16[1024,1024]{1,0:T(8,128)(2,1)} %get-tuple-element.79.mixed_ref.refs_7_.refs_1_, bf16[1024,5120]{1,0:T(8,128)(2,1)} %place_by_device.1.out_ref.query_ref.weight_ref.refs_4_.refs_5_.refs_3_, ...), custom_call_target="tpu_custom_call" | custom-call | flops 2147483648 | bytes 14680064 | tf_op jit(solution)/shard_map/cross_out_norm/pallas_call | solution.py:192
  211.4 12.5 %all-gather.5.cloned.1.call-done.weight_ref = bf16[1024,8192]{1,0:T(8,128)(2,1)} async-done(((bf16[32,8192]{1,0:T(8,128)(2,1)}), bf16[1024,8192]{1,0:T(8,128)(2,1)}) %all-gather.5.cloned.1.call-update) | async-done | bytes 16777232 | tf_op jit(solution)/shard_map/all_gather | solution.py:991
  223.9 65.7 %feed_forward_both_ways.1 = (f32[1024,1024]{1,0:T(8,128)}, f32[1024,1024]{1,0:T(8,128)}, f32[4,8,1024]{2,1,0:T(8,128)}, bf16[512,8192]{1,0:T(8,128)(2,1)}, bf16[512,8192]{1,0:T(8,128)(2,1)}) custom-call(s32[1]{0:T(128)} %bitcast.me_ref.refs_0_.refs_1_, bf16[1024,1024]{1,0:T(8,128)(2,1)} %get-tuple-element.82.normed_ref, bf16[1024,1024]{1,0:T(8,128)(2,1)} %bitcast.27, ...), custom_call_target="tpu_custom_call" | custom-call | flops 3298534883328 | bytes 2952790016 | tf_op jit(solution)/shard_map/feed_forward_both_ways/pallas_call | solution.py:444
  290.0 11.2 %norm_back_cross_out_back.1 = (f32[1024,1024]{1,0:T(8,128)}, bf16[1024,1024]{1,0:T(8,128)(2,1)}, bf16[1024,1024]{1,0:T(8,128)(2,1)}, f32[8,1024]{1,0:T(8,128)}) custom-call(f32[1024,1024]{1,0:T(8,128)} %get-tuple-element.81.hidden_ref.refs_1_, f32[1024,1024]{1,0:T(8,128)} %get-tuple-element.84.back_ref, bf16[1024,1024]{1,0:T(8,128)(2,1)} %bitcast.28, ...), custom_call_target="tpu_custom_call" | custom-call | flops 137438953472 | bytes 1342177280 | tf_op jit(solution)/shard_map/norm_back_cross_out_back/pallas_call | solution.py:502
  301.2 2.0 collective-permute-done.8.refs_2_
  303.2 9.4 %plane_pieces.3 = (bf16[128,8192]{1,0:T(8,128)(2,1)}, bf16[128,8192]{1,0:T(8,128)(2,1)}, bf16[128,8192]{1,0:T(8,128)(2,1)}, bf16[128,8192]{1,0:T(8,128)(2,1)}) custom-call(f32[8,1024]{1,0:T(8,128)} %get-tuple-element.87.refs_0_.three_ref, bf16[512,8192]{1,0:T(8,128)(2,1)} %get-tuple-element.88.refs_1_, bf16[512,8192]{1,0:T(8,128)(2,1)} %collective-permute-done.8.refs_2_), custom_call_target="tpu_custom_call" | custom-call | bytes 1610612736 | tf_op jit(solution)/shard_map/plane_pieces/pallas_call | solution.py:908
  314.7 1.5 collective-permute-start.12
  316.1 27.8 %attend_memory_back.1 = (bf16[1024,1024]{1,0:T(8,128)(2,1)}, bf16[512,1024]{1,0:T(8,128)(2,1)}, bf16[512,1024]{1,0:T(8,128)(2,1)}, f32[8,1024]{1,0:T(8,128)}) custom-call(bf16[128,8192]{1,0:T(8,128)(2,1)} %get-tuple-element.90.refs_0_, bf16[128,8192]{1,0:T(8,128)(2,1)} %get-tuple-element.91.refs_1_, bf16[128,8192]{1,0:T(8,128)(2,1)} %get-tuple-element.92.refs_2_, ...), custom_call_target="tpu_custom_call" | custom-call | flops 824633720832 | bytes 805306368 | tf_op jit(solution)/shard_map/attend_memory_back/pallas_call | solution.py:367
  343.9 11.2 %weight_grads_by_distance.2 = (bf16[512,4096]{1,0:T(8,128)(2,1)}, bf16[512,4096]{1,0:T(8,128)(2,1)}) custom-call(s32[1]{0:T(128)} %bitcast.me_ref.refs_0_.refs_1_, bf16[1024,1024]{1,0:T(8,128)(2,1)} %get-tuple-element.79.mixed_ref.refs_7_.refs_1_, bf16[1024,1024]{1,0:T(8,128)(2,1)} %get-tuple-element.85.refs_2_, ...), custom_call_target="tpu_custom_call" | custom-call | flops 412316860416 | bytes 1275068416 | tf_op jit(solution)/shard_map/weight_grads_by_distance/pallas_call | solution.py:756
  355.1 13.1 %query_norm_back_self_out_back.1 = (f32[1024,1024]{1,0:T(8,128)}, bf16[1024,1024]{1,0:T(8,128)(2,1)}, bf16[1024,1024]{1,0:T(8,128)(2,1)}, f32[8,1024]{1,0:T(8,128)}) custom-call(bf16[512,4096]{1,0:T(8,128)(2,1)} %get-tuple-element.98.refs_0_, f32[1024,1024]{1,0:T(8,128)} %get-tuple-element.80.hidden_ref.refs_1_, f32[1024,1024]{1,0:T(8,128)} %get-tuple-element.99.refs_2_, ...), custom_call_target="tpu_custom_call" | custom-call | flops 274877906944 | bytes 1610612736 | tf_op jit(solution)/shard_map/query_norm_back_self_out_back/pallas_call | solution.py:571
  368.2 5.4 %plane_pieces.4 = (bf16[128,4096]{1,0:T(8,128)(2,1)}, bf16[128,4096]{1,0:T(8,128)(2,1)}, bf16[128,4096]{1,0:T(8,128)(2,1)}, bf16[128,4096]{1,0:T(8,128)(2,1)}) custom-call(f32[1024,1024]{1,0:T(8,128)} %get-tuple-element.100.refs_0_.refs_5_, bf16[512,4096]{1,0:T(8,128)(2,1)} %get-tuple-element.101.refs_1_, bf16[512,4096]{1,0:T(8,128)(2,1)} %collective-permute-done.9.refs_2_), custom_call_target="tpu_custom_call" | custom-call | bytes 805306368 | tf_op jit(solution)/shard_map/plane_pieces/pallas_call | solution.py:908
  375.6 36.8 %attend_causal_back.1 = (bf16[1024,1024]{1,0:T(8,128)(2,1)}, bf16[1024,1024]{1,0:T(8,128)(2,1)}, bf16[1024,1024]{1,0:T(8,128)(2,1)}, f32[8,1024]{1,0:T(8,128)}) custom-call(bf16[128,4096]{1,0:T(8,128)(2,1)} %get-tuple-element.102.refs_0_, bf16[128,4096]{1,0:T(8,128)(2,1)} %get-tuple-element.103.refs_1_, bf16[128,4096]{1,0:T(8,128)(2,1)} %get-tuple-element.104.refs_2_, ...), custom_call_target="tpu_custom_call" | custom-call | flops 1649267441664 | bytes 1073741824 | tf_op jit(solution)/shard_map/attend_causal_back/pallas_call | solution.py:367
  412.3 1.5 collective-permute-start.16
  413.9 5.6 %plane_total.3.refs_0_ = bf16[128,8192]{1,0:T(8,128)(2,1)} custom-call(f32[8,1024]{1,0:T(8,128)} %get-tuple-element.107.refs_0_.self_ref, bf16[128,8192]{1,0:T(8,128)(2,1)} %get-tuple-element.108.refs_1_, bf16[128,8192]{1,0:T(8,128)(2,1)} %collective-permute-done.10.refs_2_, bf16[128,8192]{1,0:T(8,128)(2,1)} %collective-permute-done.11.refs_3_, ...), custom_call_target="tpu_custom_call" | custom-call | bytes 671088640 | tf_op jit(solution)/shard_map/plane_total/pallas_call | solution.py:934
  419.5 13.6 %weight_grads_by_distance.3 = (bf16[512,4096]{1,0:T(8,128)(2,1)}, bf16[512,4096]{1,0:T(8,128)(2,1)}) custom-call(bf16[128,8192]{1,0:T(8,128)(2,1)} %plane_total.3.refs_0_, s32[1]{0:T(128)} %bitcast.me_ref.refs_0_.refs_1_, bf16[1024,1024]{1,0:T(8,128)(2,1)} %get-tuple-element.77.mixed_ref.refs_7_.refs_2_, bf16[1024,1024]{1,0:T(8,128)(2,1)} %get-tuple-element.109.refs_3_, ...), custom_call_target="tpu_custom_call" | custom-call | flops 549755813888 | bytes 1342177280 | tf_op jit(solution)/shard_map/weight_grads_by_distance/pallas_call | solution.py:756
  433.2 6.1 %memory_back.1.refs_0_ = f32[512,1024]{1,0:T(8,128)} custom-call(bf16[512,4096]{1,0:T(8,128)(2,1)} %get-tuple-element.114.refs_0_, bf16[512,1024]{1,0:T(8,128)(2,1)} %get-tuple-element.96.refs_6_.refs_1_, bf16[512,1024]{1,0:T(8,128)(2,1)} %get-tuple-element.97.refs_7_.refs_2_, ...), custom_call_target="tpu_custom_call" | custom-call | flops 137438953472 | bytes 536870912 | tf_op jit(solution)/shard_map/memory_back/pallas_call | solution.py:633
  440.6 5.4 %plane_pieces.5 = (bf16[128,4096]{1,0:T(8,128)(2,1)}, bf16[128,4096]{1,0:T(8,128)(2,1)}, bf16[128,4096]{1,0:T(8,128)(2,1)}, bf16[128,4096]{1,0:T(8,128)(2,1)}) custom-call(f32[512,1024]{1,0:T(8,128)} %memory_back.1.refs_0_, bf16[512,4096]{1,0:T(8,128)(2,1)} %get-tuple-element.115.refs_1_, bf16[512,4096]{1,0:T(8,128)(2,1)} %collective-permute-done.13.refs_2_), custom_call_target="tpu_custom_call" | custom-call | bytes 805306368 | tf_op jit(solution)/shard_map/plane_pieces/pallas_call | solution.py:908
  448.1 1.5 collective-permute-start.24
  449.5 2.7 collective-permute-done.16.refs_4_
  452.2 3.3 plane_total.4.refs_3_
  455.6 14.6 %qkv_norm_back.1 = (f32[1024,1024]{1,0:T(8,128)}, f32[8,1024]{1,0:T(8,128)}) custom-call(bf16[128,4096]{1,0:T(8,128)(2,1)} %get-tuple-element.116.refs_0_, bf16[128,4096]{1,0:T(8,128)(2,1)} %get-tuple-element.117.refs_1_, bf16[128,4096]{1,0:T(8,128)(2,1)} %get-tuple-element.118.refs_2_, bf16[128,4096]{1,0:T(8,128)(2,1)} %plane_total.4.refs_3_, ...), custom_call_target="tpu_custom_call" | custom-call | flops 412316860416 | bytes 1476395008 | tf_op jit(solution)/shard_map/qkv_norm_back/pallas_call | solution.py:609
  470.2 1.7 small_grads.1
  472.2 9.4 %collective-permute-done.17 = f32[24,1024]{1,0:T(8,128)S(1)} collective-permute-done((f32[24,1024]{1,0:T(8,128)}, f32[24,1024]{1,0:T(8,128)S(1)}, u32[]{:S(2)}, u32[]{:S(2)}) %collective-permute-start.17) | collective-permute-done | bytes 98336 | tf_op jit(solution)/shard_map/ppermute | solution.py:999
  482.6 5.2 layer_result.1.refs_0_
  487.8 2.3 feed_own_grads.1
  490.1 4.4 collective-permute-done.18
  495.1 1.7 own_columns.2
  496.9 3.3 plane_total.5
  502.8 3.8 collective-permute-done.20
  507.7 3.6 collective-permute-done.21
  513.1 13.2 %reduce-scatter.8.cloned.1.call-done.refs_0_ = bf16[32,4096]{1,0:T(8,128)(2,1)} async-done(((bf16[128,4096]{1,0:T(8,128)(2,1)}), bf16[32,4096]{1,0:T(8,128)(2,1)}) %reduce-scatter.8.cloned.1.call-update) | async-done | bytes 262160 | tf_op jit(solution)/shard_map/reduce_scatter | solution.py:1031
  526.3 1.7 own_columns.3
  (68 shorter events, 21.2 us)
Async XLA Ops:
  7.2 99.3 %all-gather.3.cloned.1.call-start = ((), (), s32[]{:S(2)}) async-start(), calls=%async_computation.3 | async-start | bytes 6758400 | tf_op jit(solution)/shard_map/all_gather | solution.py:991
  9.8 214.1 %all-gather.5.cloned.1.call-start = ((), (), s32[]{:S(2)}) async-start(), calls=%async_computation.4 | async-start | bytes 17301504 | tf_op jit(solution)/shard_map/all_gather | solution.py:991
  10.5 477.3 %reduce-scatter.4.cloned.1.call-start = ((), (), s32[]{:S(2)}) async-start(), calls=%async_computation.5 | async-start | bytes 2621440 | tf_op jit(solution)/shard_map/reduce_scatter | solution.py:1031
  10.6 14.2 %collective-permute-start.2 = (bf16[32,5120]{1,0:T(8,128)(2,1)}, bf16[32,5120]{1,0:T(8,128)(2,1)S(1)}, u32[]{:S(2)}, u32[]{:S(2)}) collective-permute-start(bf16[32,5120]{1,0:T(8,128)(2,1)} %get-tuple-element.74), channel_id=1, source_target_pairs={{0,24},{8,16},{16,8},{24,0},{1,25},{9,17},{17,9},{25,1},{2,26},{10... | collective-permute-start | bytes 983048 | tf_op jit(solution)/shard_map/ppermute | solution.py:999
  15.7 32.5 %collective-permute-start.1 = (bf16[32,5120]{1,0:T(8,128)(2,1)}, bf16[32,5120]{1,0:T(8,128)(2,1)S(1)}, u32[]{:S(2)}, u32[]{:S(2)}) collective-permute-start(bf16[32,5120]{1,0:T(8,128)(2,1)} %get-tuple-element.74), channel_id=1, source_target_pairs={{0,16},{8,24},{16,0},{24,8},{1,17},{9,25},{17,1},{25,9},{2,18},{10... | collective-permute-start | bytes 983048 | tf_op jit(solution)/shard_map/ppermute | solution.py:999
  15.7 32.5 %collective-permute-start = (bf16[32,5120]{1,0:T(8,128)(2,1)}, bf16[32,5120]{1,0:T(8,128)(2,1)S(1)}, u32[]{:S(2)}, u32[]{:S(2)}) collective-permute-start(bf16[32,5120]{1,0:T(8,128)(2,1)} %get-tuple-element.74), channel_id=1, source_target_pairs={{0,8},{8,0},{16,24},{24,16},{1,9},{9,1},{17,25},{25,17},{2,10},{10... | collective-permute-start | bytes 983048 | tf_op jit(solution)/shard_map/ppermute | solution.py:999
  49.4 19.3 %collective-permute-start.3 = (bf16[4,32,2560]{2,1,0:T(8,128)(2,1)S(1)}, bf16[4,32,2560]{2,1,0:T(8,128)(2,1)S(1)}, u32[]{:S(2)}, u32[]{:S(2)}) collective-permute-start(bf16[4,32,2560]{2,1,0:T(8,128)(2,1)S(1)} %get-tuple-element.135), channel_id=1, source_target_pairs={{0,2},{1,3},{2,0},{3,1},{4,6},{5,7},{6,4},{7,5},{8,10},{9,11},{10,... | collective-permute-start | bytes 1966088 | tf_op jit(solution)/shard_map/ppermute | solution.py:999
  51.0 19.4 %collective-permute-start.4 = (bf16[4,32,2560]{2,1,0:T(8,128)(2,1)S(1)}, bf16[4,32,2560]{2,1,0:T(8,128)(2,1)S(1)}, u32[]{:S(2)}, u32[]{:S(2)}) collective-permute-start(bf16[4,32,2560]{2,1,0:T(8,128)(2,1)S(1)} %get-tuple-element.134), channel_id=1, source_target_pairs={{0,4},{1,5},{2,6},{3,7},{4,0},{5,1},{6,2},{7,3},{8,12},{9,13},{10,... | collective-permute-start | bytes 1966088 | tf_op jit(solution)/shard_map/ppermute | solution.py:999
  68.8 39.5 %copy-start = (bf16[8,32,2560]{2,1,0:T(8,128)(2,1)}, bf16[8,32,2560]{2,1,0:T(8,128)(2,1)S(1)}, u32[]{:S(2)}) copy-start(bf16[8,32,2560]{2,1,0:T(8,128)(2,1)S(1)} %pad_maximum_fusion.1.refs_0_.refs_1_) | copy-start | bytes 3932164
  68.8 52.1 %collective-permute-start.5 = (bf16[8,32,2560]{2,1,0:T(8,128)(2,1)S(1)}, bf16[8,32,2560]{2,1,0:T(8,128)(2,1)}, u32[]{:S(2)}, u32[]{:S(2)}) collective-permute-start(bf16[8,32,2560]{2,1,0:T(8,128)(2,1)S(1)} %pad_maximum_fusion.1.refs_0_.refs_1_), channel_id=1, source_target_pairs={{0,4},{1,5},{2,6},{3,7},{4,0},{5,1},{6,2},{7,3},{8,12},{9,13},{10,... | collective-permute-start | bytes 3932168 | tf_op jit(solution)/shard_map/ppermute | solution.py:999
  70.5 37.8 %copy-start.1 = (bf16[8,32,2560]{2,1,0:T(8,128)(2,1)}, bf16[8,32,2560]{2,1,0:T(8,128)(2,1)S(1)}, u32[]{:S(2)}) copy-start(bf16[8,32,2560]{2,1,0:T(8,128)(2,1)S(1)} %pad_maximum_fusion.2.refs_1_.refs_3_) | copy-start | bytes 3932164
  70.5 50.4 %collective-permute-start.6 = (bf16[8,32,2560]{2,1,0:T(8,128)(2,1)S(1)}, bf16[8,32,2560]{2,1,0:T(8,128)(2,1)}, u32[]{:S(2)}, u32[]{:S(2)}) collective-permute-start(bf16[8,32,2560]{2,1,0:T(8,128)(2,1)S(1)} %pad_maximum_fusion.2.refs_1_.refs_3_), channel_id=1, source_target_pairs={{0,2},{1,3},{2,0},{3,1},{4,6},{5,7},{6,4},{7,5},{8,10},{9,11},{10,... | collective-permute-start | bytes 3932168 | tf_op jit(solution)/shard_map/ppermute | solution.py:999
  129.3 25.2 %collective-permute-start.7 = (bf16[16,32,5120]{2,1,0:T(8,128)(2,1)}, bf16[16,32,5120]{2,1,0:T(8,128)(2,1)}, u32[]{:S(2)}, u32[]{:S(2)}) collective-permute-start(bf16[16,32,5120]{2,1,0:T(8,128)(2,1)} %near_rows.1.near_ref), channel_id=1, source_target_pairs={{0,1},{1,0},{2,3},{3,2},{4,5},{5,4},{6,7},{7,6},{8,9},{9,8},{10,11... | collective-permute-start | bytes 15728648 | tf_op jit(solution)/shard_map/ppermute | solution.py:999
  289.7 13.6 %collective-permute-start.8 = (bf16[512,8192]{1,0:T(8,128)(2,1)}, bf16[512,8192]{1,0:T(8,128)(2,1)}, u32[]{:S(2)}, u32[]{:S(2)}) collective-permute-start(bf16[512,8192]{1,0:T(8,128)(2,1)} %get-tuple-element.89), channel_id=1, source_target_pairs={{0,1},{1,0},{2,3},{3,2},{4,5},{5,4},{6,7},{7,6},{8,9},{9,8},{10,11... | collective-permute-start | bytes 25165832 | tf_op jit(solution)/shard_map/ppermute | solution.py:999
  312.6 99.7 %collective-permute-start.10 = (bf16[128,8192]{1,0:T(8,128)(2,1)}, bf16[128,8192]{1,0:T(8,128)(2,1)}, u32[]{:S(2)}, u32[]{:S(2)}) collective-permute-start(bf16[128,8192]{1,0:T(8,128)(2,1)} %get-tuple-element.90.refs_0_), channel_id=1, source_target_pairs={{0,2},{1,3},{2,0},{3,1},{4,6},{5,7},{6,4},{7,5},{8,10},{9,11},{10,... | collective-permute-start | bytes 6291464 | tf_op jit(solution)/shard_map/ppermute | solution.py:999
  313.9 100.0 %collective-permute-start.11 = (bf16[128,8192]{1,0:T(8,128)(2,1)}, bf16[128,8192]{1,0:T(8,128)(2,1)}, u32[]{:S(2)}, u32[]{:S(2)}) collective-permute-start(bf16[128,8192]{1,0:T(8,128)(2,1)} %get-tuple-element.91.refs_1_), channel_id=1, source_target_pairs={{0,4},{1,5},{2,6},{3,7},{4,0},{5,1},{6,2},{7,3},{8,12},{9,13},{10,... | collective-permute-start | bytes 6291464 | tf_op jit(solution)/shard_map/ppermute | solution.py:999
  314.7 99.2 %collective-permute-start.12 = (bf16[128,8192]{1,0:T(8,128)(2,1)}, bf16[128,8192]{1,0:T(8,128)(2,1)}, u32[]{:S(2)}, u32[]{:S(2)}) collective-permute-start(bf16[128,8192]{1,0:T(8,128)(2,1)} %get-tuple-element.92.refs_2_), channel_id=1, source_target_pairs={{0,6},{1,7},{2,4},{3,5},{4,2},{5,3},{6,0},{7,1},{8,14},{9,15},{10,... | collective-permute-start | bytes 6291464 | tf_op jit(solution)/shard_map/ppermute | solution.py:999
  355.1 13.1 %collective-permute-start.9 = (bf16[512,4096]{1,0:T(8,128)(2,1)}, bf16[512,4096]{1,0:T(8,128)(2,1)}, u32[]{:S(2)}, u32[]{:S(2)}) collective-permute-start(bf16[512,4096]{1,0:T(8,128)(2,1)} %get-tuple-element.98.refs_0_), channel_id=1, source_target_pairs={{0,1},{1,0},{2,3},{3,2},{4,5},{5,4},{6,7},{7,6},{8,9},{9,8},{10,11... | collective-permute-start | bytes 12582920 | tf_op jit(solution)/shard_map/ppermute | solution.py:999
  373.6 74.5 %collective-permute-start.14 = (bf16[128,4096]{1,0:T(8,128)(2,1)}, bf16[128,4096]{1,0:T(8,128)(2,1)}, u32[]{:S(2)}, u32[]{:S(2)}) collective-permute-start(bf16[128,4096]{1,0:T(8,128)(2,1)} %get-tuple-element.102.refs_0_), channel_id=1, source_target_pairs={{0,2},{1,3},{2,0},{3,1},{4,6},{5,7},{6,4},{7,5},{8,10},{9,11},{10,... | collective-permute-start | bytes 3145736 | tf_op jit(solution)/shard_map/ppermute | solution.py:999
  374.8 74.7 %collective-permute-start.15 = (bf16[128,4096]{1,0:T(8,128)(2,1)}, bf16[128,4096]{1,0:T(8,128)(2,1)}, u32[]{:S(2)}, u32[]{:S(2)}) collective-permute-start(bf16[128,4096]{1,0:T(8,128)(2,1)} %get-tuple-element.103.refs_1_), channel_id=1, source_target_pairs={{0,4},{1,5},{2,6},{3,7},{4,0},{5,1},{6,2},{7,3},{8,12},{9,13},{10,... | collective-permute-start | bytes 3145736 | tf_op jit(solution)/shard_map/ppermute | solution.py:999
  412.3 39.9 %collective-permute-start.16 = (bf16[128,4096]{1,0:T(8,128)(2,1)}, bf16[128,4096]{1,0:T(8,128)(2,1)}, u32[]{:S(2)}, u32[]{:S(2)}) collective-permute-start(bf16[128,4096]{1,0:T(8,128)(2,1)} %get-tuple-element.104.refs_2_), channel_id=1, source_target_pairs={{0,6},{1,7},{2,4},{3,5},{4,2},{5,3},{6,0},{7,1},{8,14},{9,15},{10,... | collective-permute-start | bytes 3145736 | tf_op jit(solution)/shard_map/ppermute | solution.py:999
  419.5 75.7 %reduce-scatter.6.cloned.1.call-start = ((), (), s32[]{:S(2)}) async-start(), calls=%async_computation.6 | async-start | bytes 1310720 | tf_op jit(solution)/shard_map/reduce_scatter | solution.py:1031
  433.1 7.6 %collective-permute-start.13 = (bf16[512,4096]{1,0:T(8,128)(2,1)}, bf16[512,4096]{1,0:T(8,128)(2,1)}, u32[]{:S(2)}, u32[]{:S(2)}) collective-permute-start(bf16[512,4096]{1,0:T(8,128)(2,1)} %get-tuple-element.114.refs_0_), channel_id=1, source_target_pairs={{0,1},{1,0},{2,3},{3,2},{4,5},{5,4},{6,7},{7,6},{8,9},{9,8},{10,11... | collective-permute-start | bytes 12582920 | tf_op jit(solution)/shard_map/ppermute | solution.py:999
  446.0 50.9 %collective-permute-start.22 = (bf16[128,4096]{1,0:T(8,128)(2,1)}, bf16[128,4096]{1,0:T(8,128)(2,1)}, u32[]{:S(2)}, u32[]{:S(2)}) collective-permute-start(bf16[128,4096]{1,0:T(8,128)(2,1)} %get-tuple-element.116.refs_0_), channel_id=1, source_target_pairs={{0,2},{1,3},{2,0},{3,1},{4,6},{5,7},{6,4},{7,5},{8,10},{9,11},{10,... | collective-permute-start | bytes 3145736 | tf_op jit(solution)/shard_map/ppermute | solution.py:999
  447.3 49.6 %collective-permute-start.23 = (bf16[128,4096]{1,0:T(8,128)(2,1)}, bf16[128,4096]{1,0:T(8,128)(2,1)}, u32[]{:S(2)}, u32[]{:S(2)}) collective-permute-start(bf16[128,4096]{1,0:T(8,128)(2,1)} %get-tuple-element.117.refs_1_), channel_id=1, source_target_pairs={{0,4},{1,5},{2,6},{3,7},{4,0},{5,1},{6,2},{7,3},{8,12},{9,13},{10,... | collective-permute-start | bytes 3145736 | tf_op jit(solution)/shard_map/ppermute | solution.py:999
  448.1 48.8 %collective-permute-start.24 = (bf16[128,4096]{1,0:T(8,128)(2,1)}, bf16[128,4096]{1,0:T(8,128)(2,1)}, u32[]{:S(2)}, u32[]{:S(2)}) collective-permute-start(bf16[128,4096]{1,0:T(8,128)(2,1)} %get-tuple-element.118.refs_2_), channel_id=1, source_target_pairs={{0,6},{1,7},{2,4},{3,5},{4,2},{5,3},{6,0},{7,1},{8,14},{9,15},{10,... | collective-permute-start | bytes 3145736 | tf_op jit(solution)/shard_map/ppermute | solution.py:999
  455.5 70.8 %reduce-scatter.8.cloned.1.call-start = ((), (), s32[]{:S(2)}) async-start(), calls=%async_computation.7 | async-start | bytes 1310720 | tf_op jit(solution)/shard_map/reduce_scatter | solution.py:1031
  471.8 9.8 %collective-permute-start.17 = (f32[24,1024]{1,0:T(8,128)}, f32[24,1024]{1,0:T(8,128)S(1)}, u32[]{:S(2)}, u32[]{:S(2)}) collective-permute-start(f32[24,1024]{1,0:T(8,128)} %small_grads.1), channel_id=1, source_target_pairs={{0,8},{8,0},{16,24},{24,16},{1,9},{9,1},{17,25},{25,17},{2,10},{10... | collective-permute-start | bytes 294920 | tf_op jit(solution)/shard_map/ppermute | solution.py:999
  482.5 12.0 %collective-permute-start.18 = (f32[24,1024]{1,0:T(8,128)S(1)}, f32[24,1024]{1,0:T(8,128)S(1)}, u32[]{:S(2)}, u32[]{:S(2)}) collective-permute-start(f32[24,1024]{1,0:T(8,128)S(1)} %add.29), channel_id=1, source_target_pairs={{0,16},{8,24},{16,0},{24,8},{1,17},{9,25},{17,1},{25,9},{2,18},{10... | collective-permute-start | bytes 294920 | tf_op jit(solution)/shard_map/ppermute | solution.py:999
  496.9 3.3 copy-start.2
  500.3 1.4 collective-permute-start.19
  501.6 4.9 collective-permute-start.20
  506.6 4.7 collective-permute-start.21
Sparse Core Ops, SparseCore 0:
  11.4 95.0 all-gather.2
  109.9 113.9 all-gather.4
  419.6 42.0 reduce-scatter.3
  463.9 30.6 reduce-scatter.5
  500.4 25.9 reduce-scatter.7

commit v4 on v3

--- a/solution.py
+++ b/solution.py
@@ -767,6 +767,33 @@
     )(*waits, mine, *arrays)
 
 
+def two_rows_kernel(line_x_ref, line_y_ref, got_x_ref, got_y_ref, first_x_ref, first_y_ref):
+    rows = line_x_ref.shape[0]
+    first_x_ref[:rows] = line_x_ref[...]
+    first_x_ref[rows:] = got_x_ref[...]
+    first_y_ref[:rows] = line_y_ref[...]
+    first_y_ref[rows:] = got_y_ref[...]
+
+
+def two_rows(line, got_x, got_y, waits=()):
+    rows, own, columns = got_x.shape
+    lanes = 1280
+    steps = columns // lanes
+    low = pl.BlockSpec((rows, own, lanes), lambda j: (0, 0, j))
+    high = pl.BlockSpec((rows, own, lanes), lambda j: (0, 0, j + steps))
+    kernel, in_specs = after(waits, two_rows_kernel, [low, high, low, low])
+    return pl.pallas_call(
+        kernel,
+        grid=(steps,),
+        in_specs=in_specs,
+        out_specs=[pl.BlockSpec((2 * rows, own, lanes), lambda j: (0, 0, j))] * 2,
+        out_shape=[out((2 * rows, own, columns), bf16)] * 2,
+        compiler_params=params(),
+        cost_estimate=cost(0, 8 * rows * own * columns),
+        name="two_rows",
+    )(*waits, line, line, got_x, got_y)
+
+
 def near_kernel(steps, first_x_ref, first_x_got_ref, first_y_ref, first_y_got_ref, whole_ref):
     step = pl.program_id(0)
     rows = first_x_ref.shape[0] // 2
@@ -787,7 +814,7 @@
 
 def near_rows(first_x, first_x_got, first_y, first_y_got, waits=()):
     rows, own, columns = first_x.shape
-    lanes = 512
+    lanes = 1280
     steps = columns // lanes
     low = pl.BlockSpec((rows, own, lanes), lambda j: (0, 0, jnp.minimum(j, steps - 1)))
     high = pl.BlockSpec((rows, own, lanes), lambda j: (0, 0, jnp.maximum(j - steps, 0)))
@@ -1085,9 +1112,9 @@
             [second_shard] + [exchange(second_shard, "dp", dp_size, k) for k in range(1, dp_size)]
         )
         side = line.shape[2] // 2
-        first_x, first_y = line[:, :, :side], line[:, :, side:]
-        first_x = jnp.concatenate([first_x, exchange(first_x, "fsdp", fsdp_size, 2)])
-        first_y = jnp.concatenate([first_y, exchange(first_y, "fsdp", fsdp_size, 4)])
+        got_x = exchange(line[:, :, :side], "fsdp", fsdp_size, 2)
+        got_y = exchange(line[:, :, side:], "fsdp", fsdp_size, 4)
+        first_x, first_y = two_rows(line, got_x, got_y, (first,))
         first_x_got = exchange(first_x, "fsdp", fsdp_size, 4)
         first_y_got = exchange(first_y, "fsdp", fsdp_size, 2)
         waits = (first_x, first_y)
@@ -1097,7 +1124,7 @@
     parts = [(triple, at * (width // PAIR), width) for at in range(3)]
     self_mixed, self_stats = attend(target_lengths, *parts, True)
     if by_distance:
-        near = near_rows(first_x, first_x_got, first_y, first_y_got, (triple,))
+        near = near_rows(first_x, first_x_got, first_y, first_y_got, (self_mixed,))
         second = place(mine, near, exchange(near, "fsdp", fsdp_size, 1), dp_size)
     else:
         second = gather(second_shard)

time: 544 us -> 540 us (level)
  waiting for transfers between devices: 139 us -> 131 us
  transfers between devices with their start and end apart: 30 -> 30, of which waited for: 14 -> 16; matrix products, arithmetic and copies ran while one was open for 1% -> 2% of each run, Pallas kernels for 50% -> 50%
where the time goes in v4:
time: 540 us; the launch traced here: 531 us
  Pallas kernels  348 us (64%)
  waiting for transfers between devices  131 us (24%)
  starting transfers between devices  24.9 us (5%)
  between operations  15.5 us (3%)
  local copies, waits for them, and re-layouts  7.4 us (1%)
    ppermute x25, waiting for transfers between devices, exchange(): return lax.ppermute(array, axis, [(i, i ^ distance) for i in range(size)])  71.8 us
    pallas_call x1, Pallas kernels, feed(): pl.pallas_call(functools.partial(feed_kernel, split[1:] or None), grid=(s...  65.7 us
    pallas_call x2, Pallas kernels, attend_back(): pl.pallas_call(kernel, grid=(pairs,), in_specs=in_specs, out_specs=[pair_...  64.5 us
    pallas_call x2, Pallas kernels, attend(): pl.pallas_call(functools.partial(attend_kernel, causal), grid=(pairs,), i...  45.1 us
    all_gather x2, waiting for transfers between devices, gather(): return lax.all_gather(shard, AXES, axis=0, tiled=True)  44.9 us
    pallas_call x2, Pallas kernels, weight_grads(): pl.pallas_call(kernel, grid=(len(picks),), in_specs=in_specs, out_specs=[...  24.7 us
    ppermute x25, starting transfers between devices, exchange(): return lax.ppermute(array, axis, [(i, i ^ distance) for i in range(size)])  24.6 us
    pallas_call x3, Pallas kernels, plane_pieces(): pl.pallas_call(kernel, grid=(steps,), in_specs=in_specs, out_specs=[pl.Bl...  20.2 us
  transfers between devices with their start and end apart: 30, of which 16 were waited for; matrix products, arithmetic and copies ran while one was open for 2% of the time, Pallas kernels for 50%

profile of v4, /device:TPU:0, one launch (start us, length us, event | category | flops | bytes accessed | tf_op | source)
XLA Modules:
  0.0 530.9 jit_solution(5401859232203637636)
XLA Ops:
  7.2 2.5 shards_to_gather.1
  10.6 5.1 collective-permute-start.2
  16.3 8.4 %collective-permute-done.2 = bf16[32,5120]{1,0:T(8,128)(2,1)S(1)} collective-permute-done((bf16[32,5120]{1,0:T(8,128)(2,1)}, bf16[32,5120]{1,0:T(8,128)(2,1)S(1)}, u32[]{:S(2)}, u32[]{:S(2)}) %collective-permute-start.2) | collective-permute-done | bytes 327712 | tf_op jit(solution)/shard_map/ppermute | solution.py:1026
  24.8 23.4 %collective-permute-done.1 = bf16[32,5120]{1,0:T(8,128)(2,1)S(1)} collective-permute-done((bf16[32,5120]{1,0:T(8,128)(2,1)}, bf16[32,5120]{1,0:T(8,128)(2,1)S(1)}, u32[]{:S(2)}, u32[]{:S(2)}) %collective-permute-start.1) | collective-permute-done | bytes 327712 | tf_op jit(solution)/shard_map/ppermute | solution.py:1026
  50.4 1.5 collective-permute-start.3
  51.9 1.5 collective-permute-start.4
  54.1 39.9 %all-gather.3.cloned.1.call-done.refs_0_.refs_3_.refs_6_ = bf16[1024,3200]{1,0:T(8,128)(2,1)} async-done(((bf16[32,3200]{1,0:T(8,128)(2,1)}), bf16[1024,3200]{1,0:T(8,128)(2,1)}) %all-gather.3.cloned.1.call-update) | async-done | bytes 6553616 | tf_op jit(solution)/shard_map/all_gather | solution.py:1018
  97.5 2.9 two_rows.1
  100.4 1.5 collective-permute-start.5
  103.9 12.8 %norm_and_qkv.1 = (bf16[1024,1024]{1,0:T(8,128)(2,1)}, bf16[1024,3072]{1,0:T(8,128)(2,1)}) custom-call(bf16[8,32,2560]{2,1,0:T(8,128)(2,1)} %get-tuple-element.78.refs_0_.refs_1_, bf16[8,32,2560]{2,1,0:T(8,128)(2,1)} %get-tuple-element.79.refs_1_.refs_3_, bf16[1024,1024]{1,0:T(8,128)(2,1)} %bitcast.15, ...), custom_call_target="tpu_custom_call" | custom-call | flops 6442450944 | bytes 16777216 | tf_op jit(solution)/shard_map/norm_and_qkv/pallas_call | solution.py:119
  116.7 23.7 %attend_causal.1 = (bf16[1024,1024]{1,0:T(8,128)(2,1)}, f32[8,2,1024]{2,1,0:T(2,128)}) custom-call(s32[1]{0:T(128)S(6)} %copy.36.length_ref.refs_3_, bf16[1024,3072]{1,0:T(8,128)(2,1)} %get-tuple-element.80.query_ref.key_ref.value_ref.refs_4_.refs_5_.refs_6_, bf16[1024,3072]{1,0:T(8,128)(2,1)} %get-tuple-element.80.query_ref.key_ref.value_ref.refs_4_.refs_5_.refs_6_, ...), custom_call_target="tpu_custom_call" | custom-call | flops 17179869184 | bytes 8388608 | tf_op jit(solution)/shard_map/attend_causal/pallas_call | solution.py:270
  141.2 2.4 collective-permute-done.6.refs_4_
  144.6 5.9 %near_rows.1.near_ref = bf16[16,32,5120]{2,1,0:T(8,128)(2,1)} custom-call(bf16[1024,1024]{1,0:T(8,128)(2,1)} %get-tuple-element.81.refs_0_.mixed_ref.refs_7_.refs_2_, bf16[8,32,2560]{2,1,0:T(8,128)(2,1)} %get-tuple-element.78.refs_0_.refs_1_, bf16[8,32,2560]{2,1,0:T(8,128)(2,1)} %copy-done.1, bf16[8,32,2560]{2,1,0:T(8,128)(2,1)} %get-tuple-element.79.refs_1_.refs_3_, ...), custom_call_target="tpu_custom_call" | custom-call | bytes 335544320 | tf_op jit(solution)/shard_map/near_rows/pallas_call | solution.py:822
  151.2 8.3 %collective-permute-done.7.far_ref = bf16[16,32,5120]{2,1,0:T(8,128)(2,1)} collective-permute-done((bf16[16,32,5120]{2,1,0:T(8,128)(2,1)}, bf16[16,32,5120]{2,1,0:T(8,128)(2,1)}, u32[]{:S(2)}, u32[]{:S(2)}) %collective-permute-start.7) | collective-permute-done | bytes 5242912 | tf_op jit(solution)/shard_map/ppermute | solution.py:1026
  159.5 9.9 %place_by_device.1.out_ref.query_ref.weight_ref.refs_4_.refs_5_.refs_3_ = bf16[1024,5120]{1,0:T(8,128)(2,1)} custom-call(s32[1]{0:T(128)} %bitcast.me_ref.refs_0_.refs_1_, bf16[16,32,5120]{2,1,0:T(8,128)(2,1)} %near_rows.1.near_ref, bf16[16,32,5120]{2,1,0:T(8,128)(2,1)} %collective-permute-done.7.far_ref), custom_call_target="tpu_custom_call" | custom-call | bytes 1342177280 | tf_op jit(solution)/shard_map/place_by_device/pallas_call | solution.py:851
  169.4 5.9 %memory_keys_values.1.key_ref.value_ref.refs_5_.refs_6_ = bf16[512,2048]{1,0:T(8,128)(2,1)} custom-call(bf16[512,1024]{1,0:T(8,128)(2,1)} %bitcast.19, bf16[1024,5120]{1,0:T(8,128)(2,1)} %place_by_device.1.out_ref.query_ref.weight_ref.refs_4_.refs_5_.refs_3_, f32[24,1024]{1,0:T(8,128)} %slice_convert_fusion.refs_4_.table_ref.refs_6_.refs_7_.refs_3_), custom_call_target="tpu_custom_call" | custom-call | flops 2147483648 | bytes 7340032 | tf_op jit(solution)/shard_map/memory_keys_values/pallas_call | solution.py:170
  175.3 10.0 %self_out_norm_query.1 = (f32[1024,1024]{1,0:T(8,128)}, bf16[1024,1024]{1,0:T(8,128)(2,1)}, bf16[1024,1024]{1,0:T(8,128)(2,1)}) custom-call(bf16[1024,1024]{1,0:T(8,128)(2,1)} %bitcast.16, bf16[1024,1024]{1,0:T(8,128)(2,1)} %get-tuple-element.81.refs_0_.mixed_ref.refs_7_.refs_2_, ...), custom_call_target="tpu_custom_call" | custom-call | flops 4294967296 | bytes 16777216 | tf_op jit(solution)/shard_map/self_out_norm_query/pallas_call | solution.py:143
  185.3 21.4 %attend_memory.1 = (bf16[1024,1024]{1,0:T(8,128)(2,1)}, f32[8,2,1024]{2,1,0:T(2,128)}) custom-call(s32[1]{0:T(128)S(6)} %copy.37.length_ref.refs_3_, bf16[1024,1024]{1,0:T(8,128)(2,1)} %get-tuple-element.82.query_ref.refs_4_, bf16[512,2048]{1,0:T(8,128)(2,1)} %memory_keys_values.1.key_ref.value_ref.refs_5_.refs_6_, ...), custom_call_target="tpu_custom_call" | custom-call | flops 8589934592 | bytes 6291456 | tf_op jit(solution)/shard_map/attend_memory/pallas_call | solution.py:270
  206.7 8.2 %cross_out_norm.1 = (f32[1024,1024]{1,0:T(8,128)}, bf16[1024,1024]{1,0:T(8,128)(2,1)}) custom-call(f32[1024,1024]{1,0:T(8,128)} %get-tuple-element.84.hidden_ref.refs_1_, bf16[1024,1024]{1,0:T(8,128)(2,1)} %get-tuple-element.83.mixed_ref.refs_7_.refs_1_, bf16[1024,5120]{1,0:T(8,128)(2,1)} %place_by_device.1.out_ref.query_ref.weight_ref.refs_4_.refs_5_.refs_3_, ...), custom_call_target="tpu_custom_call" | custom-call | flops 2147483648 | bytes 14680064 | tf_op jit(solution)/shard_map/cross_out_norm/pallas_call | solution.py:192
  214.9 5.0 all-gather.5.cloned.1.call-done.weight_ref
  219.9 65.7 %feed_forward_both_ways.1 = (f32[1024,1024]{1,0:T(8,128)}, f32[1024,1024]{1,0:T(8,128)}, f32[4,8,1024]{2,1,0:T(8,128)}, bf16[512,8192]{1,0:T(8,128)(2,1)}, bf16[512,8192]{1,0:T(8,128)(2,1)}) custom-call(s32[1]{0:T(128)} %bitcast.me_ref.refs_0_.refs_1_, bf16[1024,1024]{1,0:T(8,128)(2,1)} %get-tuple-element.86.normed_ref, bf16[1024,1024]{1,0:T(8,128)(2,1)} %bitcast.27, ...), custom_call_target="tpu_custom_call" | custom-call | flops 3298534883328 | bytes 2952790016 | tf_op jit(solution)/shard_map/feed_forward_both_ways/pallas_call | solution.py:444
  286.0 11.2 %norm_back_cross_out_back.1 = (f32[1024,1024]{1,0:T(8,128)}, bf16[1024,1024]{1,0:T(8,128)(2,1)}, bf16[1024,1024]{1,0:T(8,128)(2,1)}, f32[8,1024]{1,0:T(8,128)}) custom-call(f32[1024,1024]{1,0:T(8,128)} %get-tuple-element.85.hidden_ref.refs_1_, f32[1024,1024]{1,0:T(8,128)} %get-tuple-element.88.back_ref, bf16[1024,1024]{1,0:T(8,128)(2,1)} %bitcast.28, ...), custom_call_target="tpu_custom_call" | custom-call | flops 137438953472 | bytes 1342177280 | tf_op jit(solution)/shard_map/norm_back_cross_out_back/pallas_call | solution.py:502
  297.2 2.0 collective-permute-done.8.refs_2_
  299.3 9.4 %plane_pieces.3 = (bf16[128,8192]{1,0:T(8,128)(2,1)}, bf16[128,8192]{1,0:T(8,128)(2,1)}, bf16[128,8192]{1,0:T(8,128)(2,1)}, bf16[128,8192]{1,0:T(8,128)(2,1)}) custom-call(f32[8,1024]{1,0:T(8,128)} %get-tuple-element.91.refs_0_.three_ref, bf16[512,8192]{1,0:T(8,128)(2,1)} %get-tuple-element.92.refs_1_, bf16[512,8192]{1,0:T(8,128)(2,1)} %collective-permute-done.8.refs_2_), custom_call_target="tpu_custom_call" | custom-call | bytes 1610612736 | tf_op jit(solution)/shard_map/plane_pieces/pallas_call | solution.py:935
  312.2 27.8 %attend_memory_back.1 = (bf16[1024,1024]{1,0:T(8,128)(2,1)}, bf16[512,1024]{1,0:T(8,128)(2,1)}, bf16[512,1024]{1,0:T(8,128)(2,1)}, f32[8,1024]{1,0:T(8,128)}) custom-call(bf16[128,8192]{1,0:T(8,128)(2,1)} %get-tuple-element.94.refs_0_, bf16[128,8192]{1,0:T(8,128)(2,1)} %get-tuple-element.95.refs_1_, bf16[128,8192]{1,0:T(8,128)(2,1)} %get-tuple-element.96.refs_2_, ...), custom_call_target="tpu_custom_call" | custom-call | flops 824633720832 | bytes 805306368 | tf_op jit(solution)/shard_map/attend_memory_back/pallas_call | solution.py:367
  339.9 11.2 %weight_grads_by_distance.2 = (bf16[512,4096]{1,0:T(8,128)(2,1)}, bf16[512,4096]{1,0:T(8,128)(2,1)}) custom-call(s32[1]{0:T(128)} %bitcast.me_ref.refs_0_.refs_1_, bf16[1024,1024]{1,0:T(8,128)(2,1)} %get-tuple-element.83.mixed_ref.refs_7_.refs_1_, bf16[1024,1024]{1,0:T(8,128)(2,1)} %get-tuple-element.89.refs_2_, ...), custom_call_target="tpu_custom_call" | custom-call | flops 412316860416 | bytes 1275068416 | tf_op jit(solution)/shard_map/weight_grads_by_distance/pallas_call | solution.py:756
  351.2 13.1 %query_norm_back_self_out_back.1 = (f32[1024,1024]{1,0:T(8,128)}, bf16[1024,1024]{1,0:T(8,128)(2,1)}, bf16[1024,1024]{1,0:T(8,128)(2,1)}, f32[8,1024]{1,0:T(8,128)}) custom-call(bf16[512,4096]{1,0:T(8,128)(2,1)} %get-tuple-element.102.refs_0_, f32[1024,1024]{1,0:T(8,128)} %get-tuple-element.84.hidden_ref.refs_1_, f32[1024,1024]{1,0:T(8,128)} %get-tuple-element.103.refs_2_, ...), custom_call_target="tpu_custom_call" | custom-call | flops 274877906944 | bytes 1610612736 | tf_op jit(solution)/shard_map/query_norm_back_self_out_back/pallas_call | solution.py:571
  364.2 5.4 %plane_pieces.4 = (bf16[128,4096]{1,0:T(8,128)(2,1)}, bf16[128,4096]{1,0:T(8,128)(2,1)}, bf16[128,4096]{1,0:T(8,128)(2,1)}, bf16[128,4096]{1,0:T(8,128)(2,1)}) custom-call(f32[1024,1024]{1,0:T(8,128)} %get-tuple-element.104.refs_0_.refs_5_, bf16[512,4096]{1,0:T(8,128)(2,1)} %get-tuple-element.105.refs_1_, bf16[512,4096]{1,0:T(8,128)(2,1)} %collective-permute-done.9.refs_2_), custom_call_target="tpu_custom_call" | custom-call | bytes 805306368 | tf_op jit(solution)/shard_map/plane_pieces/pallas_call | solution.py:935
  371.6 36.7 %attend_causal_back.1 = (bf16[1024,1024]{1,0:T(8,128)(2,1)}, bf16[1024,1024]{1,0:T(8,128)(2,1)}, bf16[1024,1024]{1,0:T(8,128)(2,1)}, f32[8,1024]{1,0:T(8,128)}) custom-call(bf16[128,4096]{1,0:T(8,128)(2,1)} %get-tuple-element.106.refs_0_, bf16[128,4096]{1,0:T(8,128)(2,1)} %get-tuple-element.107.refs_1_, bf16[128,4096]{1,0:T(8,128)(2,1)} %get-tuple-element.108.refs_2_, ...), custom_call_target="tpu_custom_call" | custom-call | flops 1649267441664 | bytes 1073741824 | tf_op jit(solution)/shard_map/attend_causal_back/pallas_call | solution.py:367
  408.4 1.5 collective-permute-start.16
  409.9 5.6 %plane_total.3.refs_0_ = bf16[128,8192]{1,0:T(8,128)(2,1)} custom-call(f32[8,1024]{1,0:T(8,128)} %get-tuple-element.111.refs_0_.self_ref, bf16[128,8192]{1,0:T(8,128)(2,1)} %get-tuple-element.112.refs_1_, bf16[128,8192]{1,0:T(8,128)(2,1)} %collective-permute-done.10.refs_2_, bf16[128,8192]{1,0:T(8,128)(2,1)} %collective-permute-done.11.refs_3_, ...), custom_call_target="tpu_custom_call" | custom-call | bytes 671088640 | tf_op jit(solution)/shard_map/plane_total/pallas_call | solution.py:961
  415.6 13.6 %weight_grads_by_distance.3 = (bf16[512,4096]{1,0:T(8,128)(2,1)}, bf16[512,4096]{1,0:T(8,128)(2,1)}) custom-call(bf16[128,8192]{1,0:T(8,128)(2,1)} %plane_total.3.refs_0_, s32[1]{0:T(128)} %bitcast.me_ref.refs_0_.refs_1_, bf16[1024,1024]{1,0:T(8,128)(2,1)} %get-tuple-element.81.refs_0_.mixed_ref.refs_7_.refs_2_, ...), custom_call_target="tpu_custom_call" | custom-call | flops 549755813888 | bytes 1342177280 | tf_op jit(solution)/shard_map/weight_grads_by_distance/pallas_call | solution.py:756
  429.2 6.1 %memory_back.1.refs_0_ = f32[512,1024]{1,0:T(8,128)} custom-call(bf16[512,4096]{1,0:T(8,128)(2,1)} %get-tuple-element.118.refs_0_, bf16[512,1024]{1,0:T(8,128)(2,1)} %get-tuple-element.100.refs_6_.refs_1_, bf16[512,1024]{1,0:T(8,128)(2,1)} %get-tuple-element.101.refs_7_.refs_2_, ...), custom_call_target="tpu_custom_call" | custom-call | flops 137438953472 | bytes 536870912 | tf_op jit(solution)/shard_map/memory_back/pallas_call | solution.py:633
  436.7 5.4 %plane_pieces.5 = (bf16[128,4096]{1,0:T(8,128)(2,1)}, bf16[128,4096]{1,0:T(8,128)(2,1)}, bf16[128,4096]{1,0:T(8,128)(2,1)}, bf16[128,4096]{1,0:T(8,128)(2,1)}) custom-call(f32[512,1024]{1,0:T(8,128)} %memory_back.1.refs_0_, bf16[512,4096]{1,0:T(8,128)(2,1)} %get-tuple-element.119.refs_1_, bf16[512,4096]{1,0:T(8,128)(2,1)} %collective-permute-done.13.refs_2_), custom_call_target="tpu_custom_call" | custom-call | bytes 805306368 | tf_op jit(solution)/shard_map/plane_pieces/pallas_call | solution.py:935
  445.6 2.7 collective-permute-done.16.refs_4_
  448.3 3.3 plane_total.4.refs_3_
  451.7 14.6 %qkv_norm_back.1 = (f32[1024,1024]{1,0:T(8,128)}, f32[8,1024]{1,0:T(8,128)}) custom-call(bf16[128,4096]{1,0:T(8,128)(2,1)} %get-tuple-element.120.refs_0_, bf16[128,4096]{1,0:T(8,128)(2,1)} %get-tuple-element.121.refs_1_, bf16[128,4096]{1,0:T(8,128)(2,1)} %get-tuple-element.122.refs_2_, bf16[128,4096]{1,0:T(8,128)(2,1)} %plane_total.4.refs_3_, ...), custom_call_target="tpu_custom_call" | custom-call | flops 412316860416 | bytes 1476395008 | tf_op jit(solution)/shard_map/qkv_norm_back/pallas_call | solution.py:609
  466.3 1.7 small_grads.1
  468.4 9.3 %collective-permute-done.17 = f32[24,1024]{1,0:T(8,128)S(1)} collective-permute-done((f32[24,1024]{1,0:T(8,128)}, f32[24,1024]{1,0:T(8,128)S(1)}, u32[]{:S(2)}, u32[]{:S(2)}) %collective-permute-start.17) | collective-permute-done | bytes 98336 | tf_op jit(solution)/shard_map/ppermute | solution.py:1026
  478.7 5.2 layer_result.1.refs_0_
  483.9 2.3 feed_own_grads.1
  486.1 4.4 collective-permute-done.18
  491.2 1.7 own_columns.2
  493.0 3.3 plane_total.5
  498.8 3.8 collective-permute-done.20
  503.8 3.6 collective-permute-done.21
  509.2 13.2 %reduce-scatter.8.cloned.1.call-done.refs_0_ = bf16[32,4096]{1,0:T(8,128)(2,1)} async-done(((bf16[128,4096]{1,0:T(8,128)(2,1)}), bf16[32,4096]{1,0:T(8,128)(2,1)}) %reduce-scatter.8.cloned.1.call-update) | async-done | bytes 262160 | tf_op jit(solution)/shard_map/reduce_scatter | solution.py:1058
  522.4 1.7 own_columns.3
  (73 shorter events, 29.6 us)
Async XLA Ops:
  7.2 86.8 %all-gather.3.cloned.1.call-start = ((), (), s32[]{:S(2)}) async-start(), calls=%async_computation.3 | async-start | bytes 6758400 | tf_op jit(solution)/shard_map/all_gather | solution.py:1018
  9.8 210.1 %all-gather.5.cloned.1.call-start = ((), (), s32[]{:S(2)}) async-start(), calls=%async_computation.4 | async-start | bytes 17301504 | tf_op jit(solution)/shard_map/all_gather | solution.py:1018
  10.5 473.3 %reduce-scatter.4.cloned.1.call-start = ((), (), s32[]{:S(2)}) async-start(), calls=%async_computation.5 | async-start | bytes 2621440 | tf_op jit(solution)/shard_map/reduce_scatter | solution.py:1058
  10.6 14.2 %collective-permute-start.2 = (bf16[32,5120]{1,0:T(8,128)(2,1)}, bf16[32,5120]{1,0:T(8,128)(2,1)S(1)}, u32[]{:S(2)}, u32[]{:S(2)}) collective-permute-start(bf16[32,5120]{1,0:T(8,128)(2,1)} %get-tuple-element.77), channel_id=1, source_target_pairs={{0,24},{8,16},{16,8},{24,0},{1,25},{9,17},{17,9},{25,1},{2,26},{10... | collective-permute-start | bytes 983048 | tf_op jit(solution)/shard_map/ppermute | solution.py:1026
  15.7 32.5 %collective-permute-start.1 = (bf16[32,5120]{1,0:T(8,128)(2,1)}, bf16[32,5120]{1,0:T(8,128)(2,1)S(1)}, u32[]{:S(2)}, u32[]{:S(2)}) collective-permute-start(bf16[32,5120]{1,0:T(8,128)(2,1)} %get-tuple-element.77), channel_id=1, source_target_pairs={{0,16},{8,24},{16,0},{24,8},{1,17},{9,25},{17,1},{25,9},{2,18},{10... | collective-permute-start | bytes 983048 | tf_op jit(solution)/shard_map/ppermute | solution.py:1026
  15.7 32.5 %collective-permute-start = (bf16[32,5120]{1,0:T(8,128)(2,1)}, bf16[32,5120]{1,0:T(8,128)(2,1)S(1)}, u32[]{:S(2)}, u32[]{:S(2)}) collective-permute-start(bf16[32,5120]{1,0:T(8,128)(2,1)} %get-tuple-element.77), channel_id=1, source_target_pairs={{0,8},{8,0},{16,24},{24,16},{1,9},{9,1},{17,25},{25,17},{2,10},{10... | collective-permute-start | bytes 983048 | tf_op jit(solution)/shard_map/ppermute | solution.py:1026
  49.3 46.5 %copy-start = (bf16[4,32,5120]{2,1,0:T(8,128)(2,1)}, bf16[4,32,5120]{2,1,0:T(8,128)(2,1)S(1)}, u32[]{:S(2)}) copy-start(bf16[4,32,5120]{2,1,0:T(8,128)(2,1)S(1)} %pad_maximum_fusion.refs_1_.refs_2_) | copy-start | bytes 3932164
  50.4 45.4 %collective-permute-start.3 = (bf16[4,32,2560]{2,1,0:T(8,128)(2,1)}, bf16[4,32,2560]{2,1,0:T(8,128)(2,1)S(1)}, u32[]{:S(2)}, u32[]{:S(2)}) collective-permute-start(bf16[4,32,2560]{2,1,0:T(8,128)(2,1)} %get-tuple-element.139), channel_id=1, source_target_pairs={{0,2},{1,3},{2,0},{3,1},{4,6},{5,7},{6,4},{7,5},{8,10},{9,11},{10,... | collective-permute-start | bytes 1966088 | tf_op jit(solution)/shard_map/ppermute | solution.py:1026
  51.9 43.9 %collective-permute-start.4 = (bf16[4,32,2560]{2,1,0:T(8,128)(2,1)S(1)}, bf16[4,32,2560]{2,1,0:T(8,128)(2,1)S(1)}, u32[]{:S(2)}, u32[]{:S(2)}) collective-permute-start(bf16[4,32,2560]{2,1,0:T(8,128)(2,1)S(1)} %get-tuple-element.138), channel_id=1, source_target_pairs={{0,4},{1,5},{2,6},{3,7},{4,0},{5,1},{6,2},{7,3},{8,12},{9,13},{10,... | collective-permute-start | bytes 1966088 | tf_op jit(solution)/shard_map/ppermute | solution.py:1026
  95.8 0.8 copy-start.4
  96.7 0.8 copy-start.5
  100.4 40.8 %collective-permute-start.5 = (bf16[8,32,2560]{2,1,0:T(8,128)(2,1)}, bf16[8,32,2560]{2,1,0:T(8,128)(2,1)S(1)}, u32[]{:S(2)}, u32[]{:S(2)}) collective-permute-start(bf16[8,32,2560]{2,1,0:T(8,128)(2,1)} %get-tuple-element.78.refs_0_.refs_1_), channel_id=1, source_target_pairs={{0,4},{1,5},{2,6},{3,7},{4,0},{5,1},{6,2},{7,3},{8,12},{9,13},{10,... | collective-permute-start | bytes 3932168 | tf_op jit(solution)/shard_map/ppermute | solution.py:1026
  101.9 41.7 %collective-permute-start.6 = (bf16[8,32,2560]{2,1,0:T(8,128)(2,1)}, bf16[8,32,2560]{2,1,0:T(8,128)(2,1)S(1)}, u32[]{:S(2)}, u32[]{:S(2)}) collective-permute-start(bf16[8,32,2560]{2,1,0:T(8,128)(2,1)} %get-tuple-element.79.refs_1_.refs_3_), channel_id=1, source_target_pairs={{0,2},{1,3},{2,0},{3,1},{4,6},{5,7},{6,4},{7,5},{8,10},{9,11},{10,... | collective-permute-start | bytes 3932168 | tf_op jit(solution)/shard_map/ppermute | solution.py:1026
  141.2 2.4 copy-start.1
  143.6 1.1 copy-start.2
  150.5 9.0 %collective-permute-start.7 = (bf16[16,32,5120]{2,1,0:T(8,128)(2,1)}, bf16[16,32,5120]{2,1,0:T(8,128)(2,1)}, u32[]{:S(2)}, u32[]{:S(2)}) collective-permute-start(bf16[16,32,5120]{2,1,0:T(8,128)(2,1)} %near_rows.1.near_ref), channel_id=1, source_target_pairs={{0,1},{1,0},{2,3},{3,2},{4,5},{5,4},{6,7},{7,6},{8,9},{9,8},{10,11... | collective-permute-start | bytes 15728648 | tf_op jit(solution)/shard_map/ppermute | solution.py:1026
  285.7 13.6 %collective-permute-start.8 = (bf16[512,8192]{1,0:T(8,128)(2,1)}, bf16[512,8192]{1,0:T(8,128)(2,1)}, u32[]{:S(2)}, u32[]{:S(2)}) collective-permute-start(bf16[512,8192]{1,0:T(8,128)(2,1)} %get-tuple-element.93), channel_id=1, source_target_pairs={{0,1},{1,0},{2,3},{3,2},{4,5},{5,4},{6,7},{7,6},{8,9},{9,8},{10,11... | collective-permute-start | bytes 25165832 | tf_op jit(solution)/shard_map/ppermute | solution.py:1026
  308.7 99.7 %collective-permute-start.10 = (bf16[128,8192]{1,0:T(8,128)(2,1)}, bf16[128,8192]{1,0:T(8,128)(2,1)}, u32[]{:S(2)}, u32[]{:S(2)}) collective-permute-start(bf16[128,8192]{1,0:T(8,128)(2,1)} %get-tuple-element.94.refs_0_), channel_id=1, source_target_pairs={{0,2},{1,3},{2,0},{3,1},{4,6},{5,7},{6,4},{7,5},{8,10},{9,11},{10,... | collective-permute-start | bytes 6291464 | tf_op jit(solution)/shard_map/ppermute | solution.py:1026
  309.9 100.0 %collective-permute-start.11 = (bf16[128,8192]{1,0:T(8,128)(2,1)}, bf16[128,8192]{1,0:T(8,128)(2,1)}, u32[]{:S(2)}, u32[]{:S(2)}) collective-permute-start(bf16[128,8192]{1,0:T(8,128)(2,1)} %get-tuple-element.95.refs_1_), channel_id=1, source_target_pairs={{0,4},{1,5},{2,6},{3,7},{4,0},{5,1},{6,2},{7,3},{8,12},{9,13},{10,... | collective-permute-start | bytes 6291464 | tf_op jit(solution)/shard_map/ppermute | solution.py:1026
  310.7 99.2 %collective-permute-start.12 = (bf16[128,8192]{1,0:T(8,128)(2,1)}, bf16[128,8192]{1,0:T(8,128)(2,1)}, u32[]{:S(2)}, u32[]{:S(2)}) collective-permute-start(bf16[128,8192]{1,0:T(8,128)(2,1)} %get-tuple-element.96.refs_2_), channel_id=1, source_target_pairs={{0,6},{1,7},{2,4},{3,5},{4,2},{5,3},{6,0},{7,1},{8,14},{9,15},{10,... | collective-permute-start | bytes 6291464 | tf_op jit(solution)/shard_map/ppermute | solution.py:1026
  351.1 13.2 %collective-permute-start.9 = (bf16[512,4096]{1,0:T(8,128)(2,1)}, bf16[512,4096]{1,0:T(8,128)(2,1)}, u32[]{:S(2)}, u32[]{:S(2)}) collective-permute-start(bf16[512,4096]{1,0:T(8,128)(2,1)} %get-tuple-element.102.refs_0_), channel_id=1, source_target_pairs={{0,1},{1,0},{2,3},{3,2},{4,5},{5,4},{6,7},{7,6},{8,9},{9,8},{10,11... | collective-permute-start | bytes 12582920 | tf_op jit(solution)/shard_map/ppermute | solution.py:1026
  369.6 74.5 %collective-permute-start.14 = (bf16[128,4096]{1,0:T(8,128)(2,1)}, bf16[128,4096]{1,0:T(8,128)(2,1)}, u32[]{:S(2)}, u32[]{:S(2)}) collective-permute-start(bf16[128,4096]{1,0:T(8,128)(2,1)} %get-tuple-element.106.refs_0_), channel_id=1, source_target_pairs={{0,2},{1,3},{2,0},{3,1},{4,6},{5,7},{6,4},{7,5},{8,10},{9,11},{10,... | collective-permute-start | bytes 3145736 | tf_op jit(solution)/shard_map/ppermute | solution.py:1026
  370.9 74.7 %collective-permute-start.15 = (bf16[128,4096]{1,0:T(8,128)(2,1)}, bf16[128,4096]{1,0:T(8,128)(2,1)}, u32[]{:S(2)}, u32[]{:S(2)}) collective-permute-start(bf16[128,4096]{1,0:T(8,128)(2,1)} %get-tuple-element.107.refs_1_), channel_id=1, source_target_pairs={{0,4},{1,5},{2,6},{3,7},{4,0},{5,1},{6,2},{7,3},{8,12},{9,13},{10,... | collective-permute-start | bytes 3145736 | tf_op jit(solution)/shard_map/ppermute | solution.py:1026
  408.4 39.9 %collective-permute-start.16 = (bf16[128,4096]{1,0:T(8,128)(2,1)}, bf16[128,4096]{1,0:T(8,128)(2,1)}, u32[]{:S(2)}, u32[]{:S(2)}) collective-permute-start(bf16[128,4096]{1,0:T(8,128)(2,1)} %get-tuple-element.108.refs_2_), channel_id=1, source_target_pairs={{0,6},{1,7},{2,4},{3,5},{4,2},{5,3},{6,0},{7,1},{8,14},{9,15},{10,... | collective-permute-start | bytes 3145736 | tf_op jit(solution)/shard_map/ppermute | solution.py:1026
  415.5 75.7 %reduce-scatter.6.cloned.1.call-start = ((), (), s32[]{:S(2)}) async-start(), calls=%async_computation.6 | async-start | bytes 1310720 | tf_op jit(solution)/shard_map/reduce_scatter | solution.py:1058
  429.1 7.6 %collective-permute-start.13 = (bf16[512,4096]{1,0:T(8,128)(2,1)}, bf16[512,4096]{1,0:T(8,128)(2,1)}, u32[]{:S(2)}, u32[]{:S(2)}) collective-permute-start(bf16[512,4096]{1,0:T(8,128)(2,1)} %get-tuple-element.118.refs_0_), channel_id=1, source_target_pairs={{0,1},{1,0},{2,3},{3,2},{4,5},{5,4},{6,7},{7,6},{8,9},{9,8},{10,11... | collective-permute-start | bytes 12582920 | tf_op jit(solution)/shard_map/ppermute | solution.py:1026
  442.1 50.8 %collective-permute-start.22 = (bf16[128,4096]{1,0:T(8,128)(2,1)}, bf16[128,4096]{1,0:T(8,128)(2,1)}, u32[]{:S(2)}, u32[]{:S(2)}) collective-permute-start(bf16[128,4096]{1,0:T(8,128)(2,1)} %get-tuple-element.120.refs_0_), channel_id=1, source_target_pairs={{0,2},{1,3},{2,0},{3,1},{4,6},{5,7},{6,4},{7,5},{8,10},{9,11},{10,... | collective-permute-start | bytes 3145736 | tf_op jit(solution)/shard_map/ppermute | solution.py:1026
  443.4 49.6 %collective-permute-start.23 = (bf16[128,4096]{1,0:T(8,128)(2,1)}, bf16[128,4096]{1,0:T(8,128)(2,1)}, u32[]{:S(2)}, u32[]{:S(2)}) collective-permute-start(bf16[128,4096]{1,0:T(8,128)(2,1)} %get-tuple-element.121.refs_1_), channel_id=1, source_target_pairs={{0,4},{1,5},{2,6},{3,7},{4,0},{5,1},{6,2},{7,3},{8,12},{9,13},{10,... | collective-permute-start | bytes 3145736 | tf_op jit(solution)/shard_map/ppermute | solution.py:1026
  444.1 48.8 %collective-permute-start.24 = (bf16[128,4096]{1,0:T(8,128)(2,1)}, bf16[128,4096]{1,0:T(8,128)(2,1)}, u32[]{:S(2)}, u32[]{:S(2)}) collective-permute-start(bf16[128,4096]{1,0:T(8,128)(2,1)} %get-tuple-element.122.refs_2_), channel_id=1, source_target_pairs={{0,6},{1,7},{2,4},{3,5},{4,2},{5,3},{6,0},{7,1},{8,14},{9,15},{10,... | collective-permute-start | bytes 3145736 | tf_op jit(solution)/shard_map/ppermute | solution.py:1026
  451.6 70.8 %reduce-scatter.8.cloned.1.call-start = ((), (), s32[]{:S(2)}) async-start(), calls=%async_computation.7 | async-start | bytes 1310720 | tf_op jit(solution)/shard_map/reduce_scatter | solution.py:1058
  467.9 9.7 %collective-permute-start.17 = (f32[24,1024]{1,0:T(8,128)}, f32[24,1024]{1,0:T(8,128)S(1)}, u32[]{:S(2)}, u32[]{:S(2)}) collective-permute-start(f32[24,1024]{1,0:T(8,128)} %small_grads.1), channel_id=1, source_target_pairs={{0,8},{8,0},{16,24},{24,16},{1,9},{9,1},{17,25},{25,17},{2,10},{10... | collective-permute-start | bytes 294920 | tf_op jit(solution)/shard_map/ppermute | solution.py:1026
  478.6 12.0 %collective-permute-start.18 = (f32[24,1024]{1,0:T(8,128)S(1)}, f32[24,1024]{1,0:T(8,128)S(1)}, u32[]{:S(2)}, u32[]{:S(2)}) collective-permute-start(f32[24,1024]{1,0:T(8,128)S(1)} %add.29), channel_id=1, source_target_pairs={{0,16},{8,24},{16,0},{24,8},{1,17},{9,25},{17,1},{25,9},{2,18},{10... | collective-permute-start | bytes 294920 | tf_op jit(solution)/shard_map/ppermute | solution.py:1026
  493.0 3.3 copy-start.3
  496.3 1.4 collective-permute-start.19
  497.7 4.9 collective-permute-start.20
  502.6 4.7 collective-permute-start.21
Sparse Core Ops, SparseCore 0:
  11.4 82.5 all-gather.2
  97.4 122.4 all-gather.4
  415.6 42.0 reduce-scatter.3
  460.0 30.6 reduce-scatter.5
  496.4 25.9 reduce-scatter.7

commit v5 on v4

--- a/solution.py
+++ b/solution.py
@@ -242,22 +242,23 @@
     allowed = causal_block() if causal else None
     first = lane < HEAD
     value_wide = [jnp.where(heads[side][0], value, jnp.ones((), bf16)) for side in (0, 1)]
-    for at in range(0, rows, BLOCK):
-        keys = at + BLOCK if causal else keys_all
+    block = BLOCK if causal else rows
+    for at in range(0, rows, block):
+        keys = at + block if causal else keys_all
         got, tops = [], []
         for side in (0, 1):
             _, _, query_wide, _, key_wide = heads[side]
-            scores = scores_by_key(key_wide, query_wide[at : at + BLOCK], keys, allowed)
+            scores = scores_by_key(key_wide, query_wide[at : at + block], keys, allowed)
             top = jnp.max(scores, axis=0, keepdims=True)
             exponent = jnp.exp(scores - top)
             got.append(tn(exponent.astype(bf16), value_wide[side][:keys]))
             tops.append(top)
         total = jnp.where(first, got[1], got[0])
         mixed = jnp.where(first, got[0], got[1]) / pltpu.roll(total, HEAD, 1)
-        mixed_ref[at : at + BLOCK, :] = mixed.astype(bf16)
+        mixed_ref[at : at + block, :] = mixed.astype(bf16)
         logs = jnp.log(total).T
-        stat_ref[0, 0:1, at : at + BLOCK] = tops[0] + logs[HEAD : HEAD + 1]
-        stat_ref[0, 1:2, at : at + BLOCK] = tops[1] + logs[0:1]
+        stat_ref[0, 0:1, at : at + block] = tops[0] + logs[HEAD : HEAD + 1]
+        stat_ref[0, 1:2, at : at + block] = tops[1] + logs[0:1]
 
 
 def pair_block(rows, column=0):

time: 540 us -> 540 us (level)
  no operation moved by 1% of the time
where the time goes in v5:
time: 540 us; the launch traced here: 531 us
  Pallas kernels  348 us (64%)
  waiting for transfers between devices  131 us (24%)
  starting transfers between devices  24.8 us (5%)
  between operations  15.5 us (3%)
  local copies, waits for them, and re-layouts  7.4 us (1%)
    ppermute x25, waiting for transfers between devices, exchange(): return lax.ppermute(array, axis, [(i, i ^ distance) for i in range(size)])  71.9 us
    pallas_call x1, Pallas kernels, feed(): pl.pallas_call(functools.partial(feed_kernel, split[1:] or None), grid=(s...  65.7 us
    pallas_call x2, Pallas kernels, attend_back(): pl.pallas_call(kernel, grid=(pairs,), in_specs=in_specs, out_specs=[pair_...  64.5 us
    all_gather x2, waiting for transfers between devices, gather(): return lax.all_gather(shard, AXES, axis=0, tiled=True)  45.3 us
    pallas_call x2, Pallas kernels, attend(): pl.pallas_call(functools.partial(attend_kernel, causal), grid=(pairs,), i...  44.8 us
    pallas_call x2, Pallas kernels, weight_grads(): pl.pallas_call(kernel, grid=(len(picks),), in_specs=in_specs, out_specs=[...  24.7 us
    ppermute x25, starting transfers between devices, exchange(): return lax.ppermute(array, axis, [(i, i ^ distance) for i in range(size)])  24.6 us
    pallas_call x3, Pallas kernels, plane_pieces(): pl.pallas_call(kernel, grid=(steps,), in_specs=in_specs, out_specs=[pl.Bl...  20.2 us
  transfers between devices with their start and end apart: 30, of which 16 were waited for; matrix products, arithmetic and copies ran while one was open for 2% of the time, Pallas kernels for 50%

profile of v5, /device:TPU:0, one launch (start us, length us, event | category | flops | bytes accessed | tf_op | source)
XLA Modules:
  0.0 530.9 jit_solution(11124386965479896536)
XLA Ops:
  7.2 2.5 shards_to_gather.1
  10.6 5.1 collective-permute-start.2
  16.3 8.4 %collective-permute-done.2 = bf16[32,5120]{1,0:T(8,128)(2,1)S(1)} collective-permute-done((bf16[32,5120]{1,0:T(8,128)(2,1)}, bf16[32,5120]{1,0:T(8,128)(2,1)S(1)}, u32[]{:S(2)}, u32[]{:S(2)}) %collective-permute-start.2) | collective-permute-done | bytes 327712 | tf_op jit(solution)/shard_map/ppermute | solution.py:1027
  24.8 23.4 %collective-permute-done.1 = bf16[32,5120]{1,0:T(8,128)(2,1)S(1)} collective-permute-done((bf16[32,5120]{1,0:T(8,128)(2,1)}, bf16[32,5120]{1,0:T(8,128)(2,1)S(1)}, u32[]{:S(2)}, u32[]{:S(2)}) %collective-permute-start.1) | collective-permute-done | bytes 327712 | tf_op jit(solution)/shard_map/ppermute | solution.py:1027
  50.4 1.5 collective-permute-start.3
  51.9 1.5 collective-permute-start.4
  54.1 39.9 %all-gather.3.cloned.1.call-done.refs_0_.refs_3_.refs_6_ = bf16[1024,3200]{1,0:T(8,128)(2,1)} async-done(((bf16[32,3200]{1,0:T(8,128)(2,1)}), bf16[1024,3200]{1,0:T(8,128)(2,1)}) %all-gather.3.cloned.1.call-update) | async-done | bytes 6553616 | tf_op jit(solution)/shard_map/all_gather | solution.py:1019
  97.5 2.9 two_rows.1
  100.4 1.5 collective-permute-start.5
  103.9 12.8 %norm_and_qkv.1 = (bf16[1024,1024]{1,0:T(8,128)(2,1)}, bf16[1024,3072]{1,0:T(8,128)(2,1)}) custom-call(bf16[8,32,2560]{2,1,0:T(8,128)(2,1)} %get-tuple-element.78.refs_0_.refs_1_, bf16[8,32,2560]{2,1,0:T(8,128)(2,1)} %get-tuple-element.79.refs_1_.refs_3_, bf16[1024,1024]{1,0:T(8,128)(2,1)} %bitcast.15, ...), custom_call_target="tpu_custom_call" | custom-call | flops 6442450944 | bytes 16777216 | tf_op jit(solution)/shard_map/norm_and_qkv/pallas_call | solution.py:119
  116.7 23.7 %attend_causal.1 = (bf16[1024,1024]{1,0:T(8,128)(2,1)}, f32[8,2,1024]{2,1,0:T(2,128)}) custom-call(s32[1]{0:T(128)S(6)} %copy.36.length_ref.refs_3_, bf16[1024,3072]{1,0:T(8,128)(2,1)} %get-tuple-element.80.query_ref.key_ref.value_ref.refs_4_.refs_5_.refs_6_, bf16[1024,3072]{1,0:T(8,128)(2,1)} %get-tuple-element.80.query_ref.key_ref.value_ref.refs_4_.refs_5_.refs_6_, ...), custom_call_target="tpu_custom_call" | custom-call | flops 17179869184 | bytes 8388608 | tf_op jit(solution)/shard_map/attend_causal/pallas_call | solution.py:271
  141.2 2.4 collective-permute-done.6.refs_4_
  144.6 5.9 %near_rows.1.near_ref = bf16[16,32,5120]{2,1,0:T(8,128)(2,1)} custom-call(bf16[1024,1024]{1,0:T(8,128)(2,1)} %get-tuple-element.81.refs_0_.mixed_ref.refs_7_.refs_2_, bf16[8,32,2560]{2,1,0:T(8,128)(2,1)} %get-tuple-element.78.refs_0_.refs_1_, bf16[8,32,2560]{2,1,0:T(8,128)(2,1)} %copy-done.1, bf16[8,32,2560]{2,1,0:T(8,128)(2,1)} %get-tuple-element.79.refs_1_.refs_3_, ...), custom_call_target="tpu_custom_call" | custom-call | bytes 335544320 | tf_op jit(solution)/shard_map/near_rows/pallas_call | solution.py:823
  151.2 8.3 %collective-permute-done.7.far_ref = bf16[16,32,5120]{2,1,0:T(8,128)(2,1)} collective-permute-done((bf16[16,32,5120]{2,1,0:T(8,128)(2,1)}, bf16[16,32,5120]{2,1,0:T(8,128)(2,1)}, u32[]{:S(2)}, u32[]{:S(2)}) %collective-permute-start.7) | collective-permute-done | bytes 5242912 | tf_op jit(solution)/shard_map/ppermute | solution.py:1027
  159.5 9.9 %place_by_device.1.out_ref.query_ref.weight_ref.refs_4_.refs_5_.refs_3_ = bf16[1024,5120]{1,0:T(8,128)(2,1)} custom-call(s32[1]{0:T(128)} %bitcast.me_ref.refs_0_.refs_1_, bf16[16,32,5120]{2,1,0:T(8,128)(2,1)} %near_rows.1.near_ref, bf16[16,32,5120]{2,1,0:T(8,128)(2,1)} %collective-permute-done.7.far_ref), custom_call_target="tpu_custom_call" | custom-call | bytes 1342177280 | tf_op jit(solution)/shard_map/place_by_device/pallas_call | solution.py:852
  169.4 5.9 %memory_keys_values.1.key_ref.value_ref.refs_5_.refs_6_ = bf16[512,2048]{1,0:T(8,128)(2,1)} custom-call(bf16[512,1024]{1,0:T(8,128)(2,1)} %bitcast.19, bf16[1024,5120]{1,0:T(8,128)(2,1)} %place_by_device.1.out_ref.query_ref.weight_ref.refs_4_.refs_5_.refs_3_, f32[24,1024]{1,0:T(8,128)} %slice_convert_fusion.refs_4_.table_ref.refs_6_.refs_7_.refs_3_), custom_call_target="tpu_custom_call" | custom-call | flops 2147483648 | bytes 7340032 | tf_op jit(solution)/shard_map/memory_keys_values/pallas_call | solution.py:170
  175.3 10.0 %self_out_norm_query.1 = (f32[1024,1024]{1,0:T(8,128)}, bf16[1024,1024]{1,0:T(8,128)(2,1)}, bf16[1024,1024]{1,0:T(8,128)(2,1)}) custom-call(bf16[1024,1024]{1,0:T(8,128)(2,1)} %bitcast.16, bf16[1024,1024]{1,0:T(8,128)(2,1)} %get-tuple-element.81.refs_0_.mixed_ref.refs_7_.refs_2_, ...), custom_call_target="tpu_custom_call" | custom-call | flops 4294967296 | bytes 16777216 | tf_op jit(solution)/shard_map/self_out_norm_query/pallas_call | solution.py:143
  185.3 21.2 %attend_memory.1 = (bf16[1024,1024]{1,0:T(8,128)(2,1)}, f32[8,2,1024]{2,1,0:T(2,128)}) custom-call(s32[1]{0:T(128)S(6)} %copy.37.length_ref.refs_3_, bf16[1024,1024]{1,0:T(8,128)(2,1)} %get-tuple-element.82.query_ref.refs_4_, bf16[512,2048]{1,0:T(8,128)(2,1)} %memory_keys_values.1.key_ref.value_ref.refs_5_.refs_6_, ...), custom_call_target="tpu_custom_call" | custom-call | flops 8589934592 | bytes 6291456 | tf_op jit(solution)/shard_map/attend_memory/pallas_call | solution.py:271
  206.5 8.1 %cross_out_norm.1 = (f32[1024,1024]{1,0:T(8,128)}, bf16[1024,1024]{1,0:T(8,128)(2,1)}) custom-call(f32[1024,1024]{1,0:T(8,128)} %get-tuple-element.84.hidden_ref.refs_1_, bf16[1024,1024]{1,0:T(8,128)(2,1)} %get-tuple-element.83.mixed_ref.refs_7_.refs_1_, bf16[1024,5120]{1,0:T(8,128)(2,1)} %place_by_device.1.out_ref.query_ref.weight_ref.refs_4_.refs_5_.refs_3_, ...), custom_call_target="tpu_custom_call" | custom-call | flops 2147483648 | bytes 14680064 | tf_op jit(solution)/shard_map/cross_out_norm/pallas_call | solution.py:192
  214.6 5.4 %all-gather.5.cloned.1.call-done.weight_ref = bf16[1024,8192]{1,0:T(8,128)(2,1)} async-done(((bf16[32,8192]{1,0:T(8,128)(2,1)}), bf16[1024,8192]{1,0:T(8,128)(2,1)}) %all-gather.5.cloned.1.call-update) | async-done | bytes 16777232 | tf_op jit(solution)/shard_map/all_gather | solution.py:1019
  219.9 65.7 %feed_forward_both_ways.1 = (f32[1024,1024]{1,0:T(8,128)}, f32[1024,1024]{1,0:T(8,128)}, f32[4,8,1024]{2,1,0:T(8,128)}, bf16[512,8192]{1,0:T(8,128)(2,1)}, bf16[512,8192]{1,0:T(8,128)(2,1)}) custom-call(s32[1]{0:T(128)} %bitcast.me_ref.refs_0_.refs_1_, bf16[1024,1024]{1,0:T(8,128)(2,1)} %get-tuple-element.86.normed_ref, bf16[1024,1024]{1,0:T(8,128)(2,1)} %bitcast.27, ...), custom_call_target="tpu_custom_call" | custom-call | flops 3298534883328 | bytes 2952790016 | tf_op jit(solution)/shard_map/feed_forward_both_ways/pallas_call | solution.py:445
  286.0 11.2 %norm_back_cross_out_back.1 = (f32[1024,1024]{1,0:T(8,128)}, bf16[1024,1024]{1,0:T(8,128)(2,1)}, bf16[1024,1024]{1,0:T(8,128)(2,1)}, f32[8,1024]{1,0:T(8,128)}) custom-call(f32[1024,1024]{1,0:T(8,128)} %get-tuple-element.85.hidden_ref.refs_1_, f32[1024,1024]{1,0:T(8,128)} %get-tuple-element.88.back_ref, bf16[1024,1024]{1,0:T(8,128)(2,1)} %bitcast.28, ...), custom_call_target="tpu_custom_call" | custom-call | flops 137438953472 | bytes 1342177280 | tf_op jit(solution)/shard_map/norm_back_cross_out_back/pallas_call | solution.py:503
  297.2 2.0 collective-permute-done.8.refs_2_
  299.3 9.4 %plane_pieces.3 = (bf16[128,8192]{1,0:T(8,128)(2,1)}, bf16[128,8192]{1,0:T(8,128)(2,1)}, bf16[128,8192]{1,0:T(8,128)(2,1)}, bf16[128,8192]{1,0:T(8,128)(2,1)}) custom-call(f32[8,1024]{1,0:T(8,128)} %get-tuple-element.91.refs_0_.three_ref, bf16[512,8192]{1,0:T(8,128)(2,1)} %get-tuple-element.92.refs_1_, bf16[512,8192]{1,0:T(8,128)(2,1)} %collective-permute-done.8.refs_2_), custom_call_target="tpu_custom_call" | custom-call | bytes 1610612736 | tf_op jit(solution)/shard_map/plane_pieces/pallas_call | solution.py:936
  312.2 27.8 %attend_memory_back.1 = (bf16[1024,1024]{1,0:T(8,128)(2,1)}, bf16[512,1024]{1,0:T(8,128)(2,1)}, bf16[512,1024]{1,0:T(8,128)(2,1)}, f32[8,1024]{1,0:T(8,128)}) custom-call(bf16[128,8192]{1,0:T(8,128)(2,1)} %get-tuple-element.94.refs_0_, bf16[128,8192]{1,0:T(8,128)(2,1)} %get-tuple-element.95.refs_1_, bf16[128,8192]{1,0:T(8,128)(2,1)} %get-tuple-element.96.refs_2_, ...), custom_call_target="tpu_custom_call" | custom-call | flops 824633720832 | bytes 805306368 | tf_op jit(solution)/shard_map/attend_memory_back/pallas_call | solution.py:368
  339.9 11.2 %weight_grads_by_distance.2 = (bf16[512,4096]{1,0:T(8,128)(2,1)}, bf16[512,4096]{1,0:T(8,128)(2,1)}) custom-call(s32[1]{0:T(128)} %bitcast.me_ref.refs_0_.refs_1_, bf16[1024,1024]{1,0:T(8,128)(2,1)} %get-tuple-element.83.mixed_ref.refs_7_.refs_1_, bf16[1024,1024]{1,0:T(8,128)(2,1)} %get-tuple-element.89.refs_2_, ...), custom_call_target="tpu_custom_call" | custom-call | flops 412316860416 | bytes 1275068416 | tf_op jit(solution)/shard_map/weight_grads_by_distance/pallas_call | solution.py:757
  351.2 13.1 %query_norm_back_self_out_back.1 = (f32[1024,1024]{1,0:T(8,128)}, bf16[1024,1024]{1,0:T(8,128)(2,1)}, bf16[1024,1024]{1,0:T(8,128)(2,1)}, f32[8,1024]{1,0:T(8,128)}) custom-call(bf16[512,4096]{1,0:T(8,128)(2,1)} %get-tuple-element.102.refs_0_, f32[1024,1024]{1,0:T(8,128)} %get-tuple-element.84.hidden_ref.refs_1_, f32[1024,1024]{1,0:T(8,128)} %get-tuple-element.103.refs_2_, ...), custom_call_target="tpu_custom_call" | custom-call | flops 274877906944 | bytes 1610612736 | tf_op jit(solution)/shard_map/query_norm_back_self_out_back/pallas_call | solution.py:572
  364.2 5.4 %plane_pieces.4 = (bf16[128,4096]{1,0:T(8,128)(2,1)}, bf16[128,4096]{1,0:T(8,128)(2,1)}, bf16[128,4096]{1,0:T(8,128)(2,1)}, bf16[128,4096]{1,0:T(8,128)(2,1)}) custom-call(f32[1024,1024]{1,0:T(8,128)} %get-tuple-element.104.refs_0_.refs_5_, bf16[512,4096]{1,0:T(8,128)(2,1)} %get-tuple-element.105.refs_1_, bf16[512,4096]{1,0:T(8,128)(2,1)} %collective-permute-done.9.refs_2_), custom_call_target="tpu_custom_call" | custom-call | bytes 805306368 | tf_op jit(solution)/shard_map/plane_pieces/pallas_call | solution.py:936
  371.6 36.7 %attend_causal_back.1 = (bf16[1024,1024]{1,0:T(8,128)(2,1)}, bf16[1024,1024]{1,0:T(8,128)(2,1)}, bf16[1024,1024]{1,0:T(8,128)(2,1)}, f32[8,1024]{1,0:T(8,128)}) custom-call(bf16[128,4096]{1,0:T(8,128)(2,1)} %get-tuple-element.106.refs_0_, bf16[128,4096]{1,0:T(8,128)(2,1)} %get-tuple-element.107.refs_1_, bf16[128,4096]{1,0:T(8,128)(2,1)} %get-tuple-element.108.refs_2_, ...), custom_call_target="tpu_custom_call" | custom-call | flops 1649267441664 | bytes 1073741824 | tf_op jit(solution)/shard_map/attend_causal_back/pallas_call | solution.py:368
  408.4 1.5 collective-permute-start.16
  409.9 5.6 %plane_total.3.refs_0_ = bf16[128,8192]{1,0:T(8,128)(2,1)} custom-call(f32[8,1024]{1,0:T(8,128)} %get-tuple-element.111.refs_0_.self_ref, bf16[128,8192]{1,0:T(8,128)(2,1)} %get-tuple-element.112.refs_1_, bf16[128,8192]{1,0:T(8,128)(2,1)} %collective-permute-done.10.refs_2_, bf16[128,8192]{1,0:T(8,128)(2,1)} %collective-permute-done.11.refs_3_, ...), custom_call_target="tpu_custom_call" | custom-call | bytes 671088640 | tf_op jit(solution)/shard_map/plane_total/pallas_call | solution.py:962
  415.6 13.6 %weight_grads_by_distance.3 = (bf16[512,4096]{1,0:T(8,128)(2,1)}, bf16[512,4096]{1,0:T(8,128)(2,1)}) custom-call(bf16[128,8192]{1,0:T(8,128)(2,1)} %plane_total.3.refs_0_, s32[1]{0:T(128)} %bitcast.me_ref.refs_0_.refs_1_, bf16[1024,1024]{1,0:T(8,128)(2,1)} %get-tuple-element.81.refs_0_.mixed_ref.refs_7_.refs_2_, ...), custom_call_target="tpu_custom_call" | custom-call | flops 549755813888 | bytes 1342177280 | tf_op jit(solution)/shard_map/weight_grads_by_distance/pallas_call | solution.py:757
  429.2 6.1 %memory_back.1.refs_0_ = f32[512,1024]{1,0:T(8,128)} custom-call(bf16[512,4096]{1,0:T(8,128)(2,1)} %get-tuple-element.118.refs_0_, bf16[512,1024]{1,0:T(8,128)(2,1)} %get-tuple-element.100.refs_6_.refs_1_, bf16[512,1024]{1,0:T(8,128)(2,1)} %get-tuple-element.101.refs_7_.refs_2_, ...), custom_call_target="tpu_custom_call" | custom-call | flops 137438953472 | bytes 536870912 | tf_op jit(solution)/shard_map/memory_back/pallas_call | solution.py:634
  436.7 5.4 %plane_pieces.5 = (bf16[128,4096]{1,0:T(8,128)(2,1)}, bf16[128,4096]{1,0:T(8,128)(2,1)}, bf16[128,4096]{1,0:T(8,128)(2,1)}, bf16[128,4096]{1,0:T(8,128)(2,1)}) custom-call(f32[512,1024]{1,0:T(8,128)} %memory_back.1.refs_0_, bf16[512,4096]{1,0:T(8,128)(2,1)} %get-tuple-element.119.refs_1_, bf16[512,4096]{1,0:T(8,128)(2,1)} %collective-permute-done.13.refs_2_), custom_call_target="tpu_custom_call" | custom-call | bytes 805306368 | tf_op jit(solution)/shard_map/plane_pieces/pallas_call | solution.py:936
  445.6 2.7 collective-permute-done.16.refs_4_
  448.3 3.3 plane_total.4.refs_3_
  451.7 14.6 %qkv_norm_back.1 = (f32[1024,1024]{1,0:T(8,128)}, f32[8,1024]{1,0:T(8,128)}) custom-call(bf16[128,4096]{1,0:T(8,128)(2,1)} %get-tuple-element.120.refs_0_, bf16[128,4096]{1,0:T(8,128)(2,1)} %get-tuple-element.121.refs_1_, bf16[128,4096]{1,0:T(8,128)(2,1)} %get-tuple-element.122.refs_2_, bf16[128,4096]{1,0:T(8,128)(2,1)} %plane_total.4.refs_3_, ...), custom_call_target="tpu_custom_call" | custom-call | flops 412316860416 | bytes 1476395008 | tf_op jit(solution)/shard_map/qkv_norm_back/pallas_call | solution.py:610
  466.3 1.7 small_grads.1
  468.4 9.3 %collective-permute-done.17 = f32[24,1024]{1,0:T(8,128)S(1)} collective-permute-done((f32[24,1024]{1,0:T(8,128)}, f32[24,1024]{1,0:T(8,128)S(1)}, u32[]{:S(2)}, u32[]{:S(2)}) %collective-permute-start.17) | collective-permute-done | bytes 98336 | tf_op jit(solution)/shard_map/ppermute | solution.py:1027
  478.7 5.2 layer_result.1.refs_0_
  483.9 2.3 feed_own_grads.1
  486.1 4.4 collective-permute-done.18
  491.2 1.7 own_columns.2
  493.0 3.3 plane_total.5
  498.7 3.9 collective-permute-done.20
  503.8 3.5 collective-permute-done.21
  509.2 13.2 %reduce-scatter.8.cloned.1.call-done.refs_0_ = bf16[32,4096]{1,0:T(8,128)(2,1)} async-done(((bf16[128,4096]{1,0:T(8,128)(2,1)}), bf16[32,4096]{1,0:T(8,128)(2,1)}) %reduce-scatter.8.cloned.1.call-update) | async-done | bytes 262160 | tf_op jit(solution)/shard_map/reduce_scatter | solution.py:1059
  522.4 1.7 own_columns.3
  (73 shorter events, 29.5 us)
Async XLA Ops:
  7.2 86.8 %all-gather.3.cloned.1.call-start = ((), (), s32[]{:S(2)}) async-start(), calls=%async_computation.3 | async-start | bytes 6758400 | tf_op jit(solution)/shard_map/all_gather | solution.py:1019
  9.8 210.1 %all-gather.5.cloned.1.call-start = ((), (), s32[]{:S(2)}) async-start(), calls=%async_computation.4 | async-start | bytes 17301504 | tf_op jit(solution)/shard_map/all_gather | solution.py:1019
  10.5 473.3 %reduce-scatter.4.cloned.1.call-start = ((), (), s32[]{:S(2)}) async-start(), calls=%async_computation.5 | async-start | bytes 2621440 | tf_op jit(solution)/shard_map/reduce_scatter | solution.py:1059
  10.6 14.2 %collective-permute-start.2 = (bf16[32,5120]{1,0:T(8,128)(2,1)}, bf16[32,5120]{1,0:T(8,128)(2,1)S(1)}, u32[]{:S(2)}, u32[]{:S(2)}) collective-permute-start(bf16[32,5120]{1,0:T(8,128)(2,1)} %get-tuple-element.77), channel_id=1, source_target_pairs={{0,24},{8,16},{16,8},{24,0},{1,25},{9,17},{17,9},{25,1},{2,26},{10... | collective-permute-start | bytes 983048 | tf_op jit(solution)/shard_map/ppermute | solution.py:1027
  15.7 32.5 %collective-permute-start.1 = (bf16[32,5120]{1,0:T(8,128)(2,1)}, bf16[32,5120]{1,0:T(8,128)(2,1)S(1)}, u32[]{:S(2)}, u32[]{:S(2)}) collective-permute-start(bf16[32,5120]{1,0:T(8,128)(2,1)} %get-tuple-element.77), channel_id=1, source_target_pairs={{0,16},{8,24},{16,0},{24,8},{1,17},{9,25},{17,1},{25,9},{2,18},{10... | collective-permute-start | bytes 983048 | tf_op jit(solution)/shard_map/ppermute | solution.py:1027
  15.7 32.5 %collective-permute-start = (bf16[32,5120]{1,0:T(8,128)(2,1)}, bf16[32,5120]{1,0:T(8,128)(2,1)S(1)}, u32[]{:S(2)}, u32[]{:S(2)}) collective-permute-start(bf16[32,5120]{1,0:T(8,128)(2,1)} %get-tuple-element.77), channel_id=1, source_target_pairs={{0,8},{8,0},{16,24},{24,16},{1,9},{9,1},{17,25},{25,17},{2,10},{10... | collective-permute-start | bytes 983048 | tf_op jit(solution)/shard_map/ppermute | solution.py:1027
  49.3 46.5 %copy-start = (bf16[4,32,5120]{2,1,0:T(8,128)(2,1)}, bf16[4,32,5120]{2,1,0:T(8,128)(2,1)S(1)}, u32[]{:S(2)}) copy-start(bf16[4,32,5120]{2,1,0:T(8,128)(2,1)S(1)} %pad_maximum_fusion.refs_1_.refs_2_) | copy-start | bytes 3932164
  50.4 45.4 %collective-permute-start.3 = (bf16[4,32,2560]{2,1,0:T(8,128)(2,1)}, bf16[4,32,2560]{2,1,0:T(8,128)(2,1)S(1)}, u32[]{:S(2)}, u32[]{:S(2)}) collective-permute-start(bf16[4,32,2560]{2,1,0:T(8,128)(2,1)} %get-tuple-element.139), channel_id=1, source_target_pairs={{0,2},{1,3},{2,0},{3,1},{4,6},{5,7},{6,4},{7,5},{8,10},{9,11},{10,... | collective-permute-start | bytes 1966088 | tf_op jit(solution)/shard_map/ppermute | solution.py:1027
  51.9 43.9 %collective-permute-start.4 = (bf16[4,32,2560]{2,1,0:T(8,128)(2,1)S(1)}, bf16[4,32,2560]{2,1,0:T(8,128)(2,1)S(1)}, u32[]{:S(2)}, u32[]{:S(2)}) collective-permute-start(bf16[4,32,2560]{2,1,0:T(8,128)(2,1)S(1)} %get-tuple-element.138), channel_id=1, source_target_pairs={{0,4},{1,5},{2,6},{3,7},{4,0},{5,1},{6,2},{7,3},{8,12},{9,13},{10,... | collective-permute-start | bytes 1966088 | tf_op jit(solution)/shard_map/ppermute | solution.py:1027
  95.8 0.8 copy-start.4
  96.7 0.8 copy-start.5
  100.4 40.8 %collective-permute-start.5 = (bf16[8,32,2560]{2,1,0:T(8,128)(2,1)}, bf16[8,32,2560]{2,1,0:T(8,128)(2,1)S(1)}, u32[]{:S(2)}, u32[]{:S(2)}) collective-permute-start(bf16[8,32,2560]{2,1,0:T(8,128)(2,1)} %get-tuple-element.78.refs_0_.refs_1_), channel_id=1, source_target_pairs={{0,4},{1,5},{2,6},{3,7},{4,0},{5,1},{6,2},{7,3},{8,12},{9,13},{10,... | collective-permute-start | bytes 3932168 | tf_op jit(solution)/shard_map/ppermute | solution.py:1027
  101.9 41.7 %collective-permute-start.6 = (bf16[8,32,2560]{2,1,0:T(8,128)(2,1)}, bf16[8,32,2560]{2,1,0:T(8,128)(2,1)S(1)}, u32[]{:S(2)}, u32[]{:S(2)}) collective-permute-start(bf16[8,32,2560]{2,1,0:T(8,128)(2,1)} %get-tuple-element.79.refs_1_.refs_3_), channel_id=1, source_target_pairs={{0,2},{1,3},{2,0},{3,1},{4,6},{5,7},{6,4},{7,5},{8,10},{9,11},{10,... | collective-permute-start | bytes 3932168 | tf_op jit(solution)/shard_map/ppermute | solution.py:1027
  141.2 2.4 copy-start.1
  143.6 1.1 copy-start.2
  150.5 9.0 %collective-permute-start.7 = (bf16[16,32,5120]{2,1,0:T(8,128)(2,1)}, bf16[16,32,5120]{2,1,0:T(8,128)(2,1)}, u32[]{:S(2)}, u32[]{:S(2)}) collective-permute-start(bf16[16,32,5120]{2,1,0:T(8,128)(2,1)} %near_rows.1.near_ref), channel_id=1, source_target_pairs={{0,1},{1,0},{2,3},{3,2},{4,5},{5,4},{6,7},{7,6},{8,9},{9,8},{10,11... | collective-permute-start | bytes 15728648 | tf_op jit(solution)/shard_map/ppermute | solution.py:1027
  285.7 13.6 %collective-permute-start.8 = (bf16[512,8192]{1,0:T(8,128)(2,1)}, bf16[512,8192]{1,0:T(8,128)(2,1)}, u32[]{:S(2)}, u32[]{:S(2)}) collective-permute-start(bf16[512,8192]{1,0:T(8,128)(2,1)} %get-tuple-element.93), channel_id=1, source_target_pairs={{0,1},{1,0},{2,3},{3,2},{4,5},{5,4},{6,7},{7,6},{8,9},{9,8},{10,11... | collective-permute-start | bytes 25165832 | tf_op jit(solution)/shard_map/ppermute | solution.py:1027
  308.7 99.7 %collective-permute-start.10 = (bf16[128,8192]{1,0:T(8,128)(2,1)}, bf16[128,8192]{1,0:T(8,128)(2,1)}, u32[]{:S(2)}, u32[]{:S(2)}) collective-permute-start(bf16[128,8192]{1,0:T(8,128)(2,1)} %get-tuple-element.94.refs_0_), channel_id=1, source_target_pairs={{0,2},{1,3},{2,0},{3,1},{4,6},{5,7},{6,4},{7,5},{8,10},{9,11},{10,... | collective-permute-start | bytes 6291464 | tf_op jit(solution)/shard_map/ppermute | solution.py:1027
  309.9 100.0 %collective-permute-start.11 = (bf16[128,8192]{1,0:T(8,128)(2,1)}, bf16[128,8192]{1,0:T(8,128)(2,1)}, u32[]{:S(2)}, u32[]{:S(2)}) collective-permute-start(bf16[128,8192]{1,0:T(8,128)(2,1)} %get-tuple-element.95.refs_1_), channel_id=1, source_target_pairs={{0,4},{1,5},{2,6},{3,7},{4,0},{5,1},{6,2},{7,3},{8,12},{9,13},{10,... | collective-permute-start | bytes 6291464 | tf_op jit(solution)/shard_map/ppermute | solution.py:1027
  310.7 99.2 %collective-permute-start.12 = (bf16[128,8192]{1,0:T(8,128)(2,1)}, bf16[128,8192]{1,0:T(8,128)(2,1)}, u32[]{:S(2)}, u32[]{:S(2)}) collective-permute-start(bf16[128,8192]{1,0:T(8,128)(2,1)} %get-tuple-element.96.refs_2_), channel_id=1, source_target_pairs={{0,6},{1,7},{2,4},{3,5},{4,2},{5,3},{6,0},{7,1},{8,14},{9,15},{10,... | collective-permute-start | bytes 6291464 | tf_op jit(solution)/shard_map/ppermute | solution.py:1027
  351.1 13.2 %collective-permute-start.9 = (bf16[512,4096]{1,0:T(8,128)(2,1)}, bf16[512,4096]{1,0:T(8,128)(2,1)}, u32[]{:S(2)}, u32[]{:S(2)}) collective-permute-start(bf16[512,4096]{1,0:T(8,128)(2,1)} %get-tuple-element.102.refs_0_), channel_id=1, source_target_pairs={{0,1},{1,0},{2,3},{3,2},{4,5},{5,4},{6,7},{7,6},{8,9},{9,8},{10,11... | collective-permute-start | bytes 12582920 | tf_op jit(solution)/shard_map/ppermute | solution.py:1027
  369.6 74.5 %collective-permute-start.14 = (bf16[128,4096]{1,0:T(8,128)(2,1)}, bf16[128,4096]{1,0:T(8,128)(2,1)}, u32[]{:S(2)}, u32[]{:S(2)}) collective-permute-start(bf16[128,4096]{1,0:T(8,128)(2,1)} %get-tuple-element.106.refs_0_), channel_id=1, source_target_pairs={{0,2},{1,3},{2,0},{3,1},{4,6},{5,7},{6,4},{7,5},{8,10},{9,11},{10,... | collective-permute-start | bytes 3145736 | tf_op jit(solution)/shard_map/ppermute | solution.py:1027
  370.9 74.7 %collective-permute-start.15 = (bf16[128,4096]{1,0:T(8,128)(2,1)}, bf16[128,4096]{1,0:T(8,128)(2,1)}, u32[]{:S(2)}, u32[]{:S(2)}) collective-permute-start(bf16[128,4096]{1,0:T(8,128)(2,1)} %get-tuple-element.107.refs_1_), channel_id=1, source_target_pairs={{0,4},{1,5},{2,6},{3,7},{4,0},{5,1},{6,2},{7,3},{8,12},{9,13},{10,... | collective-permute-start | bytes 3145736 | tf_op jit(solution)/shard_map/ppermute | solution.py:1027
  408.4 39.9 %collective-permute-start.16 = (bf16[128,4096]{1,0:T(8,128)(2,1)}, bf16[128,4096]{1,0:T(8,128)(2,1)}, u32[]{:S(2)}, u32[]{:S(2)}) collective-permute-start(bf16[128,4096]{1,0:T(8,128)(2,1)} %get-tuple-element.108.refs_2_), channel_id=1, source_target_pairs={{0,6},{1,7},{2,4},{3,5},{4,2},{5,3},{6,0},{7,1},{8,14},{9,15},{10,... | collective-permute-start | bytes 3145736 | tf_op jit(solution)/shard_map/ppermute | solution.py:1027
  415.5 75.7 %reduce-scatter.6.cloned.1.call-start = ((), (), s32[]{:S(2)}) async-start(), calls=%async_computation.6 | async-start | bytes 1310720 | tf_op jit(solution)/shard_map/reduce_scatter | solution.py:1059
  429.1 7.6 %collective-permute-start.13 = (bf16[512,4096]{1,0:T(8,128)(2,1)}, bf16[512,4096]{1,0:T(8,128)(2,1)}, u32[]{:S(2)}, u32[]{:S(2)}) collective-permute-start(bf16[512,4096]{1,0:T(8,128)(2,1)} %get-tuple-element.118.refs_0_), channel_id=1, source_target_pairs={{0,1},{1,0},{2,3},{3,2},{4,5},{5,4},{6,7},{7,6},{8,9},{9,8},{10,11... | collective-permute-start | bytes 12582920 | tf_op jit(solution)/shard_map/ppermute | solution.py:1027
  442.1 50.8 %collective-permute-start.22 = (bf16[128,4096]{1,0:T(8,128)(2,1)}, bf16[128,4096]{1,0:T(8,128)(2,1)}, u32[]{:S(2)}, u32[]{:S(2)}) collective-permute-start(bf16[128,4096]{1,0:T(8,128)(2,1)} %get-tuple-element.120.refs_0_), channel_id=1, source_target_pairs={{0,2},{1,3},{2,0},{3,1},{4,6},{5,7},{6,4},{7,5},{8,10},{9,11},{10,... | collective-permute-start | bytes 3145736 | tf_op jit(solution)/shard_map/ppermute | solution.py:1027
  443.4 49.6 %collective-permute-start.23 = (bf16[128,4096]{1,0:T(8,128)(2,1)}, bf16[128,4096]{1,0:T(8,128)(2,1)}, u32[]{:S(2)}, u32[]{:S(2)}) collective-permute-start(bf16[128,4096]{1,0:T(8,128)(2,1)} %get-tuple-element.121.refs_1_), channel_id=1, source_target_pairs={{0,4},{1,5},{2,6},{3,7},{4,0},{5,1},{6,2},{7,3},{8,12},{9,13},{10,... | collective-permute-start | bytes 3145736 | tf_op jit(solution)/shard_map/ppermute | solution.py:1027
  444.1 48.8 %collective-permute-start.24 = (bf16[128,4096]{1,0:T(8,128)(2,1)}, bf16[128,4096]{1,0:T(8,128)(2,1)}, u32[]{:S(2)}, u32[]{:S(2)}) collective-permute-start(bf16[128,4096]{1,0:T(8,128)(2,1)} %get-tuple-element.122.refs_2_), channel_id=1, source_target_pairs={{0,6},{1,7},{2,4},{3,5},{4,2},{5,3},{6,0},{7,1},{8,14},{9,15},{10,... | collective-permute-start | bytes 3145736 | tf_op jit(solution)/shard_map/ppermute | solution.py:1027
  451.6 70.7 %reduce-scatter.8.cloned.1.call-start = ((), (), s32[]{:S(2)}) async-start(), calls=%async_computation.7 | async-start | bytes 1310720 | tf_op jit(solution)/shard_map/reduce_scatter | solution.py:1059
  467.9 9.7 %collective-permute-start.17 = (f32[24,1024]{1,0:T(8,128)}, f32[24,1024]{1,0:T(8,128)S(1)}, u32[]{:S(2)}, u32[]{:S(2)}) collective-permute-start(f32[24,1024]{1,0:T(8,128)} %small_grads.1), channel_id=1, source_target_pairs={{0,8},{8,0},{16,24},{24,16},{1,9},{9,1},{17,25},{25,17},{2,10},{10... | collective-permute-start | bytes 294920 | tf_op jit(solution)/shard_map/ppermute | solution.py:1027
  478.6 12.0 %collective-permute-start.18 = (f32[24,1024]{1,0:T(8,128)S(1)}, f32[24,1024]{1,0:T(8,128)S(1)}, u32[]{:S(2)}, u32[]{:S(2)}) collective-permute-start(f32[24,1024]{1,0:T(8,128)S(1)} %add.29), channel_id=1, source_target_pairs={{0,16},{8,24},{16,0},{24,8},{1,17},{9,25},{17,1},{25,9},{2,18},{10... | collective-permute-start | bytes 294920 | tf_op jit(solution)/shard_map/ppermute | solution.py:1027
  493.0 3.3 copy-start.3
  496.3 1.4 collective-permute-start.19
  497.7 4.9 collective-permute-start.20
  502.6 4.7 collective-permute-start.21
Sparse Core Ops, SparseCore 0:
  11.4 82.5 all-gather.2
  97.4 122.4 all-gather.4
  415.6 42.0 reduce-scatter.3
  459.9 30.6 reduce-scatter.5
  496.4 25.9 reduce-scatter.7
